TPU v7x, 256 devices: a whole 4x4x8 slice. The times are simulated.
256 devices in a mesh: ctx: 32 (over y_hi, z, core), head: 8 (over x, y_lo).
Axes of the slice: x: 4, y: 4 (y_hi: 2, y_lo: 2; y = y_hi * 2 + y_lo), z: 8, core: 2. Of those that a mesh axis runs over, the one named last changes fastest.
Arguments:
- query_heads: bfloat16 [2, 16384, 4096], P(None, 'ctx', 'head'), may hold values from -140 to 140
- key_heads: bfloat16 [2, 16384, 1024], P(None, 'ctx', 'head'), may hold values from -6 to 6
- value_heads: bfloat16 [2, 16384, 1024], P(None, 'ctx', 'head'), may hold values from -6 to 6
- doc_start: int32 [2, 16384], P(None, 'ctx'), may hold values from 0 to 32767, as said below
- out_weight: bfloat16 [4096, 4096], P('head'), may hold values from -0.125 to 0.125
Outputs:
- layer_output: bfloat16 [2, 16384, 4096], P(None, 'ctx', 'head')
Inputs may be any that keep to these rules, and one draw needn't show every extreme that they name: `doc_start`: documents are contiguous runs of positions; positions 0 and 32767 each begin one; each token holds the first position of its own document, which is at most its own position.
All inputs are finite; a program needn't handle non-finite values.
Results may differ from a plain program's by a relative error of at most 0.017.
Values may be sent and summed in bfloat16 or wider, within the bound.
No kernel may reach another device: no remote copies, remote signals or barrier semaphores. Data moves between devices by JAX's collectives and lax.ppermute only.
A program may use at most 128 MiB of HBM per device.

v0:
```python
import jax
import jax.numpy as jnp
from jax import lax
from jax.sharding import PartitionSpec as P

HD = 128
WSTEPS = 4


def shifted(array, axis, by):
    length = lax.axis_size(axis)
    pairs = [(i, i + by) for i in range(length) if 0 <= i + by < length]
    return lax.ppermute(array, axis, pairs)


def attend(query_heads, keys_sel, values_sel, query_pos, key_pos, first_pos, window):
    halves, block_rows, q_cols = query_heads.shape
    groups = keys_sel.shape[2]
    head_dim = keys_sel.shape[3]
    per_group = q_cols // (groups * head_dim)
    grouped = query_heads.reshape(halves, block_rows, groups, per_group, head_dim)
    scores = jnp.einsum(
        "htgrd,hlgd->hgrtl", grouped, keys_sel, preferred_element_type=jnp.float32
    ) * head_dim ** (-0.5)
    allowed = (
        (key_pos[:, None, :] >= first_pos[:, :, None])
        & (key_pos[:, None, :] <= query_pos[:, :, None])
        & (query_pos[:, :, None] - key_pos[:, None, :] < window)
    )
    allowed = allowed[:, None, None]
    highest = jnp.max(jnp.where(allowed, scores, -1e30), axis=-1, keepdims=True)
    weights = jnp.where(allowed, jnp.exp(scores - highest), 0.0)
    weight_sum = jnp.sum(weights, axis=-1)
    mixed = jnp.einsum(
        "hgrtl,hlgd->htgrd",
        weights.astype(jnp.bfloat16),
        values_sel,
        preferred_element_type=jnp.float32,
    )
    mixed = mixed / jnp.transpose(weight_sum, (0, 3, 1, 2))[..., None]
    return mixed.reshape(halves, block_rows, q_cols).astype(jnp.bfloat16)


def on_device(query_heads, key_heads, value_heads, doc_start, out_weight):
    ctx_size = lax.axis_size("ctx")
    device = lax.axis_index("ctx")
    block_rows = key_heads.shape[1]
    kv_cols = key_heads.shape[2]
    groups = kv_cols // HD
    depth = WSTEPS
    slots = 2 * depth + 1
    lower_side = []
    upper_side = []
    for distance in range(1, depth + 1):
        lower_side.append(shifted((key_heads, value_heads), "ctx", distance))
        upper_side.append(shifted((key_heads, value_heads), "ctx", -distance))
    ordered = lower_side[::-1] + [(key_heads, value_heads)] + upper_side
    near_keys = jnp.stack([entry[0] for entry in ordered], axis=1)
    near_values = jnp.stack([entry[1] for entry in ordered], axis=1)
    flat_keys = near_keys.reshape(2 * slots, block_rows, kv_cols)
    flat_values = near_values.reshape(2 * slots, block_rows, kv_cols)
    blocks = jnp.stack([device, 2 * ctx_size - 1 - device])
    lag_steps = jnp.arange(depth + 1, dtype=jnp.int32)
    key_block = blocks[:, None] - lag_steps[None, :]
    owner = jnp.where(key_block < ctx_size, key_block, 2 * ctx_size - 1 - key_block)
    source_slot = jnp.where(key_block < ctx_size, 0, slots) + owner - device + depth
    source_slot = jnp.where(key_block < 0, depth, source_slot).reshape(-1)
    keys_sel = jnp.take(flat_keys, source_slot, axis=0).reshape(
        2, (depth + 1) * block_rows, groups, HD
    )
    values_sel = jnp.take(flat_values, source_slot, axis=0).reshape(
        2, (depth + 1) * block_rows, groups, HD
    )
    row_offsets = jnp.arange(block_rows, dtype=jnp.int32)
    key_pos = (key_block[:, :, None] * block_rows + row_offsets[None, None, :]).reshape(2, -1)
    query_pos = blocks[:, None] * block_rows + row_offsets[None, :]
    attended = attend(
        query_heads, keys_sel, values_sel, query_pos, key_pos, doc_start, WSTEPS * block_rows
    )
    partial_terms = jnp.einsum(
        "hrq,qe->hre", attended, out_weight, preferred_element_type=jnp.float32
    ).astype(jnp.bfloat16)
    return (
        lax.psum_scatter(partial_terms, "head", scatter_dimension=2, tiled=True)
        .astype(jnp.float32)
        .astype(jnp.bfloat16)
    )


def solution(mesh):
    in_specs = (
        P(None, "ctx", "head"),
        P(None, "ctx", "head"),
        P(None, "ctx", "head"),
        P(None, "ctx"),
        P("head", None),
    )
    out_specs = P(None, "ctx", "head")
    return jax.shard_map(
        on_device, mesh=mesh, in_specs=in_specs, out_specs=out_specs, check_vma=False
    )
```

profile of v0, /device:TPU:24, one launch (start us, length us, event | category | flops | bytes accessed | tf_op | source)
XLA Modules:
  0.0 397.8 jit_solution(12982881874355950595)
XLA Ops:
  6.5 0.0 copy-start
  6.5 0.0 copy-start.7
  6.5 0.0 copy-start.6
  6.5 0.0 reduce-scatter.2.cloned.1.call-start
  6.5 8.6 %collective-permute-start.13 = (bf16[2,512,128]{2,1,0:T(8,128)(2,1)}, bf16[2,512,128]{2,1,0:T(8,128)(2,1)S(1)}, u32[]{:S(2)}, u32[]{:S(2)}) collective-permute-start(bf16[2,512,128]{2,1,0:T(8,128)(2,1)} %param.8), channel_id=1, source_target_pairs={{16,0},{24,8},{32,16},{40,24},{48,32},{56,40},{64,48},{72,56},{80,... | collective-permute-start | bytes 786440 | tf_op jit(solution)/shard_map/ppermute | solution.py:13
  15.1 2.1 collective-permute-start.12
  17.2 2.3 collective-permute-start.11
  19.5 1.9 collective-permute-start.1
  21.4 3.0 collective-permute-start
  24.4 0.1 broadcast_multiply_fusion.1
  24.5 0.1 broadcast_multiply_fusion
  24.6 0.1 sub.60
  24.7 0.1 iota_add_fusion
  24.7 0.1 broadcast_bitcast_fusion
  24.9 4.9 %fusion.9 = pred[2,512,2560]{1,2,0:T(8,128)(4,1)} fusion(s32[2,512]{1,0:T(2,128)S(1)} %iota_add_fusion, s32[2,512]{1,0:T(2,128)} %param.10, s32[2,2560]{1,0:T(2,128)S(1)} %broadcast_add_fusion), kind=kLoop, calls=%fused_computation.13 | loop fusion | flops 15728640 | bytes 2650112 | tf_op jit(solution)/shard_map/and | solution.py:26
  29.8 17.9 %collective-permute-done = bf16[2,512,128]{2,1,0:T(8,128)(2,1)S(1)} collective-permute-done((bf16[2,512,128]{2,1,0:T(8,128)(2,1)}, bf16[2,512,128]{2,1,0:T(8,128)(2,1)S(1)}, u32[]{:S(2)}, u32[]{:S(2)}) %collective-permute-start) | collective-permute-done | bytes 262176 | tf_op jit(solution)/shard_map/ppermute | solution.py:13
  47.7 0.0 copy-done.6
  47.7 4.1 %collective-permute-start.2 = (bf16[2,512,128]{2,1,0:T(8,128)(2,1)S(1)}, bf16[2,512,128]{2,1,0:T(8,128)(2,1)S(1)}, u32[]{:S(2)}, u32[]{:S(2)}) collective-permute-start(bf16[2,512,128]{2,1,0:T(8,128)(2,1)S(1)} %copy-done.6), channel_id=1, source_target_pairs={{0,16},{8,24},{16,32},{24,40},{32,48},{40,56},{48,64},{56,72},{64,... | collective-permute-start | bytes 786440 | tf_op jit(solution)/shard_map/ppermute | solution.py:13
  51.9 0.0 collective-permute-done.1
  51.9 1.9 collective-permute-start.3
  53.9 8.1 %collective-permute-done.2 = bf16[2,512,128]{2,1,0:T(8,128)(2,1)S(1)} collective-permute-done((bf16[2,512,128]{2,1,0:T(8,128)(2,1)S(1)}, bf16[2,512,128]{2,1,0:T(8,128)(2,1)S(1)}, u32[]{:S(2)}, u32[]{:S(2)}) %collective-permute-start.2) | collective-permute-done | bytes 262176 | tf_op jit(solution)/shard_map/ppermute | solution.py:13
  62.0 0.0 copy-done.7
  62.0 1.9 collective-permute-start.9
  64.0 0.1 collective-permute-done.3
  64.0 1.9 collective-permute-start.8
  66.0 19.9 %collective-permute-done.8 = bf16[2,512,128]{2,1,0:T(8,128)(2,1)S(1)} collective-permute-done((bf16[2,512,128]{2,1,0:T(8,128)(2,1)S(1)}, bf16[2,512,128]{2,1,0:T(8,128)(2,1)S(1)}, u32[]{:S(2)}, u32[]{:S(2)}) %collective-permute-start.8) | collective-permute-done | bytes 262176 | tf_op jit(solution)/shard_map/ppermute | solution.py:13
  86.0 5.7 %collective-permute-start.10 = (bf16[2,512,128]{2,1,0:T(8,128)(2,1)S(1)}, bf16[2,512,128]{2,1,0:T(8,128)(2,1)S(1)}, u32[]{:S(2)}, u32[]{:S(2)}) collective-permute-start(bf16[2,512,128]{2,1,0:T(8,128)(2,1)S(1)} %copy-done.7), channel_id=1, source_target_pairs={{0,16},{8,24},{16,32},{24,40},{32,48},{40,56},{48,64},{56,72},{64,... | collective-permute-start | bytes 786440 | tf_op jit(solution)/shard_map/ppermute | solution.py:13
  91.6 0.0 collective-permute-done.9
  91.7 1.9 collective-permute-start.15
  93.6 6.5 %collective-permute-done.10 = bf16[2,512,128]{2,1,0:T(8,128)(2,1)S(1)} collective-permute-done((bf16[2,512,128]{2,1,0:T(8,128)(2,1)S(1)}, bf16[2,512,128]{2,1,0:T(8,128)(2,1)S(1)}, u32[]{:S(2)}, u32[]{:S(2)}) %collective-permute-start.10) | collective-permute-done | bytes 262176 | tf_op jit(solution)/shard_map/ppermute | solution.py:13
  100.1 1.9 collective-permute-start.5
  102.1 0.0 collective-permute-done.11
  102.1 1.9 collective-permute-start.4
  104.1 9.4 %collective-permute-done.4 = bf16[2,512,128]{2,1,0:T(8,128)(2,1)S(1)} collective-permute-done((bf16[2,512,128]{2,1,0:T(8,128)(2,1)S(1)}, bf16[2,512,128]{2,1,0:T(8,128)(2,1)S(1)}, u32[]{:S(2)}, u32[]{:S(2)}) %collective-permute-start.4) | collective-permute-done | bytes 262176 | tf_op jit(solution)/shard_map/ppermute | solution.py:13
  113.5 1.9 collective-permute-start.6
  115.5 0.0 collective-permute-done.5
  115.5 1.9 collective-permute-start.7
  117.4 5.1 %collective-permute-done.6 = bf16[2,512,128]{2,1,0:T(8,128)(2,1)S(1)} collective-permute-done((bf16[2,512,128]{2,1,0:T(8,128)(2,1)S(1)}, bf16[2,512,128]{2,1,0:T(8,128)(2,1)S(1)}, u32[]{:S(2)}, u32[]{:S(2)}) %collective-permute-start.6) | collective-permute-done | bytes 262176 | tf_op jit(solution)/shard_map/ppermute | solution.py:13
  122.5 5.8 %collective-permute-start.14 = (bf16[2,512,128]{2,1,0:T(8,128)(2,1)S(1)}, bf16[2,512,128]{2,1,0:T(8,128)(2,1)S(1)}, u32[]{:S(2)}, u32[]{:S(2)}) collective-permute-start(bf16[2,512,128]{2,1,0:T(8,128)(2,1)S(1)} %copy-done.7), channel_id=1, source_target_pairs={{24,0},{32,8},{40,16},{48,24},{56,32},{64,40},{72,48},{80,56},{88,... | collective-permute-start | bytes 786440 | tf_op jit(solution)/shard_map/ppermute | solution.py:13
  128.4 9.3 %collective-permute-done.7 = bf16[2,512,128]{2,1,0:T(8,128)(2,1)S(1)} collective-permute-done((bf16[2,512,128]{2,1,0:T(8,128)(2,1)S(1)}, bf16[2,512,128]{2,1,0:T(8,128)(2,1)S(1)}, u32[]{:S(2)}, u32[]{:S(2)}) %collective-permute-start.7) | collective-permute-done | bytes 262176 | tf_op jit(solution)/shard_map/ppermute | solution.py:13
  137.7 0.0 copy-start.4
  137.7 0.0 collective-permute-done.12
  137.7 0.0 collective-permute-done.13
  137.8 1.3 copy-done.4
  139.1 0.0 copy-start.5
  139.1 1.4 copy-done.5
  140.6 2.5 gather_fusion
  143.0 3.5 collective-permute-done.14
  146.5 0.7 bitcast_dynamic-update-slice_fusion.1
  147.2 0.0 collective-permute-done.15
  147.2 0.7 bitcast_dynamic-update-slice_fusion
  148.0 3.5 gather_fusion.1
  151.5 3.2 broadcast_select_fusion
  154.7 0.0 copy-done
  154.7 18.5 %fusion = (f32[2,4,512]{2,1,0:T(4,128)S(1)}, f32[2,2560,512,4]{2,1,3,0:T(8,128)}) fusion(pred[2,512,2560]{1,2,0:T(8,128)(4,1)} %fusion.9, bf16[2,2560,128,1]{2,1,3,0:T(8,128)(2,1)} %bitcast.106, bf16[2,512,512]{2,1,0:T(8,128)(2,1)S(1)} %copy-done), kind=kOutput, calls=%fused_computation.4 | convolution fusion | flops 2715807744 | bytes 46940160 | tf_op jit(solution)/shard_map/htgrd,hlgd->hgrtl/dot_general | solution.py:22
  173.2 0.0 copy-start.3
  173.2 19.0 %fusion.3 = f32[2,4,512]{2,1,0:T(4,128)S(1)} fusion(f32[2,2560,512,4]{2,1,3,0:T(8,128)} %get-tuple-element.15, f32[2,4,512]{2,1,0:T(4,128)S(1)} %get-tuple-element.14, pred[2,512,2560]{1,2,0:T(8,128)(4,1)} %fusion.9), kind=kLoop, calls=%fused_computation.7 | loop fusion | flops 41938944 | bytes 44597248 | tf_op jit(solution)/shard_map/reduce_sum | solution.py:33
  192.2 0.0 copy-done.2
  192.2 0.0 copy-done.3
  192.2 16.8 %fusion.11 = bf16[2,512,1,4,128]{1,4,3,0,2:T(8,128)(2,1)S(1)} fusion(bf16[2,2560,128,1]{2,1,3,0:T(8,128)(2,1)S(1)} %bitcast.105, f32[2,2560,512,4]{2,1,3,0:T(8,128)} %get-tuple-element.15, f32[2,4,512]{2,1,0:T(4,128)S(1)} %get-tuple-element.14, pred[2,512,2560]{1,2,0:T(8,128)(4,1)S(1)} %copy-done.2, f32[2,512,4]{1,2,0:T(4,128)S(1)} %bitcast.110), kind=kOutput, calls=%fused_computation.17 | convolution fusion | flops 2727346176 | bytes 46956544 | tf_op jit(solution)/shard_map/hgrtl,hlgd->htgrd/dot_general | solution.py:34
  209.0 9.0 %convolution_convert_fusion = bf16[2,512,4096]{2,1,0:T(8,128)(2,1)} fusion(bf16[2,512,512]{1,2,0:T(8,128)(2,1)S(1)} %bitcast.111, bf16[512,4096]{1,0:T(8,128)(2,1)} %param.11), kind=kOutput, calls=%fused_computation.14 | convolution fusion | flops 4299161600 | bytes 13631488 | tf_op jit(solution)/shard_map/hrq,qe->hre/dot_general | solution.py:80
  218.0 0.0 reduce-scatter.2.cloned.1.call-update
  218.0 172.9 %reduce-scatter.2.cloned.1.call-done = bf16[2,512,512]{2,1,0:T(8,128)(2,1)} async-done(((bf16[2,512,4096]{2,1,0:T(8,128)(2,1)}), bf16[2,512,512]{2,1,0:T(8,128)(2,1)}) %reduce-scatter.2.cloned.1.call-update) | async-done | bytes 1048592 | tf_op jit(solution)/shard_map/reduce_scatter | solution.py:84
  391.0 0.0 copy-done.1
  (24 shorter events, 0.6 us)
Async XLA Ops:
  6.5 148.2 %copy-start = (bf16[2,512,512]{2,1,0:T(8,128)(2,1)S(1)}, bf16[2,512,512]{2,1,0:T(8,128)(2,1)}, u32[]{:S(2)}) copy-start(bf16[2,512,512]{2,1,0:T(8,128)(2,1)} %param.7) | copy-start | bytes 3145732
  6.5 55.5 %copy-start.7 = (bf16[2,512,128]{2,1,0:T(8,128)(2,1)S(1)}, bf16[2,512,128]{2,1,0:T(8,128)(2,1)}, u32[]{:S(2)}) copy-start(bf16[2,512,128]{2,1,0:T(8,128)(2,1)} %param.8) | copy-start | bytes 786436
  6.5 41.2 %copy-start.6 = (bf16[2,512,128]{2,1,0:T(8,128)(2,1)S(1)}, bf16[2,512,128]{2,1,0:T(8,128)(2,1)}, u32[]{:S(2)}) copy-start(bf16[2,512,128]{2,1,0:T(8,128)(2,1)} %param.9) | copy-start | bytes 786436
  6.5 384.4 %reduce-scatter.2.cloned.1.call-start = ((), (), s32[]{:S(2)}) async-start(), calls=%async_computation.1 | async-start | bytes 9437184 | tf_op jit(solution)/shard_map/reduce_scatter | solution.py:84
  6.5 131.2 %collective-permute-start.13 = (bf16[2,512,128]{2,1,0:T(8,128)(2,1)}, bf16[2,512,128]{2,1,0:T(8,128)(2,1)S(1)}, u32[]{:S(2)}, u32[]{:S(2)}) collective-permute-start(bf16[2,512,128]{2,1,0:T(8,128)(2,1)} %param.8), channel_id=1, source_target_pairs={{16,0},{24,8},{32,16},{40,24},{48,32},{56,40},{64,48},{72,56},{80,... | collective-permute-start | bytes 786440 | tf_op jit(solution)/shard_map/ppermute | solution.py:13
  15.1 122.6 %collective-permute-start.12 = (bf16[2,512,128]{2,1,0:T(8,128)(2,1)}, bf16[2,512,128]{2,1,0:T(8,128)(2,1)S(1)}, u32[]{:S(2)}, u32[]{:S(2)}) collective-permute-start(bf16[2,512,128]{2,1,0:T(8,128)(2,1)} %param.8), channel_id=1, source_target_pairs={{8,0},{16,8},{24,16},{32,24},{40,32},{48,40},{56,48},{64,56},{72,6... | collective-permute-start | bytes 786440 | tf_op jit(solution)/shard_map/ppermute | solution.py:13
  17.2 84.9 %collective-permute-start.11 = (bf16[2,512,128]{2,1,0:T(8,128)(2,1)}, bf16[2,512,128]{2,1,0:T(8,128)(2,1)S(1)}, u32[]{:S(2)}, u32[]{:S(2)}) collective-permute-start(bf16[2,512,128]{2,1,0:T(8,128)(2,1)} %param.8), channel_id=1, source_target_pairs={{0,8},{8,16},{16,24},{24,32},{32,40},{40,48},{48,56},{56,64},{64,7... | collective-permute-start | bytes 786440 | tf_op jit(solution)/shard_map/ppermute | solution.py:13
  19.5 32.4 %collective-permute-start.1 = (bf16[2,512,128]{2,1,0:T(8,128)(2,1)}, bf16[2,512,128]{2,1,0:T(8,128)(2,1)S(1)}, u32[]{:S(2)}, u32[]{:S(2)}) collective-permute-start(bf16[2,512,128]{2,1,0:T(8,128)(2,1)} %param.9), channel_id=1, source_target_pairs={{0,24},{8,32},{16,40},{24,48},{32,56},{40,64},{48,72},{56,80},{64,... | collective-permute-start | bytes 786440 | tf_op jit(solution)/shard_map/ppermute | solution.py:13
  21.4 26.3 %collective-permute-start = (bf16[2,512,128]{2,1,0:T(8,128)(2,1)}, bf16[2,512,128]{2,1,0:T(8,128)(2,1)S(1)}, u32[]{:S(2)}, u32[]{:S(2)}) collective-permute-start(bf16[2,512,128]{2,1,0:T(8,128)(2,1)} %param.9), channel_id=1, source_target_pairs={{0,32},{8,40},{16,48},{24,56},{32,64},{40,72},{48,80},{56,88},{64,... | collective-permute-start | bytes 786440 | tf_op jit(solution)/shard_map/ppermute | solution.py:13
  47.7 14.3 %collective-permute-start.2 = (bf16[2,512,128]{2,1,0:T(8,128)(2,1)S(1)}, bf16[2,512,128]{2,1,0:T(8,128)(2,1)S(1)}, u32[]{:S(2)}, u32[]{:S(2)}) collective-permute-start(bf16[2,512,128]{2,1,0:T(8,128)(2,1)S(1)} %copy-done.6), channel_id=1, source_target_pairs={{0,16},{8,24},{16,32},{24,40},{32,48},{40,56},{48,64},{56,72},{64,... | collective-permute-start | bytes 786440 | tf_op jit(solution)/shard_map/ppermute | solution.py:13
  51.9 12.1 %collective-permute-start.3 = (bf16[2,512,128]{2,1,0:T(8,128)(2,1)S(1)}, bf16[2,512,128]{2,1,0:T(8,128)(2,1)S(1)}, u32[]{:S(2)}, u32[]{:S(2)}) collective-permute-start(bf16[2,512,128]{2,1,0:T(8,128)(2,1)S(1)} %copy-done.6), channel_id=1, source_target_pairs={{0,8},{8,16},{16,24},{24,32},{32,40},{40,48},{48,56},{56,64},{64,7... | collective-permute-start | bytes 786440 | tf_op jit(solution)/shard_map/ppermute | solution.py:13
  62.0 29.7 %collective-permute-start.9 = (bf16[2,512,128]{2,1,0:T(8,128)(2,1)S(1)}, bf16[2,512,128]{2,1,0:T(8,128)(2,1)S(1)}, u32[]{:S(2)}, u32[]{:S(2)}) collective-permute-start(bf16[2,512,128]{2,1,0:T(8,128)(2,1)S(1)} %copy-done.7), channel_id=1, source_target_pairs={{0,24},{8,32},{16,40},{24,48},{32,56},{40,64},{48,72},{56,80},{64,... | collective-permute-start | bytes 786440 | tf_op jit(solution)/shard_map/ppermute | solution.py:13
  64.0 21.9 %collective-permute-start.8 = (bf16[2,512,128]{2,1,0:T(8,128)(2,1)S(1)}, bf16[2,512,128]{2,1,0:T(8,128)(2,1)S(1)}, u32[]{:S(2)}, u32[]{:S(2)}) collective-permute-start(bf16[2,512,128]{2,1,0:T(8,128)(2,1)S(1)} %copy-done.7), channel_id=1, source_target_pairs={{0,32},{8,40},{16,48},{24,56},{32,64},{40,72},{48,80},{56,88},{64,... | collective-permute-start | bytes 786440 | tf_op jit(solution)/shard_map/ppermute | solution.py:13
  86.0 14.2 %collective-permute-start.10 = (bf16[2,512,128]{2,1,0:T(8,128)(2,1)S(1)}, bf16[2,512,128]{2,1,0:T(8,128)(2,1)S(1)}, u32[]{:S(2)}, u32[]{:S(2)}) collective-permute-start(bf16[2,512,128]{2,1,0:T(8,128)(2,1)S(1)} %copy-done.7), channel_id=1, source_target_pairs={{0,16},{8,24},{16,32},{24,40},{32,48},{40,56},{48,64},{56,72},{64,... | collective-permute-start | bytes 786440 | tf_op jit(solution)/shard_map/ppermute | solution.py:13
  91.7 55.6 %collective-permute-start.15 = (bf16[2,512,128]{2,1,0:T(8,128)(2,1)S(1)}, bf16[2,512,128]{2,1,0:T(8,128)(2,1)S(1)}, u32[]{:S(2)}, u32[]{:S(2)}) collective-permute-start(bf16[2,512,128]{2,1,0:T(8,128)(2,1)S(1)} %copy-done.7), channel_id=1, source_target_pairs={{32,0},{40,8},{48,16},{56,24},{64,32},{72,40},{80,48},{88,56},{96,... | collective-permute-start | bytes 786440 | tf_op jit(solution)/shard_map/ppermute | solution.py:13
  100.1 15.3 %collective-permute-start.5 = (bf16[2,512,128]{2,1,0:T(8,128)(2,1)S(1)}, bf16[2,512,128]{2,1,0:T(8,128)(2,1)S(1)}, u32[]{:S(2)}, u32[]{:S(2)}) collective-permute-start(bf16[2,512,128]{2,1,0:T(8,128)(2,1)S(1)} %copy-done.6), channel_id=1, source_target_pairs={{16,0},{24,8},{32,16},{40,24},{48,32},{56,40},{64,48},{72,56},{80,... | collective-permute-start | bytes 786440 | tf_op jit(solution)/shard_map/ppermute | solution.py:13
  102.1 11.4 %collective-permute-start.4 = (bf16[2,512,128]{2,1,0:T(8,128)(2,1)S(1)}, bf16[2,512,128]{2,1,0:T(8,128)(2,1)S(1)}, u32[]{:S(2)}, u32[]{:S(2)}) collective-permute-start(bf16[2,512,128]{2,1,0:T(8,128)(2,1)S(1)} %copy-done.6), channel_id=1, source_target_pairs={{8,0},{16,8},{24,16},{32,24},{40,32},{48,40},{56,48},{64,56},{72,6... | collective-permute-start | bytes 786440 | tf_op jit(solution)/shard_map/ppermute | solution.py:13
  113.5 9.0 %collective-permute-start.6 = (bf16[2,512,128]{2,1,0:T(8,128)(2,1)S(1)}, bf16[2,512,128]{2,1,0:T(8,128)(2,1)S(1)}, u32[]{:S(2)}, u32[]{:S(2)}) collective-permute-start(bf16[2,512,128]{2,1,0:T(8,128)(2,1)S(1)} %copy-done.6), channel_id=1, source_target_pairs={{24,0},{32,8},{40,16},{48,24},{56,32},{64,40},{72,48},{80,56},{88,... | collective-permute-start | bytes 786440 | tf_op jit(solution)/shard_map/ppermute | solution.py:13
  115.5 22.2 %collective-permute-start.7 = (bf16[2,512,128]{2,1,0:T(8,128)(2,1)S(1)}, bf16[2,512,128]{2,1,0:T(8,128)(2,1)S(1)}, u32[]{:S(2)}, u32[]{:S(2)}) collective-permute-start(bf16[2,512,128]{2,1,0:T(8,128)(2,1)S(1)} %copy-done.6), channel_id=1, source_target_pairs={{32,0},{40,8},{48,16},{56,24},{64,32},{72,40},{80,48},{88,56},{96,... | collective-permute-start | bytes 786440 | tf_op jit(solution)/shard_map/ppermute | solution.py:13
  122.5 24.0 %collective-permute-start.14 = (bf16[2,512,128]{2,1,0:T(8,128)(2,1)S(1)}, bf16[2,512,128]{2,1,0:T(8,128)(2,1)S(1)}, u32[]{:S(2)}, u32[]{:S(2)}) collective-permute-start(bf16[2,512,128]{2,1,0:T(8,128)(2,1)S(1)} %copy-done.7), channel_id=1, source_target_pairs={{24,0},{32,8},{40,16},{48,24},{56,32},{64,40},{72,48},{80,56},{88,... | collective-permute-start | bytes 786440 | tf_op jit(solution)/shard_map/ppermute | solution.py:13
  137.7 1.4 copy-start.4
  139.1 1.4 copy-start.5
  173.2 19.0 %copy-start.2 = (pred[2,512,2560]{1,2,0:T(8,128)(4,1)S(1)}, pred[2,512,2560]{1,2,0:T(8,128)(4,1)}, u32[]{:S(2)}) copy-start(pred[2,512,2560]{1,2,0:T(8,128)(4,1)} %fusion.9) | copy-start | bytes 7864324
  173.2 19.0 %copy-start.3 = (bf16[10,512,128]{2,1,0:T(8,128)(2,1)S(1)}, bf16[10,512,128]{2,1,0:T(8,128)(2,1)}, u32[]{:S(2)}) copy-start(bf16[10,512,128]{2,1,0:T(8,128)(2,1)} %get-tuple-element.13) | copy-start | bytes 3932164
  218.0 173.0 %copy-start.1 = (bf16[2,512,512]{2,1,0:T(8,128)(2,1)S(1)}, bf16[2,512,512]{2,1,0:T(8,128)(2,1)}, u32[]{:S(2)}) copy-start(bf16[2,512,512]{2,1,0:T(8,128)(2,1)} %param.7) | copy-start | bytes 3145732
Sparse Core Ops, SparseCore 0:
  218.2 172.7 reduce-scatter.1
where the time goes:
time: 400 us; the launch traced here: 398 us
  waiting for transfers between devices  253 us (63%)
  starting transfers between devices  48.7 us (12%)
  matrix products  44.3 us (11%)
  other arithmetic  27.4 us (7%)
  between operations  13.8 us (3%)
  local copies, waits for them, and re-layouts  11 us (3%)
    reduce_scatter x1, waiting for transfers between devices, on_device(): lax.psum_scatter(partial_terms, 'head', scatter_dimension=2, tiled=True)  173 us
    ppermute x16, waiting for transfers between devices, shifted(): return lax.ppermute(array, axis, pairs)  79.8 us
    ppermute x16, starting transfers between devices, shifted(): return lax.ppermute(array, axis, pairs)  48.7 us
    reduce_sum x1, other arithmetic, attend(): weight_sum = jnp.sum(weights, axis=-1)  19 us
    dot_general x1, matrix products, attend(): jnp.einsum('htgrd,hlgd->hgrtl', grouped, keys_sel, preferred_element_type...  18.5 us
    dot_general x1, matrix products, attend(): jnp.einsum('hgrtl,hlgd->htgrd', weights.astype(jnp.bfloat16), values_sel,...  16.8 us
    dot_general x1, matrix products, on_device(): jnp.einsum('hrq,qe->hre', attended, out_weight, preferred_element_type=jn...  8.98 us
  transfers between devices with their start and end apart: 17, of which 10 were waited for; matrix products, arithmetic and copies ran while one was open for 2% of the time, Pallas kernels for 0%

commit v1 on v0

v1 whole, which is shorter than its diff:
```python
import functools
import math

import jax
import jax.numpy as jnp
from jax import lax
from jax.experimental import pallas as pl
from jax.experimental.pallas import tpu as pltpu
from jax.sharding import PartitionSpec as P

HD = 128
LAGS = 4
TILE = 256
NEG = -1e30
NT = (((1,), (1,)), ((), ()))
NN = (((1,), (0,)), ((), ()))
VMEM = pl.BlockSpec(memory_space=pltpu.VMEM)
SMEM = pl.BlockSpec(memory_space=pltpu.SMEM)
F32 = jnp.float32
BF16 = jnp.bfloat16


def mm(a, b, dims=NN):
    return lax.dot_general(a, b, dims, preferred_element_type=F32)


def attn_kernel(
    info_ref, q_ref, doc_ref, own_ref, swap0_ref, near_ref, swap1_ref, far_ref, swap2_ref,
    o_ref, kk, vv, sbuf,
):
    blk = own_ref.shape[1]
    heads = q_ref.shape[1] // HD
    base = info_ref[0]
    hard = info_ref[1] == 1

    def fill(lag, ref):
        rows = pl.ds(lag * blk, blk)
        k = ref[0]
        kk[rows, :HD] = k
        kk[rows, HD:] = k
        vv[rows, :HD] = ref[1]
        vv[rows, HD:] = jnp.ones((blk, HD), BF16)

    fill(0, own_ref)
    fill(2, near_ref)
    fill(4, far_ref)

    @pl.when(hard)
    def _():
        fill(1, swap1_ref)
        fill(3, swap2_ref)

    @pl.when(jnp.logical_not(hard))
    def _():
        fill(1, swap0_ref)
        fill(3, swap1_ref)

    factor = HD ** -0.5 * math.log2(math.e)
    tiles = blk // TILE
    for t in range(tiles):
        r0 = t * TILE
        rel = doc_ref[r0:r0 + TILE, :] - base
        col = lax.broadcasted_iota(jnp.int32, (TILE, blk), 1)
        row_t = lax.broadcasted_iota(jnp.int32, (TILE, TILE), 0)
        col_t = lax.broadcasted_iota(jnp.int32, (TILE, TILE), 1)
        tri = col_t <= row_t
        for a in range(heads):
            sb = sbuf.at[(t * heads + a) % 2]
            qf = q_ref[r0:r0 + TILE, a * HD:(a + 1) * HD].astype(F32) * factor
            hi = qf.astype(BF16)
            lo = (qf - hi.astype(F32)).astype(BF16)
            qq = jnp.concatenate([hi, lo], axis=1)

            def scores(first, count):
                return mm(qq, kk[first:first + count, :], NT)

            def running(m, s):
                for x in range(s.shape[1] // HD):
                    p = s[:, x * HD:(x + 1) * HD]
                    m = p if m is None else jnp.maximum(m, p)
                return m

            m = None
            pieces = []
            off = 0
            for lag in (3, 2, 1):
                s = jnp.where(col - lag * blk >= rel, scores(lag * blk, blk), NEG)
                m = running(m, s)
                sb[:, off:off + blk] = s
                pieces.append((off, blk, lag * blk))
                off += blk
            for u in range(tiles):
                if u == t:
                    continue
                lag = 0 if u < t else LAGS
                first = lag * blk + u * TILE
                s = jnp.where(col_t + (u * TILE - lag * blk) >= rel, scores(first, TILE), NEG)
                m = running(m, s)
                sb[:, off:off + TILE] = s
                pieces.append((off, TILE, first))
                off += TILE
            far = LAGS * blk
            s = jnp.where(tri, scores(r0, TILE), scores(far + r0, TILE))
            position = jnp.where(tri, col_t + r0, col_t + (r0 - far))
            s = jnp.where(position >= rel, s, NEG)
            m = running(m, s)
            sb[:, off:off + TILE] = s
            top = jnp.max(m, axis=1, keepdims=True)
            acc = jnp.zeros((TILE, 2 * HD), F32)
            for begin, count, first in pieces:
                p = jnp.exp2(sb[:, begin:begin + count] - top).astype(BF16)
                acc = acc + mm(p, vv[first:first + count, :])
            p = jnp.exp2(sb[:, off:off + TILE] - top).astype(BF16)
            zero = jnp.zeros_like(p)
            acc = acc + mm(jnp.where(tri, p, zero), vv[r0:r0 + TILE, :])
            acc = acc + mm(jnp.where(tri, zero, p), vv[far + r0:far + r0 + TILE, :])
            o_ref[r0:r0 + TILE, a * HD:(a + 1) * HD] = (acc[:, :HD] / acc[:, HD:]).astype(BF16)


def attention(name, info, q, doc, *blocks):
    rows, cols = q.shape
    keys = (LAGS + 1) * rows
    flops = 4 * rows * cols * keys
    return pl.pallas_call(
        attn_kernel,
        out_shape=jax.ShapeDtypeStruct((rows, cols), BF16),
        in_specs=[SMEM] + [VMEM] * (2 + len(blocks)),
        out_specs=VMEM,
        scratch_shapes=[
            pltpu.VMEM((keys, 2 * HD), BF16),
            pltpu.VMEM((keys, 2 * HD), BF16),
            pltpu.VMEM((2, TILE, LAGS * rows), F32),
        ],
        compiler_params=pltpu.CompilerParams(vmem_limit_bytes=40 * 2**20),
        cost_estimate=pl.CostEstimate(
            flops=4 * flops, bytes_accessed=4 * 2**20, transcendentals=rows * cols // HD * keys
        ),
        name=name,
    )(info, q, doc, *blocks)


def halves(core, rows):
    h = rows // 2
    return pl.ds(pl.multiple_of(core * h, h), h), pl.ds(pl.multiple_of((1 - core) * h, h), h)


def gather_first_kernel(
    info_ref, own_ref, left_ref, right_ref, fa_ref, fb_ref, w_ref,
    wl_ref, wlp_ref, wr_ref, wrp_ref, wf_ref, wfp_ref, send_ref, keep_ref,
):
    x, y, core = info_ref[0], info_ref[1], info_ref[2]
    rows, width = own_ref.shape
    mine, other = halves(core, width)
    cut = rows // 2

    def block(side, r):
        wide = pl.ds(pl.multiple_of(side * width, width), width)
        own_cols = pl.ds(pl.multiple_of((2 * x + side) * width, width), width)
        acc = mm(own_ref[r, :], w_ref[:, own_cols])
        for ref, wm, wp in ((left_ref, wl_ref, wlp_ref), (right_ref, wr_ref, wrp_ref)):
            acc = acc + mm(ref[r, mine], wm[:, wide])
            acc = acc + mm(ref[r, other], wp[:, wide])
        ref = fa_ref if r.start == 0 else fb_ref
        acc = acc + mm(ref[:, mine], wf_ref[:, wide])
        acc = acc + mm(ref[:, other], wfp_ref[:, wide])
        return acc.astype(BF16)

    for r in (slice(0, cut), slice(cut, rows)):
        send_ref[r, :] = block(1 - y, r)
    for r in (slice(0, cut), slice(cut, rows)):
        keep_ref[r, :] = block(y, r)


def reduce_first_kernel(
    info_ref, own_ref, peer_ref, w_ref, wm_ref, wp_ref, fa_ref, fb_ref, up_ref, down_ref, keep_ref
):
    x, y, core = info_ref[0], info_ref[1], info_ref[2]
    rows, width = own_ref.shape
    mine, other = halves(core, width)
    cut = rows // 2
    h = width // 2

    def block(target, r):
        own_cols = pl.ds(pl.multiple_of((2 * target + y) * width, width), width)
        w_rows = pl.ds(pl.multiple_of(target * h, h), h)
        acc = mm(own_ref[r, :], w_ref[:, own_cols])
        acc = acc + mm(peer_ref[r, mine], wm_ref[w_rows, :])
        acc = acc + mm(peer_ref[r, other], wp_ref[w_rows, :])
        return acc.astype(BF16)

    lower, upper = slice(0, cut), slice(cut, rows)
    ring = 4
    opposite = lax.rem(x + 2, ring)
    fa_ref[...] = block(opposite, lower)
    fb_ref[...] = block(opposite, upper)
    for ref, target in (
        (up_ref, lax.rem(x + 1, ring)), (down_ref, lax.rem(x + ring - 1, ring)), (keep_ref, x)
    ):
        for r in (lower, upper):
            ref[r, :] = block(target, r)


def project(kernel, name, outs, args, flops):
    return pl.pallas_call(
        kernel,
        out_shape=[jax.ShapeDtypeStruct(s, BF16) for s in outs],
        in_specs=[SMEM] + [VMEM] * (len(args) - 1),
        out_specs=[VMEM] * len(outs),
        compiler_params=pltpu.CompilerParams(vmem_limit_bytes=40 * 2**20),
        cost_estimate=pl.CostEstimate(flops=2 * flops, bytes_accessed=10 * 2**20, transcendentals=0),
        name=name,
    )(*args)


def on_device(query_heads, key_heads, value_heads, doc_start, out_weight):
    ctx_size = lax.axis_size("ctx")
    c = lax.axis_index("ctx")
    head = lax.axis_index("head")
    core = c % 2
    x, y = head // 2, head % 2
    ring = lax.axis_size("head") // 2
    blk = key_heads.shape[1]
    width = query_heads.shape[2]

    def ctx_move(array, to):
        return lax.ppermute(
            array, "ctx", [(i, to(i)) for i in range(ctx_size) if 0 <= to(i) < ctx_size]
        )

    def head_move(array, to):
        return lax.ppermute(array, "head", [(i, to(i)) for i in range(2 * ring)])

    def swap(array):
        return ctx_move(array, lambda i: i ^ 1)

    def plus(array):
        return head_move(array, lambda i: (i + 2) % (2 * ring))

    def minus(array):
        return head_move(array, lambda i: (i - 2) % (2 * ring))

    def across(array):
        return head_move(array, lambda i: (i + 4) % (2 * ring))

    def mirror(array):
        return head_move(array, lambda i: i ^ 1)

    kv = jnp.stack([key_heads, value_heads], axis=1)
    near0 = ctx_move(kv[0], lambda i: i + 2)
    near1 = ctx_move(kv[1], lambda i: i - 2)
    traded = swap(kv)
    last = c >= ctx_size - 2

    def piece(col_start, cols):
        return lax.dynamic_slice(
            out_weight, (core * (width // 2), col_start), (width // 2, cols)
        )

    w_left = plus(piece(((x + 1) % ring) * 2 * width, 2 * width))
    w_right = minus(piece(((x - 1) % ring) * 2 * width, 2 * width))
    w_far = across(piece(((x + 2) % ring) * 2 * width, 2 * width))
    w_peer = mirror(
        jnp.concatenate([piece((2 * i + 1 - y) * width, width) for i in range(ring)], axis=0)
    )

    near1 = jnp.where(last, traded[0], near1)
    far0 = ctx_move(near0, lambda i: i + 2)
    far1 = ctx_move(near1, lambda i: i - 2)
    near0_traded = swap(near0)
    near1_traded = swap(near1)
    far1 = jnp.where(last, near0_traded, far1)
    far_traded = swap(jnp.where(core == 0, far1, far0))

    def attend(half, near, far, near_traded):
        block = c if half == 0 else 2 * ctx_size - 1 - c
        info = jnp.stack([block * blk, (core == half).astype(jnp.int32)]).astype(jnp.int32)
        return attention(
            "attend" + str(half), info, query_heads[half], doc_start[half][:, None],
            kv[half], traded[half], near, near_traded, far, far_traded,
        )

    info = jnp.stack([x, y, core]).astype(jnp.int32)
    cut = blk // 2
    mixed0 = attend(0, near0, far0, near0_traded)
    left = plus(mixed0)
    right = minus(mixed0)
    mixed1 = attend(1, near1, far1, near1_traded)
    peer = mirror(mixed1)
    opposite_a = plus(left[:cut])
    opposite_b = minus(right[cut:])

    w_left2, w_right2, w_far2, w_peer2 = swap(w_left), swap(w_right), swap(w_far), swap(w_peer)

    fa, fb, up, down, keep1 = project(
        reduce_first_kernel, "reduce_first",
        [(cut, width), (cut, width)] + [(blk, width)] * 3,
        [info, mixed1, peer, out_weight, w_peer, w_peer2],
        2 * blk * width * 8 * width,
    )
    got_a = plus(fa)
    got_b = minus(fb)
    send, keep0 = project(
        gather_first_kernel, "gather_first",
        [(blk, width)] * 2,
        [info, mixed0, left, right, opposite_a, opposite_b, out_weight,
         w_left, w_left2, w_right, w_right2, w_far, w_far2],
        2 * blk * width * 8 * width,
    )
    got0 = mirror(send)
    up = jnp.concatenate([(up[:cut].astype(F32) + got_a.astype(F32)).astype(BF16), up[cut:]], axis=0)
    down = jnp.concatenate([down[:cut], (down[cut:].astype(F32) + got_b.astype(F32)).astype(BF16)], axis=0)
    got_up = plus(up)
    got_down = minus(down)
    out0 = (keep0.astype(F32) + got0.astype(F32)).astype(BF16)
    out1 = (keep1.astype(F32) + got_up.astype(F32) + got_down.astype(F32)).astype(BF16)
    return jnp.stack([out0, out1], axis=0)


def solution(mesh):
    in_specs = (
        P(None, "ctx", "head"),
        P(None, "ctx", "head"),
        P(None, "ctx", "head"),
        P(None, "ctx"),
        P("head", None),
    )
    out_specs = P(None, "ctx", "head")
    return jax.shard_map(
        on_device, mesh=mesh, in_specs=in_specs, out_specs=out_specs, check_vma=False
    )
```

time: 400 us -> 114 us (0.28)
  waiting for transfers between devices: 253 us -> 34 us
  matrix products: 44.3 us -> 0 us
  Pallas kernels: 0 us -> 25.1 us
  other arithmetic: 27.4 us -> 5.88 us
  between operations: 13.8 us -> 0.29 us
  starting transfers between devices: 48.7 us -> 41 us
    reduce_scatter x1 -> x0, waiting for transfers between devices: 173 us -> none  [on_device(): lax.psum_scatter(partial_terms, 'head', scatter_dimension=2, tiled=True)]
    ppermute x16 -> x26, waiting for transfers between devices: 79.8 us -> 34 us  [the longest x14 30.6 us: head_move(): return lax.ppermute(array, 'head', [(i, to(i)) for i in range(2 * ring)])]
    dot_general x3 -> x0, matrix products: 44.3 us -> none  [the longest x1 18.5 us: attend(): jnp.einsum('htgrd,hlgd->hgrtl', grouped, keys_sel, preferred_element_type...]
    pallas_call x0 -> x4, Pallas kernels: none -> 25.1 us  [the longest x2 17.8 us: attention(): pl.pallas_call(attn_kernel, out_shape=jax.ShapeDtypeStruct((rows, cols),...]
    reduce_sum x1 -> x0, other arithmetic: 19 us -> none  [attend(): weight_sum = jnp.sum(weights, axis=-1)]
    ppermute x16 -> x26, starting transfers between devices: 48.7 us -> 41 us  [the longest x14 20.5 us: head_move(): return lax.ppermute(array, 'head', [(i, to(i)) for i in range(2 * ring)])]
    gather x2 -> x0, local copies, waits for them, and re-layouts: 5.99 us -> none  [the longest x1 3.53 us: on_device(): jnp.take(flat_keys, source_slot, axis=0)]
    and x2 -> x0, other arithmetic: 4.93 us -> none  [the longest x1 4.92 us: attend(): (key_pos[:, None, :] >= first_pos[:, :, None]) & (key_pos[:, None, :] <=...]
  transfers between devices with their start and end apart: 17 -> 26, of which waited for: 10 -> 11; matrix products, arithmetic and copies ran while one was open for 2% -> 9% of each run, Pallas kernels for 0% -> 22%
where the time goes in v1:
time: 114 us
  starting transfers between devices  41 us (36%)
  waiting for transfers between devices  34 us (30%)
  Pallas kernels  25.1 us (22%)
  local copies, waits for them, and re-layouts  7.34 us (6%)
  other arithmetic  5.88 us (5%)
    ppermute x14, waiting for transfers between devices, head_move(): return lax.ppermute(array, 'head', [(i, to(i)) for i in range(2 * ring)])  30.6 us
    ppermute x14, starting transfers between devices, head_move(): return lax.ppermute(array, 'head', [(i, to(i)) for i in range(2 * ring)])  20.5 us
    ppermute x12, starting transfers between devices, ctx_move(): lax.ppermute(array, 'ctx', [(i, to(i)) for i in range(ctx_size) if 0 <= t...  20.4 us
    pallas_call x2, Pallas kernels, attention(): pl.pallas_call(attn_kernel, out_shape=jax.ShapeDtypeStruct((rows, cols),...  17.8 us
    pallas_call x2, Pallas kernels, project(): pl.pallas_call(kernel, out_shape=[jax.ShapeDtypeStruct(s, BF16) for s in...  7.33 us
    dynamic_slice x2, local copies, waits for them, and re-layouts, piece(): lax.dynamic_slice(out_weight, (core * (width // 2), col_start), (width //...  3.85 us
    ppermute x12, waiting for transfers between devices, ctx_move(): lax.ppermute(array, 'ctx', [(i, to(i)) for i in range(ctx_size) if 0 <= t...  3.37 us
  transfers between devices with their start and end apart: 26, of which 11 were waited for; matrix products, arithmetic and copies ran while one was open for 9% of the time, Pallas kernels for 22%

profile of v1, /device:TPU:24, one launch (start us, length us, event | category | flops | bytes accessed | tf_op | source)
XLA Modules:
  0.0 113.5 jit_solution(13336667398690641520)
XLA Ops:
  0.0 1.1 %fusion.3 = (bf16[2,512,128]{2,1,0:T(8,128)(2,1)S(1)}, bf16[2,512,128]{2,1,0:T(8,128)(2,1)S(1)}) fusion(bf16[2,1,512,128]{3,2,1,0:T(8,128)(2,1)} %bitcast.31, bf16[2,1,512,128]{3,2,1,0:T(8,128)(2,1)} %bitcast.33), kind=kLoop, calls=%fused_computation.18 | loop fusion | flops 262144 | bytes 1048576 | tf_op jit(solution)/shard_map/squeeze | solution.py:279
  1.1 3.8 %collective-permute-start.1 = (bf16[2,512,128]{2,1,0:T(8,128)(2,1)S(1)}, bf16[2,512,128]{2,1,0:T(8,128)(2,1)S(1)}, u32[]{:S(2)}, u32[]{:S(2)}) collective-permute-start(bf16[2,512,128]{2,1,0:T(8,128)(2,1)S(1)} %get-tuple-element.32.own_ref), channel_id=1, source_target_pairs={{0,16},{8,24},{16,32},{24,40},{32,48},{40,56},{48,64},{56,72},{64,... | collective-permute-start | bytes 786440 | tf_op jit(solution)/shard_map/ppermute | solution.py:226
  5.0 6.5 %collective-permute-start.4 = (bf16[2,512,128]{2,1,0:T(8,128)(2,1)S(1)}, bf16[2,512,128]{2,1,0:T(8,128)(2,1)S(1)}, u32[]{:S(2)}, u32[]{:S(2)}) collective-permute-start(bf16[2,512,128]{2,1,0:T(8,128)(2,1)S(1)} %get-tuple-element.33.own_ref), channel_id=1, source_target_pairs={{16,0},{24,8},{32,16},{40,24},{48,32},{56,40},{64,48},{72,56},{80,... | collective-permute-start | bytes 786440 | tf_op jit(solution)/shard_map/ppermute | solution.py:226
  11.5 1.1 pad_maximum_fusion.2
  12.6 0.1 collective-permute-start
  12.7 1.3 %fusion.7 = (bf16[256,512]{1,0:T(8,128)(2,1)S(1)}, bf16[256,512]{1,0:T(8,128)(2,1)S(1)}, bf16[256,512]{1,0:T(8,128)(2,1)S(1)}, bf16[256,512]{1,0:T(8,128)(2,1)S(1)}) fusion(bf16[512,4096]{1,0:T(8,128)(2,1)} %w_ref.3, s32[]{:T(128)S(6)} %select_n.83, s32[]{:T(128)S(6)} %select_n.90, s32[]{:T(128)S(6)} %select_n.92, s32[]{:T(128)S(6)} %select_n.91, ...), kind=kLoop, calls=%fused_computation.32 | loop fusion | bytes 2097172 | tf_op jit(solution)/shard_map/dynamic_slice | solution.py:255
  14.0 1.0 pad_maximum_fusion
  15.1 0.0 collective-permute-start.20
  15.1 2.6 %fusion.6 = (bf16[256,1024]{1,0:T(8,128)(2,1)}, bf16[256,1024]{1,0:T(8,128)(2,1)}, bf16[256,1024]{1,0:T(8,128)(2,1)}) fusion(bf16[512,4096]{1,0:T(8,128)(2,1)} %w_ref.3, s32[]{:T(128)S(6)} %select_n.83, s32[]{:T(128)S(6)} %select_n.89, s32[]{:T(128)S(6)} %select_n.87, s32[]{:T(128)S(6)} %select_n.85), kind=kLoop, calls=%fused_computation.31 | loop fusion | bytes 3145744 | tf_op jit(solution)/shard_map/dynamic_slice | solution.py:255
  17.6 3.0 %collective-permute-start.15 = (bf16[256,1024]{1,0:T(8,128)(2,1)}, bf16[256,1024]{1,0:T(8,128)(2,1)}, u32[]{:S(2)}, u32[]{:S(2)}) collective-permute-start(bf16[256,1024]{1,0:T(8,128)(2,1)} %get-tuple-element.21), channel_id=1, source_target_pairs={{0,4},{1,5},{2,6},{3,7},{4,0},{5,1},{6,2},{7,3},{8,12},{9,13},{10,... | collective-permute-start | bytes 1572872 | tf_op jit(solution)/shard_map/ppermute | solution.py:231
  20.7 0.1 pad_add_fusion.1.info_ref
  20.8 1.9 %collective-permute-start.3 = (bf16[2,512,128]{2,1,0:T(8,128)(2,1)S(1)}, bf16[2,512,128]{2,1,0:T(8,128)(2,1)S(1)}, u32[]{:S(2)}, u32[]{:S(2)}) collective-permute-start(bf16[2,512,128]{2,1,0:T(8,128)(2,1)S(1)} %collective-permute-done.1.near_ref), channel_id=1, source_target_pairs={{0,16},{8,24},{16,32},{24,40},{32,48},{40,56},{48,64},{56,72},{64,... | collective-permute-start | bytes 786440 | tf_op jit(solution)/shard_map/ppermute | solution.py:226
  22.7 0.0 collective-permute-done.4
  22.7 0.3 collective-permute-start.2
  22.9 0.0 collective-permute-done
  23.0 0.8 copy-done.1
  23.8 7.4 %collective-permute-start.5 = (bf16[2,512,128]{2,1,0:T(8,128)(2,1)S(1)}, bf16[2,512,128]{2,1,0:T(8,128)(2,1)S(1)}, u32[]{:S(2)}, u32[]{:S(2)}) collective-permute-start(bf16[2,512,128]{2,1,0:T(8,128)(2,1)S(1)} %broadcast_select_fusion.1.near_ref), channel_id=1, source_target_pairs={{16,0},{24,8},{32,16},{40,24},{48,32},{56,40},{64,48},{72,56},{80,... | collective-permute-start | bytes 786440 | tf_op jit(solution)/shard_map/ppermute | solution.py:226
  31.1 1.3 %slice_bitcast_fusion.1 = (bf16[512,512]{1,0:T(8,128)(2,1)S(1)}, bf16[512,512]{1,0:T(8,128)(2,1)S(1)}) fusion(bf16[2,512,512]{2,1,0:T(8,128)(2,1)} %param.5), kind=kLoop, calls=%fused_computation.16 | loop fusion | bytes 2097152 | tf_op jit(solution)/shard_map/squeeze | solution.py:278
  32.4 2.3 %collective-permute-done.3.far_ref = bf16[2,512,128]{2,1,0:T(8,128)(2,1)S(1)} collective-permute-done((bf16[2,512,128]{2,1,0:T(8,128)(2,1)S(1)}, bf16[2,512,128]{2,1,0:T(8,128)(2,1)S(1)}, u32[]{:S(2)}, u32[]{:S(2)}) %collective-permute-start.3) | collective-permute-done | bytes 262176 | tf_op jit(solution)/shard_map/ppermute | solution.py:226
  34.7 1.1 %collective-permute-start.13 = (bf16[256,1024]{1,0:T(8,128)(2,1)}, bf16[256,1024]{1,0:T(8,128)(2,1)}, u32[]{:S(2)}, u32[]{:S(2)}) collective-permute-start(bf16[256,1024]{1,0:T(8,128)(2,1)} %get-tuple-element.22), channel_id=1, source_target_pairs={{0,6},{1,7},{2,0},{3,1},{4,2},{5,3},{6,4},{7,5},{8,14},{9,15},{10,... | collective-permute-start | bytes 1572872 | tf_op jit(solution)/shard_map/ppermute | solution.py:231
  35.9 0.0 collective-permute-done.2.swap1_ref
  35.9 0.9 collective-permute-start.11
  36.8 0.6 collective-permute-done.5
  37.4 0.8 broadcast_select_fusion.2
  38.1 0.1 pad_add_fusion.2.info_ref
  38.2 0.1 copy.6.doc_ref
  38.4 0.1 copy.7.doc_ref
  38.5 1.1 slice_bitcast_fusion.3
  39.6 0.4 collective-permute-done.6.swap2_ref
  40.0 0.2 collective-permute-start.18
  40.2 8.8 %attend0.1.own_ref = bf16[512,512]{1,0:T(8,128)(2,1)S(1)} custom-call(s32[2]{0:T(128)S(1)} %pad_add_fusion.1.info_ref, bf16[512,512]{1,0:T(8,128)(2,1)S(1)} %get-tuple-element.28.q_ref, s32[512,1]{1,0:T(8,128)S(1)} %copy.6.doc_ref, bf16[2,512,128]{2,1,0:T(8,128)(2,1)S(1)} %get-tuple-element.32.own_ref, bf16[2,512,128]{2,1,0:T(8,128)(2,1)S(1)} %get-tuple-element.30.swap0_ref, ...), custom_call_target="tpu_custom_call" | custom-call | flops 10737418240 | bytes 4194304 | tf_op jit(solution)/shard_map/attend0/pallas_call | solution.py:124
  49.0 0.0 collective-permute-done.15.wf_ref
  49.0 1.8 %collective-permute-start.8 = (bf16[512,512]{1,0:T(8,128)(2,1)S(1)}, bf16[512,512]{1,0:T(8,128)(2,1)S(1)}, u32[]{:S(2)}, u32[]{:S(2)}) collective-permute-start(bf16[512,512]{1,0:T(8,128)(2,1)S(1)} %attend0.1.own_ref), channel_id=1, source_target_pairs={{0,6},{1,7},{2,0},{3,1},{4,2},{5,3},{6,4},{7,5},{8,14},{9,15},{10,... | collective-permute-start | bytes 1572872 | tf_op jit(solution)/shard_map/ppermute | solution.py:231
  50.8 0.3 collective-permute-start.7
  51.1 0.0 collective-permute-done.20.wm_ref
  51.1 0.0 collective-permute-start.21
  51.1 9.0 %attend1.1.own_ref = bf16[512,512]{1,0:T(8,128)(2,1)S(1)} custom-call(s32[2]{0:T(128)S(1)} %pad_add_fusion.2.info_ref, bf16[512,512]{1,0:T(8,128)(2,1)S(1)} %get-tuple-element.29.q_ref, s32[512,1]{1,0:T(8,128)S(1)} %copy.7.doc_ref, bf16[2,512,128]{2,1,0:T(8,128)(2,1)S(1)} %get-tuple-element.33.own_ref, bf16[2,512,128]{2,1,0:T(8,128)(2,1)S(1)} %get-tuple-element.31.swap0_ref, ...), custom_call_target="tpu_custom_call" | custom-call | flops 10737418240 | bytes 4194304 | tf_op jit(solution)/shard_map/attend1/pallas_call | solution.py:124
  60.1 2.1 %collective-permute-start.19 = (bf16[512,512]{1,0:T(8,128)(2,1)S(1)}, bf16[512,512]{1,0:T(8,128)(2,1)S(1)}, u32[]{:S(2)}, u32[]{:S(2)}) collective-permute-start(bf16[512,512]{1,0:T(8,128)(2,1)S(1)} %attend1.1.own_ref), channel_id=1, source_target_pairs={{0,1},{1,0},{2,3},{3,2},{4,5},{5,4},{6,7},{7,6},{8,9},{9,8},{10,11... | collective-permute-start | bytes 1572872 | tf_op jit(solution)/shard_map/ppermute | solution.py:231
  62.2 0.2 collective-permute-start.16
  62.5 0.8 collective-permute-done.8.right_ref
  63.2 2.7 %collective-permute-done.7.left_ref = bf16[512,512]{1,0:T(8,128)(2,1)S(1)} collective-permute-done((bf16[512,512]{1,0:T(8,128)(2,1)S(1)}, bf16[512,512]{1,0:T(8,128)(2,1)S(1)}, u32[]{:S(2)}, u32[]{:S(2)}) %collective-permute-start.7) | collective-permute-done | bytes 524320 | tf_op jit(solution)/shard_map/ppermute | solution.py:231
  65.9 0.0 collective-permute-start.12
  65.9 0.1 pad_add_fusion.info_ref
  66.1 8.8 %collective-permute-done.19.peer_ref = bf16[512,512]{1,0:T(8,128)(2,1)S(1)} collective-permute-done((bf16[512,512]{1,0:T(8,128)(2,1)S(1)}, bf16[512,512]{1,0:T(8,128)(2,1)S(1)}, u32[]{:S(2)}, u32[]{:S(2)}) %collective-permute-start.19) | collective-permute-done | bytes 524320 | tf_op jit(solution)/shard_map/ppermute | solution.py:231
  74.8 2.7 %collective-permute-start.10 = (bf16[256,512]{1,0:T(8,128)(2,1)S(1)}, bf16[256,512]{1,0:T(8,128)(2,1)S(1)}, u32[]{:S(2)}, u32[]{:S(2)}) collective-permute-start(bf16[256,512]{1,0:T(8,128)(2,1)S(1)} %slice.65), channel_id=1, source_target_pairs={{0,6},{1,7},{2,0},{3,1},{4,2},{5,3},{6,4},{7,5},{8,14},{9,15},{10,... | collective-permute-start | bytes 786440 | tf_op jit(solution)/shard_map/ppermute | solution.py:231
  77.5 0.0 collective-permute-start.9
  77.5 3.6 %reduce_first.1 = (bf16[256,512]{1,0:T(8,128)(2,1)S(1)}, bf16[256,512]{1,0:T(8,128)(2,1)S(1)}, bf16[512,512]{1,0:T(8,128)(2,1)S(1)}, bf16[512,512]{1,0:T(8,128)(2,1)S(1)}, bf16[512,512]{1,0:T(8,128)(2,1)S(1)}) custom-call(s32[3]{0:T(128)S(1)} %pad_add_fusion.info_ref, bf16[512,512]{1,0:T(8,128)(2,1)S(1)} %attend1.1.own_ref, ...), custom_call_target="tpu_custom_call" | custom-call | flops 4294967296 | bytes 10485760 | tf_op jit(solution)/shard_map/reduce_first/pallas_call | solution.py:204
  81.1 3.3 %collective-permute-start.24 = (bf16[256,512]{1,0:T(8,128)(2,1)S(1)}, bf16[256,512]{1,0:T(8,128)(2,1)S(1)}, u32[]{:S(2)}, u32[]{:S(2)}) collective-permute-start(bf16[256,512]{1,0:T(8,128)(2,1)S(1)} %get-tuple-element.18), channel_id=1, source_target_pairs={{0,6},{1,7},{2,0},{3,1},{4,2},{5,3},{6,4},{7,5},{8,14},{9,15},{10,... | collective-permute-start | bytes 786440 | tf_op jit(solution)/shard_map/ppermute | solution.py:231
  84.4 0.0 collective-permute-done.14.wrp_ref
  84.5 1.9 %collective-permute-done.9.fa_ref = bf16[256,512]{1,0:T(8,128)(2,1)S(1)} collective-permute-done((bf16[256,512]{1,0:T(8,128)(2,1)S(1)}, bf16[256,512]{1,0:T(8,128)(2,1)S(1)}, u32[]{:S(2)}, u32[]{:S(2)}) %collective-permute-start.9) | collective-permute-done | bytes 262176 | tf_op jit(solution)/shard_map/ppermute | solution.py:231
  86.4 3.7 %gather_first.1 = (bf16[512,512]{1,0:T(8,128)(2,1)S(1)}, bf16[512,512]{1,0:T(8,128)(2,1)S(1)}) custom-call(s32[3]{0:T(128)S(1)} %pad_add_fusion.info_ref, bf16[512,512]{1,0:T(8,128)(2,1)S(1)} %attend0.1.own_ref, bf16[512,512]{1,0:T(8,128)(2,1)S(1)} %collective-permute-done.7.left_ref, bf16[512,512]{1,0:T(8,128)(2,1)S(1)} %collective-permute-done.8.right_ref, ...), custom_call_target="tpu_custom_call" | custom-call | flops 4294967296 | bytes 10485760 | tf_op jit(solution)/shard_map/gather_first/pallas_call | solution.py:204
  90.1 1.8 %collective-permute-start.17 = (bf16[512,512]{1,0:T(8,128)(2,1)S(1)}, bf16[512,512]{1,0:T(8,128)(2,1)S(1)}, u32[]{:S(2)}, u32[]{:S(2)}) collective-permute-start(bf16[512,512]{1,0:T(8,128)(2,1)S(1)} %get-tuple-element.13), channel_id=1, source_target_pairs={{0,1},{1,0},{2,3},{3,2},{4,5},{5,4},{6,7},{7,6},{8,9},{9,8},{10,11... | collective-permute-start | bytes 1572872 | tf_op jit(solution)/shard_map/ppermute | solution.py:231
  92.0 0.1 collective-permute-start.22
  92.1 0.1 add_convert_fusion.2
  92.2 3.3 %collective-permute-start.25 = (bf16[512,512]{1,0:T(8,128)(2,1)S(1)}, bf16[512,512]{1,0:T(8,128)(2,1)S(1)}, u32[]{:S(2)}, u32[]{:S(2)}) collective-permute-start(bf16[512,512]{1,0:T(8,128)(2,1)S(1)} %pad_maximum_fusion.4), channel_id=1, source_target_pairs={{0,6},{1,7},{2,0},{3,1},{4,2},{5,3},{6,4},{7,5},{8,14},{9,15},{10,... | collective-permute-start | bytes 1572872 | tf_op jit(solution)/shard_map/ppermute | solution.py:231
  95.5 4.2 %collective-permute-done.22 = bf16[256,512]{1,0:T(8,128)(2,1)S(1)} collective-permute-done((bf16[256,512]{1,0:T(8,128)(2,1)S(1)}, bf16[256,512]{1,0:T(8,128)(2,1)S(1)}, u32[]{:S(2)}, u32[]{:S(2)}) %collective-permute-start.22) | collective-permute-done | bytes 262176 | tf_op jit(solution)/shard_map/ppermute | solution.py:231
  99.7 0.1 add_convert_fusion.3
  99.8 0.1 collective-permute-start.23
  99.9 2.6 %collective-permute-done.17 = bf16[512,512]{1,0:T(8,128)(2,1)S(1)} collective-permute-done((bf16[512,512]{1,0:T(8,128)(2,1)S(1)}, bf16[512,512]{1,0:T(8,128)(2,1)S(1)}, u32[]{:S(2)}, u32[]{:S(2)}) %collective-permute-start.17) | collective-permute-done | bytes 524320 | tf_op jit(solution)/shard_map/ppermute | solution.py:231
  102.6 0.1 fusion
  102.7 2.1 %collective-permute-done.25 = bf16[512,512]{1,0:T(8,128)(2,1)S(1)} collective-permute-done((bf16[512,512]{1,0:T(8,128)(2,1)S(1)}, bf16[512,512]{1,0:T(8,128)(2,1)S(1)}, u32[]{:S(2)}, u32[]{:S(2)}) %collective-permute-start.25) | collective-permute-done | bytes 524320 | tf_op jit(solution)/shard_map/ppermute | solution.py:231
  104.8 7.5 %collective-permute-done.23 = bf16[512,512]{1,0:T(8,128)(2,1)S(1)} collective-permute-done((bf16[512,512]{1,0:T(8,128)(2,1)S(1)}, bf16[512,512]{1,0:T(8,128)(2,1)S(1)}, u32[]{:S(2)}, u32[]{:S(2)}) %collective-permute-start.23) | collective-permute-done | bytes 524320 | tf_op jit(solution)/shard_map/ppermute | solution.py:231
  112.3 0.2 fusion.1
  112.5 1.1 pad_maximum_fusion.1
  (24 shorter events, 0.2 us)
Async XLA Ops:
  1.1 19.6 %collective-permute-start.1 = (bf16[2,512,128]{2,1,0:T(8,128)(2,1)S(1)}, bf16[2,512,128]{2,1,0:T(8,128)(2,1)S(1)}, u32[]{:S(2)}, u32[]{:S(2)}) collective-permute-start(bf16[2,512,128]{2,1,0:T(8,128)(2,1)S(1)} %get-tuple-element.32.own_ref), channel_id=1, source_target_pairs={{0,16},{8,24},{16,32},{24,40},{32,48},{40,56},{48,64},{56,72},{64,... | collective-permute-start | bytes 786440 | tf_op jit(solution)/shard_map/ppermute | solution.py:226
  5.0 17.7 %collective-permute-start.4 = (bf16[2,512,128]{2,1,0:T(8,128)(2,1)S(1)}, bf16[2,512,128]{2,1,0:T(8,128)(2,1)S(1)}, u32[]{:S(2)}, u32[]{:S(2)}) collective-permute-start(bf16[2,512,128]{2,1,0:T(8,128)(2,1)S(1)} %get-tuple-element.33.own_ref), channel_id=1, source_target_pairs={{16,0},{24,8},{32,16},{40,24},{48,32},{56,40},{64,48},{72,56},{80,... | collective-permute-start | bytes 786440 | tf_op jit(solution)/shard_map/ppermute | solution.py:226
  12.6 10.3 %collective-permute-start = (bf16[2,2,512,128]{3,2,1,0:T(8,128)(2,1)S(1)}, bf16[2,2,512,128]{3,2,1,0:T(8,128)(2,1)S(1)}, u32[]{:S(2)}, u32[]{:S(2)}) collective-permute-start(bf16[2,2,512,128]{3,2,1,0:T(8,128)(2,1)S(1)} %pad_maximum_fusion.2), channel_id=1, source_target_pairs={{0,8},{8,0},{16,24},{24,16},{32,40},{40,32},{48,56},{56,48},{64,72... | collective-permute-start | bytes 1572872 | tf_op jit(solution)/shard_map/ppermute | solution.py:226
  15.1 5.7 %copy-start.2 = (s32[2,512]{1,0:T(2,128)S(1)}, s32[2,512]{1,0:T(2,128)}, u32[]{:S(2)}) copy-start(s32[2,512]{1,0:T(2,128)} %param.8) | copy-start | bytes 12292
  15.1 36.1 %collective-permute-start.20 = (bf16[1024,512]{1,0:T(8,128)(2,1)}, bf16[1024,512]{1,0:T(8,128)(2,1)}, u32[]{:S(2)}, u32[]{:S(2)}) collective-permute-start(bf16[1024,512]{1,0:T(8,128)(2,1)} %pad_maximum_fusion), channel_id=1, source_target_pairs={{0,1},{1,0},{2,3},{3,2},{4,5},{5,4},{6,7},{7,6},{8,9},{9,8},{10,11... | collective-permute-start | bytes 3145736 | tf_op jit(solution)/shard_map/ppermute | solution.py:231
  17.6 31.4 %collective-permute-start.15 = (bf16[256,1024]{1,0:T(8,128)(2,1)}, bf16[256,1024]{1,0:T(8,128)(2,1)}, u32[]{:S(2)}, u32[]{:S(2)}) collective-permute-start(bf16[256,1024]{1,0:T(8,128)(2,1)} %get-tuple-element.21), channel_id=1, source_target_pairs={{0,4},{1,5},{2,6},{3,7},{4,0},{5,1},{6,2},{7,3},{8,12},{9,13},{10,... | collective-permute-start | bytes 1572872 | tf_op jit(solution)/shard_map/ppermute | solution.py:231
  20.8 14.0 %collective-permute-start.3 = (bf16[2,512,128]{2,1,0:T(8,128)(2,1)S(1)}, bf16[2,512,128]{2,1,0:T(8,128)(2,1)S(1)}, u32[]{:S(2)}, u32[]{:S(2)}) collective-permute-start(bf16[2,512,128]{2,1,0:T(8,128)(2,1)S(1)} %collective-permute-done.1.near_ref), channel_id=1, source_target_pairs={{0,16},{8,24},{16,32},{24,40},{32,48},{40,56},{48,64},{56,72},{64,... | collective-permute-start | bytes 786440 | tf_op jit(solution)/shard_map/ppermute | solution.py:226
  22.7 13.2 %collective-permute-start.2 = (bf16[2,512,128]{2,1,0:T(8,128)(2,1)S(1)}, bf16[2,512,128]{2,1,0:T(8,128)(2,1)S(1)}, u32[]{:S(2)}, u32[]{:S(2)}) collective-permute-start(bf16[2,512,128]{2,1,0:T(8,128)(2,1)S(1)} %collective-permute-done.1.near_ref), channel_id=1, source_target_pairs={{0,8},{8,0},{16,24},{24,16},{32,40},{40,32},{48,56},{56,48},{64,72... | collective-permute-start | bytes 786440 | tf_op jit(solution)/shard_map/ppermute | solution.py:226
  22.9 0.8 copy-start.1
  23.8 13.6 %collective-permute-start.5 = (bf16[2,512,128]{2,1,0:T(8,128)(2,1)S(1)}, bf16[2,512,128]{2,1,0:T(8,128)(2,1)S(1)}, u32[]{:S(2)}, u32[]{:S(2)}) collective-permute-start(bf16[2,512,128]{2,1,0:T(8,128)(2,1)S(1)} %broadcast_select_fusion.1.near_ref), channel_id=1, source_target_pairs={{16,0},{24,8},{32,16},{40,24},{48,32},{56,40},{64,48},{72,56},{80,... | collective-permute-start | bytes 786440 | tf_op jit(solution)/shard_map/ppermute | solution.py:226
  34.7 25.4 %collective-permute-start.13 = (bf16[256,1024]{1,0:T(8,128)(2,1)}, bf16[256,1024]{1,0:T(8,128)(2,1)}, u32[]{:S(2)}, u32[]{:S(2)}) collective-permute-start(bf16[256,1024]{1,0:T(8,128)(2,1)} %get-tuple-element.22), channel_id=1, source_target_pairs={{0,6},{1,7},{2,0},{3,1},{4,2},{5,3},{6,4},{7,5},{8,14},{9,15},{10,... | collective-permute-start | bytes 1572872 | tf_op jit(solution)/shard_map/ppermute | solution.py:231
  35.9 26.4 %collective-permute-start.11 = (bf16[256,1024]{1,0:T(8,128)(2,1)}, bf16[256,1024]{1,0:T(8,128)(2,1)}, u32[]{:S(2)}, u32[]{:S(2)}) collective-permute-start(bf16[256,1024]{1,0:T(8,128)(2,1)} %get-tuple-element.23), channel_id=1, source_target_pairs={{0,2},{1,3},{2,4},{3,5},{4,6},{5,7},{6,0},{7,1},{8,10},{9,11},{10,... | collective-permute-start | bytes 1572872 | tf_op jit(solution)/shard_map/ppermute | solution.py:231
  38.1 1.9 %collective-permute-start.6 = (bf16[2,512,128]{2,1,0:T(8,128)(2,1)}, bf16[2,512,128]{2,1,0:T(8,128)(2,1)}, u32[]{:S(2)}, u32[]{:S(2)}) collective-permute-start(bf16[2,512,128]{2,1,0:T(8,128)(2,1)} %get-tuple-element.19), channel_id=1, source_target_pairs={{0,8},{8,0},{16,24},{24,16},{32,40},{40,32},{48,56},{56,48},{64,72... | collective-permute-start | bytes 786440 | tf_op jit(solution)/shard_map/ppermute | solution.py:226
  40.0 10.8 %collective-permute-start.18 = (bf16[2,512,128]{2,1,0:T(8,128)(2,1)S(1)}, bf16[2,512,128]{2,1,0:T(8,128)(2,1)S(1)}, u32[]{:S(2)}, u32[]{:S(2)}) collective-permute-start(bf16[2,512,128]{2,1,0:T(8,128)(2,1)S(1)} %broadcast_select_fusion.1.near_ref), channel_id=1, source_target_pairs={{0,8},{8,0},{16,24},{24,16},{32,40},{40,32},{48,56},{56,48},{64,72... | collective-permute-start | bytes 786440 | tf_op jit(solution)/shard_map/ppermute | solution.py:226
  49.0 14.2 %collective-permute-start.8 = (bf16[512,512]{1,0:T(8,128)(2,1)S(1)}, bf16[512,512]{1,0:T(8,128)(2,1)S(1)}, u32[]{:S(2)}, u32[]{:S(2)}) collective-permute-start(bf16[512,512]{1,0:T(8,128)(2,1)S(1)} %attend0.1.own_ref), channel_id=1, source_target_pairs={{0,6},{1,7},{2,0},{3,1},{4,2},{5,3},{6,4},{7,5},{8,14},{9,15},{10,... | collective-permute-start | bytes 1572872 | tf_op jit(solution)/shard_map/ppermute | solution.py:231
  50.8 15.1 %collective-permute-start.7 = (bf16[512,512]{1,0:T(8,128)(2,1)S(1)}, bf16[512,512]{1,0:T(8,128)(2,1)S(1)}, u32[]{:S(2)}, u32[]{:S(2)}) collective-permute-start(bf16[512,512]{1,0:T(8,128)(2,1)S(1)} %attend0.1.own_ref), channel_id=1, source_target_pairs={{0,2},{1,3},{2,4},{3,5},{4,6},{5,7},{6,0},{7,1},{8,10},{9,11},{10,... | collective-permute-start | bytes 1572872 | tf_op jit(solution)/shard_map/ppermute | solution.py:231
  51.1 26.4 %collective-permute-start.21 = (bf16[1024,512]{1,0:T(8,128)(2,1)}, bf16[1024,512]{1,0:T(8,128)(2,1)S(1)}, u32[]{:S(2)}, u32[]{:S(2)}) collective-permute-start(bf16[1024,512]{1,0:T(8,128)(2,1)} %collective-permute-done.20.wm_ref), channel_id=1, source_target_pairs={{0,8},{8,0},{16,24},{24,16},{32,40},{40,32},{48,56},{56,48},{64,72... | collective-permute-start | bytes 3145736 | tf_op jit(solution)/shard_map/ppermute | solution.py:226
  51.1 26.4 %copy-start = (bf16[512,4096]{1,0:T(8,128)(2,1)S(1)}, bf16[512,4096]{1,0:T(8,128)(2,1)}, u32[]{:S(2)}) copy-start(bf16[512,4096]{1,0:T(8,128)(2,1)} %w_ref.3) | copy-start | bytes 12582916
  60.1 14.7 %collective-permute-start.19 = (bf16[512,512]{1,0:T(8,128)(2,1)S(1)}, bf16[512,512]{1,0:T(8,128)(2,1)S(1)}, u32[]{:S(2)}, u32[]{:S(2)}) collective-permute-start(bf16[512,512]{1,0:T(8,128)(2,1)S(1)} %attend1.1.own_ref), channel_id=1, source_target_pairs={{0,1},{1,0},{2,3},{3,2},{4,5},{5,4},{6,7},{7,6},{8,9},{9,8},{10,11... | collective-permute-start | bytes 1572872 | tf_op jit(solution)/shard_map/ppermute | solution.py:231
  62.2 18.9 %collective-permute-start.16 = (bf16[256,1024]{1,0:T(8,128)(2,1)}, bf16[256,1024]{1,0:T(8,128)(2,1)S(1)}, u32[]{:S(2)}, u32[]{:S(2)}) collective-permute-start(bf16[256,1024]{1,0:T(8,128)(2,1)} %collective-permute-done.15.wf_ref), channel_id=1, source_target_pairs={{0,8},{8,0},{16,24},{24,16},{32,40},{40,32},{48,56},{56,48},{64,72... | collective-permute-start | bytes 1572872 | tf_op jit(solution)/shard_map/ppermute | solution.py:226
  63.2 21.2 %collective-permute-start.14 = (bf16[256,1024]{1,0:T(8,128)(2,1)}, bf16[256,1024]{1,0:T(8,128)(2,1)S(1)}, u32[]{:S(2)}, u32[]{:S(2)}) collective-permute-start(bf16[256,1024]{1,0:T(8,128)(2,1)} %collective-permute-done.13.wr_ref), channel_id=1, source_target_pairs={{0,8},{8,0},{16,24},{24,16},{32,40},{40,32},{48,56},{56,48},{64,72... | collective-permute-start | bytes 1572872 | tf_op jit(solution)/shard_map/ppermute | solution.py:226
  65.9 18.5 %collective-permute-start.12 = (bf16[256,1024]{1,0:T(8,128)(2,1)}, bf16[256,1024]{1,0:T(8,128)(2,1)S(1)}, u32[]{:S(2)}, u32[]{:S(2)}) collective-permute-start(bf16[256,1024]{1,0:T(8,128)(2,1)} %collective-permute-done.11.wl_ref), channel_id=1, source_target_pairs={{0,8},{8,0},{16,24},{24,16},{32,40},{40,32},{48,56},{56,48},{64,72... | collective-permute-start | bytes 1572872 | tf_op jit(solution)/shard_map/ppermute | solution.py:226
  74.8 9.6 %collective-permute-start.10 = (bf16[256,512]{1,0:T(8,128)(2,1)S(1)}, bf16[256,512]{1,0:T(8,128)(2,1)S(1)}, u32[]{:S(2)}, u32[]{:S(2)}) collective-permute-start(bf16[256,512]{1,0:T(8,128)(2,1)S(1)} %slice.65), channel_id=1, source_target_pairs={{0,6},{1,7},{2,0},{3,1},{4,2},{5,3},{6,4},{7,5},{8,14},{9,15},{10,... | collective-permute-start | bytes 786440 | tf_op jit(solution)/shard_map/ppermute | solution.py:231
  77.5 8.9 %collective-permute-start.9 = (bf16[256,512]{1,0:T(8,128)(2,1)S(1)}, bf16[256,512]{1,0:T(8,128)(2,1)S(1)}, u32[]{:S(2)}, u32[]{:S(2)}) collective-permute-start(bf16[256,512]{1,0:T(8,128)(2,1)S(1)} %slice.64), channel_id=1, source_target_pairs={{0,2},{1,3},{2,4},{3,5},{4,6},{5,7},{6,0},{7,1},{8,10},{9,11},{10,... | collective-permute-start | bytes 786440 | tf_op jit(solution)/shard_map/ppermute | solution.py:231
  81.1 11.0 %collective-permute-start.24 = (bf16[256,512]{1,0:T(8,128)(2,1)S(1)}, bf16[256,512]{1,0:T(8,128)(2,1)S(1)}, u32[]{:S(2)}, u32[]{:S(2)}) collective-permute-start(bf16[256,512]{1,0:T(8,128)(2,1)S(1)} %get-tuple-element.18), channel_id=1, source_target_pairs={{0,6},{1,7},{2,0},{3,1},{4,2},{5,3},{6,4},{7,5},{8,14},{9,15},{10,... | collective-permute-start | bytes 786440 | tf_op jit(solution)/shard_map/ppermute | solution.py:231
  90.1 12.4 %collective-permute-start.17 = (bf16[512,512]{1,0:T(8,128)(2,1)S(1)}, bf16[512,512]{1,0:T(8,128)(2,1)S(1)}, u32[]{:S(2)}, u32[]{:S(2)}) collective-permute-start(bf16[512,512]{1,0:T(8,128)(2,1)S(1)} %get-tuple-element.13), channel_id=1, source_target_pairs={{0,1},{1,0},{2,3},{3,2},{4,5},{5,4},{6,7},{7,6},{8,9},{9,8},{10,11... | collective-permute-start | bytes 1572872 | tf_op jit(solution)/shard_map/ppermute | solution.py:231
  92.0 7.7 %collective-permute-start.22 = (bf16[256,512]{1,0:T(8,128)(2,1)S(1)}, bf16[256,512]{1,0:T(8,128)(2,1)S(1)}, u32[]{:S(2)}, u32[]{:S(2)}) collective-permute-start(bf16[256,512]{1,0:T(8,128)(2,1)S(1)} %get-tuple-element.16), channel_id=1, source_target_pairs={{0,2},{1,3},{2,4},{3,5},{4,6},{5,7},{6,0},{7,1},{8,10},{9,11},{10,... | collective-permute-start | bytes 786440 | tf_op jit(solution)/shard_map/ppermute | solution.py:231
  92.2 12.6 %collective-permute-start.25 = (bf16[512,512]{1,0:T(8,128)(2,1)S(1)}, bf16[512,512]{1,0:T(8,128)(2,1)S(1)}, u32[]{:S(2)}, u32[]{:S(2)}) collective-permute-start(bf16[512,512]{1,0:T(8,128)(2,1)S(1)} %pad_maximum_fusion.4), channel_id=1, source_target_pairs={{0,6},{1,7},{2,0},{3,1},{4,2},{5,3},{6,4},{7,5},{8,14},{9,15},{10,... | collective-permute-start | bytes 1572872 | tf_op jit(solution)/shard_map/ppermute | solution.py:231
  99.8 12.4 %collective-permute-start.23 = (bf16[512,512]{1,0:T(8,128)(2,1)S(1)}, bf16[512,512]{1,0:T(8,128)(2,1)S(1)}, u32[]{:S(2)}, u32[]{:S(2)}) collective-permute-start(bf16[512,512]{1,0:T(8,128)(2,1)S(1)} %pad_maximum_fusion.3), channel_id=1, source_target_pairs={{0,2},{1,3},{2,4},{3,5},{4,6},{5,7},{6,0},{7,1},{8,10},{9,11},{10,... | collective-permute-start | bytes 1572872 | tf_op jit(solution)/shard_map/ppermute | solution.py:231

commit v2 on v1

v2 whole, which is shorter than its diff:
```python
import functools
import math

import jax
import jax.numpy as jnp
from jax import lax
from jax.experimental import pallas as pl
from jax.experimental.pallas import tpu as pltpu
from jax.sharding import PartitionSpec as P

HD = 128
LAGS = 4
TILE = 256
NEG = -1e30
NT = (((1,), (1,)), ((), ()))
NN = (((1,), (0,)), ((), ()))
VMEM = pl.BlockSpec(memory_space=pltpu.VMEM)
SMEM = pl.BlockSpec(memory_space=pltpu.SMEM)
STEP = 10**9
SMALL = pl.CostEstimate(flops=1, bytes_accessed=1, transcendentals=0)
F32 = jnp.float32
BF16 = jnp.bfloat16


def mm(a, b, dims=NN):
    return lax.dot_general(a, b, dims, preferred_element_type=F32)


def attn_kernel(
    half, info_ref, q_ref, doc_ref, own_ref, traded_ref, near_ref, near_traded_ref, far_ref,
    far_traded_ref, fold_near_ref, fold_traded_ref, *refs,
):
    *out_refs, kk, vv, sbuf = refs
    blk = own_ref.shape[1]
    heads = q_ref.shape[2] // HD
    base = info_ref[0]
    hard = info_ref[1] == 1
    easy = info_ref[1] == 0

    def fill(lag, ref):
        rows = pl.ds(lag * blk, blk)
        k = ref[0]
        kk[rows, :HD] = k
        kk[rows, HD:] = k
        vv[rows, :HD] = ref[1]
        vv[rows, HD:] = jnp.ones((blk, HD), BF16)

    def choose(lag, cases):
        for condition, ref in cases:
            pl.when(condition)(functools.partial(fill, lag, ref))

    fill(0, own_ref)
    fill(2, near_ref)
    choose(1, ((hard, near_traded_ref), (easy, traded_ref)))
    if half == 0:
        fill(4, far_ref)
        choose(3, ((hard, far_traded_ref), (easy, near_traded_ref)))
    else:
        folded = info_ref[2] == 1
        plain = info_ref[2] == 0
        choose(4, ((folded, fold_traded_ref), (plain, far_ref)))
        choose(3, (
            (jnp.logical_and(hard, plain), far_traded_ref),
            (jnp.logical_and(hard, folded), fold_near_ref),
            (easy, near_traded_ref),
        ))

    factor = HD ** -0.5 * math.log2(math.e)
    tiles = blk // TILE
    far = LAGS * blk
    for t in range(tiles):
        r0 = t * TILE
        rel = doc_ref[r0:r0 + TILE, :] - base
        col = lax.broadcasted_iota(jnp.int32, (TILE, blk), 1)
        row_t = lax.broadcasted_iota(jnp.int32, (TILE, TILE), 0)
        col_t = lax.broadcasted_iota(jnp.int32, (TILE, TILE), 1)
        tri = col_t <= row_t
        for a in range(heads):
            sb = sbuf.at[(t * heads + a) % 2]
            qf = q_ref[half, r0:r0 + TILE, a * HD:(a + 1) * HD].astype(F32) * factor
            hi = qf.astype(BF16)
            lo = (qf - hi.astype(F32)).astype(BF16)
            qq = jnp.concatenate([hi, lo], axis=1)

            def scores(first, count):
                return mm(qq, kk[first:first + count, :], NT)

            def running(m, s):
                for x in range(s.shape[1] // HD):
                    p = s[:, x * HD:(x + 1) * HD]
                    m = p if m is None else jnp.maximum(m, p)
                return m

            m = None
            pieces = []
            off = 0
            for lag in (3, 2, 1):
                s = jnp.where(col - lag * blk >= rel, scores(lag * blk, blk), NEG)
                m = running(m, s)
                sb[:, off:off + blk] = s
                pieces.append((off, blk, lag * blk))
                off += blk
            for u in range(tiles):
                if u == t:
                    continue
                lag = 0 if u < t else LAGS
                first = lag * blk + u * TILE
                s = jnp.where(col_t + (u * TILE - lag * blk) >= rel, scores(first, TILE), NEG)
                m = running(m, s)
                sb[:, off:off + TILE] = s
                pieces.append((off, TILE, first))
                off += TILE
            s = jnp.where(tri, scores(r0, TILE), scores(far + r0, TILE))
            position = jnp.where(tri, col_t + r0, col_t + (r0 - far))
            s = jnp.where(position >= rel, s, NEG)
            m = running(m, s)
            sb[:, off:off + TILE] = s
            top = jnp.max(m, axis=1, keepdims=True)
            acc = jnp.zeros((TILE, 2 * HD), F32)
            for begin, count, first in pieces:
                p = jnp.exp2(sb[:, begin:begin + count] - top).astype(BF16)
                acc = acc + mm(p, vv[first:first + count, :])
            p = jnp.exp2(sb[:, off:off + TILE] - top).astype(BF16)
            zero = jnp.zeros_like(p)
            acc = acc + mm(jnp.where(tri, p, zero), vv[r0:r0 + TILE, :])
            acc = acc + mm(jnp.where(tri, zero, p), vv[far + r0:far + r0 + TILE, :])
            result = (acc[:, :HD] / acc[:, HD:]).astype(BF16)
            count = out_refs[0].shape[0]
            out_refs[r0 // count][r0 % count:r0 % count + TILE, a * HD:(a + 1) * HD] = result


def attention(half, outs, info, q, doc, *blocks):
    _, rows, cols = q.shape
    keys = (LAGS + 1) * rows
    return pl.pallas_call(
        functools.partial(attn_kernel, half),
        out_shape=[jax.ShapeDtypeStruct((rows // outs, cols), BF16)] * outs,
        in_specs=[SMEM] + [VMEM] * (2 + len(blocks)),
        out_specs=[VMEM] * outs,
        scratch_shapes=[
            pltpu.VMEM((keys, 2 * HD), BF16),
            pltpu.VMEM((keys, 2 * HD), BF16),
            pltpu.VMEM((2, TILE, LAGS * rows), F32),
        ],
        compiler_params=pltpu.CompilerParams(vmem_limit_bytes=16 * 2**20),
        cost_estimate=pl.CostEstimate(flops=4 * 10**9, bytes_accessed=1, transcendentals=0) if half == 0 else pl.CostEstimate(
            flops=16 * rows * cols * keys, bytes_accessed=4 * 2**20,
            transcendentals=rows * cols // HD * keys,
        ),
        name="attend" + str(half),
    )(info, q, doc, *blocks)


def weights_kernel(info_ref, w_ref, side_ref, far_ref, peer_ref):
    x, y, core = info_ref[0], info_ref[1], info_ref[2]
    rows, wide = far_ref.shape
    width = wide // 2
    ring = peer_ref.shape[0] // rows
    mine = pl.ds(pl.multiple_of(core * rows, rows), rows)

    def columns(first, count):
        return pl.ds(pl.multiple_of(first * count, count), count)

    side_ref[...] = w_ref[:, columns(lax.rem(x + 1 + (ring - 2) * core, ring), wide)]
    far_ref[...] = w_ref[mine, columns(lax.rem(x + 2, ring), wide)]
    for i in range(ring):
        peer_ref[i * rows:(i + 1) * rows, :] = w_ref[mine, columns(2 * i + 1 - y, width)]


def split_weights(info, w, ring):
    rows, cols = w.shape
    return pl.pallas_call(
        weights_kernel,
        out_shape=[
            jax.ShapeDtypeStruct((rows, cols // ring), BF16),
            jax.ShapeDtypeStruct((rows // 2, cols // ring), BF16),
            jax.ShapeDtypeStruct((rows // 2 * ring, cols // ring // 2), BF16),
        ],
        in_specs=[SMEM, VMEM],
        out_specs=[VMEM] * 3,
        compiler_params=pltpu.CompilerParams(vmem_limit_bytes=16 * 2**20),
        cost_estimate=SMALL,
        name="split_weights",
    )(info, w)


def halves(core, rows):
    h = rows // 2
    return pl.ds(pl.multiple_of(core * h, h), h), pl.ds(pl.multiple_of((1 - core) * h, h), h)


def gather_first_kernel(
    info_ref, own_ref, left_ref, right_ref, far_ref, w_ref,
    ws_ref, wsp_ref, wf_ref, wfp_ref, send_ref, keep_ref,
):
    x, y, core = info_ref[0], info_ref[1], info_ref[2]
    rows, width = own_ref.shape
    mine, other = halves(core, width)
    cut = rows // 2

    def block(side, r):
        wide = pl.ds(pl.multiple_of(side * width, width), width)
        own_cols = pl.ds(pl.multiple_of((2 * x + side) * width, width), width)
        left, right = left_ref[r, :], right_ref[r, :]
        acc = mm(own_ref[r, :], w_ref[:, own_cols])
        acc = acc + mm(jnp.where(core == 0, left, right), ws_ref[:, wide])
        acc = acc + mm(jnp.where(core == 0, right, left), wsp_ref[:, wide])
        acc = acc + mm(far_ref[r, mine], wf_ref[:, wide])
        acc = acc + mm(far_ref[r, other], wfp_ref[:, wide])
        return acc.astype(BF16)

    for r in (slice(0, cut), slice(cut, rows)):
        send_ref[r, :] = block(1 - y, r)
    for r in (slice(0, cut), slice(cut, rows)):
        keep_ref[r, :] = block(y, r)


def targets(x, ring):
    return lax.rem(x + 2, ring), lax.rem(x + 1, ring), lax.rem(x + ring - 1, ring), x


def own_part_kernel(info_ref, own_ref, w_ref, part_ref):
    x, y = info_ref[0], info_ref[1]
    width = own_ref.shape[1]
    for i, target in enumerate(targets(x, part_ref.shape[0])):
        cols = pl.ds(pl.multiple_of((2 * target + y) * width, width), width)
        part_ref[i] = mm(own_ref[...], w_ref[:, cols])


def reduce_first_kernel(
    info_ref, peer_ref, part_ref, wm_ref, wp_ref, far_ref, up_ref, down_ref, keep_ref
):
    x, core = info_ref[0], info_ref[2]
    rows, width = peer_ref.shape
    mine, other = halves(core, width)
    h = width // 2
    ring = part_ref.shape[0]
    for i, (ref, target) in enumerate(
        zip((far_ref, up_ref, down_ref, keep_ref), targets(x, ring))
    ):
        w_rows = pl.ds(pl.multiple_of(target * h, h), h)
        for r in (slice(0, rows // 2), slice(rows // 2, rows)):
            acc = part_ref[i, r, :] + mm(peer_ref[r, mine], wm_ref[w_rows, :])
            ref[r, :] = (acc + mm(peer_ref[r, other], wp_ref[w_rows, :])).astype(BF16)


def total_kernel(info_ref, first_ref, *refs):
    *more, o_ref = refs
    total = first_ref[...].astype(F32)
    for ref in more:
        total = total + ref[...].astype(F32)
    o_ref[...] = total.astype(BF16)


def finish_kernel(info_ref, keep_ref, got_ref, done_ref, o_ref):
    o_ref[0] = (keep_ref[...].astype(F32) + got_ref[...].astype(F32)).astype(BF16)
    o_ref[1] = done_ref[...]


def project(kernel, name, outs, args, cost=0):
    return pl.pallas_call(
        kernel,
        out_shape=outs,
        in_specs=[SMEM] + [VMEM] * (len(args) - 1),
        out_specs=[VMEM] * len(outs),
        compiler_params=pltpu.CompilerParams(vmem_limit_bytes=16 * 2**20),
        cost_estimate=pl.CostEstimate(flops=cost, bytes_accessed=1, transcendentals=0),
        name=name,
    )(*args)


def after(array, *others):
    return lax.optimization_barrier((array, *others))[0]


def on_device(query_heads, key_heads, value_heads, doc_start, out_weight):
    ctx_size = lax.axis_size("ctx")
    c = lax.axis_index("ctx")
    head = lax.axis_index("head")
    core = c % 2
    x, y = head // 2, head % 2
    ring = lax.axis_size("head") // 2
    blk = key_heads.shape[1]
    width = query_heads.shape[2]

    def ctx_move(array, to):
        return lax.ppermute(
            array, "ctx", [(i, to(i)) for i in range(ctx_size) if 0 <= to(i) < ctx_size]
        )

    def head_move(array, to):
        return lax.ppermute(array, "head", [(i, to(i)) for i in range(2 * ring)])

    def swap(array):
        return ctx_move(array, lambda i: i ^ 1)

    def plus(array):
        return head_move(array, lambda i: (i + 2) % (2 * ring))

    def minus(array):
        return head_move(array, lambda i: (i - 2) % (2 * ring))

    def across(array):
        return head_move(array, lambda i: (i + 4) % (2 * ring))

    def mirror(array):
        return head_move(array, lambda i: i ^ 1)

    kv0 = jnp.stack([key_heads[0], value_heads[0]])
    kv1 = jnp.stack([key_heads[1], value_heads[1]])
    near0 = ctx_move(kv0, lambda i: i + 2)
    near1 = ctx_move(kv1, lambda i: i - 2)
    traded0 = swap(kv0)
    traded1 = swap(kv1)

    place = jnp.stack([x, y, core]).astype(jnp.int32)
    w_side, w_far, w_peer = split_weights(place, out_weight, ring)
    heads = 2 * ring
    w_side, w_far = after(w_side, traded0, traded1), after(w_far, traded0, traded1)
    w_side = lax.ppermute(w_side, ("ctx", "head"), [
        (i * heads + j, i * heads + (j + (2 if i % 2 == 0 else heads - 2)) % heads)
        for i in range(ctx_size) for j in range(heads)
    ])
    w_far = across(w_far)

    last = c >= ctx_size - 2
    near0 = after(near0, near1, traded0, traded1, w_peer)
    far0 = ctx_move(near0, lambda i: i + 2)
    near0_traded = swap(near0)
    near1 = jnp.where(last, traded0, after(near1, near0))
    far1 = ctx_move(near1, lambda i: i - 2)
    near1_traded = swap(near1)
    far0_traded = swap(far0)
    far1_traded = swap(far1)

    def facts(half):
        block = c if half == 0 else 2 * ctx_size - 1 - c
        info = jnp.stack([block * blk, core == half, last]).astype(jnp.int32)
        return info, query_heads, doc_start[half][:, None]

    w_peer = mirror(after(w_peer, far0))
    [mixed0] = attention(
        0, 1, *facts(0), kv0, traded0, near0, after(near0_traded, near1_traded), far0, far0_traded,
        near0, near0_traded,
    )
    kv1 = after(kv1, mixed0)
    mixed0 = after(mixed0, far1_traded, w_side, w_far)
    left, right, opposite = plus(mixed0), minus(mixed0), across(mixed0)
    [mixed1] = attention(
        1, 1, *facts(1), kv1, traded1, near1, near1_traded, far1, far1_traded, near0, near0_traded
    )
    peer = mirror(mixed1)
    piece = jax.ShapeDtypeStruct((blk, width), BF16)
    [part] = project(
        own_part_kernel, "own_part", [jax.ShapeDtypeStruct((ring, blk, width), F32)],
        [place, after(mixed1, left, right, opposite), out_weight], STEP,
    )
    w_peer2 = swap(after(w_peer, peer, part))
    far, up, down, keep1 = project(
        reduce_first_kernel, "reduce_first", [piece] * 4, [place, peer, part, w_peer, w_peer2]
    )
    got_far, got_up, got_down = across(far), plus(up), minus(down)
    w_side2, w_far2 = swap(after(w_side, far)), swap(after(w_far, far))
    send, keep0 = project(
        gather_first_kernel, "gather_first", [piece] * 2,
        [place, mixed0, left, right, opposite, out_weight, w_side, w_side2, w_far, w_far2],
    )
    got0 = mirror(send)
    [out1] = project(
        total_kernel, "total", [piece], [place, keep1, got_far, got_up, got_down], STEP
    )
    return project(
        finish_kernel, "finish", [jax.ShapeDtypeStruct((2, blk, width), BF16)],
        [place, keep0, got0, out1],
    )[0]


def solution(mesh):
    in_specs = (
        P(None, "ctx", "head"),
        P(None, "ctx", "head"),
        P(None, "ctx", "head"),
        P(None, "ctx"),
        P("head", None),
    )
    out_specs = P(None, "ctx", "head")
    return jax.shard_map(
        on_device, mesh=mesh, in_specs=in_specs, out_specs=out_specs, check_vma=False
    )
```

time: 114 us -> 112 us (0.982)
  other arithmetic: 5.88 us -> 0.33 us
  waiting for transfers between devices: 34 us -> 38.6 us
  Pallas kernels: 25.1 us -> 29.1 us
  starting transfers between devices: 41 us -> 37.3 us
    ppermute x14 -> x10, starting transfers between devices: 20.5 us -> 13.4 us  [head_move(): return lax.ppermute(array, 'head', [(i, to(i)) for i in range(2 * ring)])]
    unnamed x6 -> x14, local copies, waits for them, and re-layouts: 0.78 us -> 5.11 us
    pallas_call x4 -> x8, Pallas kernels: 25.1 us -> 29.1 us  [the longest x2 18.2 us: attention(): pl.pallas_call(functools.partial(attn_kernel, half), out_shape=[jax.Shape...]
    dynamic_slice x2 -> x0, local copies, waits for them, and re-layouts: 3.85 us -> none  [piece(): lax.dynamic_slice(out_weight, (core * (width // 2), col_start), (width //...]
    ppermute x14 -> x10, waiting for transfers between devices: 30.6 us -> 33.3 us  [head_move(): return lax.ppermute(array, 'head', [(i, to(i)) for i in range(2 * ring)])]
    another operation x7 -> x5, other arithmetic: 2.71 us -> 0.29 us  [the longest x2 0.15 us: facts(): info = jnp.stack([block * blk, core == half, last]).astype(jnp.int32)]
    squeeze x2 -> x0, local copies, waits for them, and re-layouts: 2.34 us -> none  [the longest x1 1.27 us: attend(): query_heads[half]]
    ppermute x12 -> x13, waiting for transfers between devices: 3.37 us -> 5.29 us  [ctx_move(): lax.ppermute(array, 'ctx', [(i, to(i)) for i in range(ctx_size) if 0 <= t...]
  transfers between devices with their start and end apart: 26 -> 24, of which waited for: 11 -> 9; matrix products, arithmetic and copies ran while one was open for 9% -> 1% of each run, Pallas kernels for 22% -> 23%
where the time goes in v2:
time: 112 us
  waiting for transfers between devices  38.6 us (34%)
  starting transfers between devices  37.3 us (33%)
  Pallas kernels  29.1 us (26%)
  local copies, waits for them, and re-layouts  6.55 us (6%)
    ppermute x10, waiting for transfers between devices, head_move(): return lax.ppermute(array, 'head', [(i, to(i)) for i in range(2 * ring)])  33.3 us
    ppermute x13, starting transfers between devices, ctx_move(): lax.ppermute(array, 'ctx', [(i, to(i)) for i in range(ctx_size) if 0 <= t...  22.3 us
    pallas_call x2, Pallas kernels, attention(): pl.pallas_call(functools.partial(attn_kernel, half), out_shape=[jax.Shape...  18.2 us
    ppermute x10, starting transfers between devices, head_move(): return lax.ppermute(array, 'head', [(i, to(i)) for i in range(2 * ring)])  13.4 us
    pallas_call x5, Pallas kernels, project(): pl.pallas_call(kernel, out_shape=outs, in_specs=[SMEM] + [VMEM] * (len(ar...  9.04 us
    ppermute x13, waiting for transfers between devices, ctx_move(): lax.ppermute(array, 'ctx', [(i, to(i)) for i in range(ctx_size) if 0 <= t...  5.29 us
    unnamed x14, local copies, waits for them, and re-layouts  5.11 us
  transfers between devices with their start and end apart: 24, of which 9 were waited for; matrix products, arithmetic and copies ran while one was open for 1% of the time, Pallas kernels for 23%

profile of v2, /device:TPU:24, one launch (start us, length us, event | category | flops | bytes accessed | tf_op | source)
XLA Modules:
  0.0 112.0 jit_solution(7149337525143496683)
XLA Ops:
  0.0 1.1 %fusion = (bf16[1,512,128]{2,1,0:T(8,128)(2,1)S(1)}, bf16[1,512,128]{2,1,0:T(8,128)(2,1)S(1)}, bf16[1,512,128]{2,1,0:T(8,128)(2,1)S(1)}, bf16[1,512,128]{2,1,0:T(8,128)(2,1)S(1)}) fusion(bf16[2,512,128]{2,1,0:T(8,128)(2,1)} %param.6, bf16[2,512,128]{2,1,0:T(8,128)(2,1)} %param.7), kind=kLoop, calls=%fused_computation.8 | loop fusion | bytes 1048576 | tf_op jit(solution)/shard_map/slice | solution.py:310
  1.2 0.1 collective-permute-start
  1.3 0.6 collective-permute-start.3
  1.9 3.8 %collective-permute-start.1 = (bf16[2,512,128]{2,1,0:T(8,128)(2,1)S(1)}, bf16[2,512,128]{2,1,0:T(8,128)(2,1)}, u32[]{:S(2)}, u32[]{:S(2)}) collective-permute-start(bf16[2,512,128]{2,1,0:T(8,128)(2,1)S(1)} %pad_maximum_fusion.own_ref), channel_id=1, source_target_pairs={{0,16},{8,24},{16,32},{24,40},{32,48},{40,56},{48,64},{56,72},{64,... | collective-permute-start | bytes 786440 | tf_op jit(solution)/shard_map/ppermute | solution.py:287
  5.7 6.5 %collective-permute-start.2 = (bf16[2,512,128]{2,1,0:T(8,128)(2,1)S(1)}, bf16[2,512,128]{2,1,0:T(8,128)(2,1)S(1)}, u32[]{:S(2)}, u32[]{:S(2)}) collective-permute-start(bf16[2,512,128]{2,1,0:T(8,128)(2,1)S(1)} %pad_maximum_fusion.1.own_ref), channel_id=1, source_target_pairs={{16,0},{24,8},{32,16},{40,24},{48,32},{56,40},{64,48},{72,56},{80,... | collective-permute-start | bytes 786440 | tf_op jit(solution)/shard_map/ppermute | solution.py:287
  12.3 0.1 pad_add_fusion.info_ref
  12.4 2.2 %copy-done = bf16[512,4096]{1,0:T(8,128)(2,1)S(1)} copy-done((bf16[512,4096]{1,0:T(8,128)(2,1)S(1)}, bf16[512,4096]{1,0:T(8,128)(2,1)}, u32[]{:S(2)}) %copy-start) | copy-done | bytes 4194328
  14.6 1.9 %split_weights.1 = (bf16[512,1024]{1,0:T(8,128)(2,1)}, bf16[256,1024]{1,0:T(8,128)(2,1)}, bf16[1024,512]{1,0:T(8,128)(2,1)S(1)}) custom-call(s32[3]{0:T(128)S(1)} %pad_add_fusion.info_ref, bf16[512,4096]{1,0:T(8,128)(2,1)S(1)} %copy-done), custom_call_target="tpu_custom_call" | custom-call | flops 1 | bytes 1 | tf_op jit(solution)/shard_map/split_weights/pallas_call | solution.py:172
  16.4 1.0 copy-done.3
  17.4 0.0 collective-permute-done.traded_ref
  17.4 0.0 collective-permute-done.3.traded_ref
  17.4 0.0 collective-permute-done.1.near_ref.fold_near_ref
  17.4 0.6 collective-permute-done.2
  18.0 1.9 %collective-permute-start.6 = (bf16[2,512,128]{2,1,0:T(8,128)(2,1)}, bf16[2,512,128]{2,1,0:T(8,128)(2,1)}, u32[]{:S(2)}, u32[]{:S(2)}) collective-permute-start(bf16[2,512,128]{2,1,0:T(8,128)(2,1)} %collective-permute-done.1.near_ref.fold_near_ref), channel_id=1, source_target_pairs={{0,16},{8,24},{16,32},{24,40},{32,48},{40,56},{48,64},{56,72},{64,... | collective-permute-start | bytes 786440 | tf_op jit(solution)/shard_map/ppermute | solution.py:287
  19.9 1.6 %collective-permute-start.10 = (bf16[512,1024]{1,0:T(8,128)(2,1)}, bf16[512,1024]{1,0:T(8,128)(2,1)S(1)}, u32[]{:S(2)}, u32[]{:S(2)}) collective-permute-start(bf16[512,1024]{1,0:T(8,128)(2,1)} %get-tuple-element.31), channel_id=1, source_target_pairs={{0,2},{1,3},{2,4},{3,5},{4,6},{5,7},{6,0},{7,1},{8,14},{9,15},{10,... | collective-permute-start | bytes 3145736 | tf_op jit(solution)/shard_map/ppermute | solution.py:320
  21.5 0.3 collective-permute-start.5
  21.8 8.0 %collective-permute-start.8 = (bf16[2,512,128]{2,1,0:T(8,128)(2,1)S(1)}, bf16[2,512,128]{2,1,0:T(8,128)(2,1)}, u32[]{:S(2)}, u32[]{:S(2)}) collective-permute-start(bf16[2,512,128]{2,1,0:T(8,128)(2,1)S(1)} %broadcast_select_fusion.near_ref), channel_id=1, source_target_pairs={{16,0},{24,8},{32,16},{40,24},{48,32},{56,40},{64,48},{72,56},{80,... | collective-permute-start | bytes 786440 | tf_op jit(solution)/shard_map/ppermute | solution.py:287
  29.8 0.2 collective-permute-start.4
  29.9 2.0 %collective-permute-done.6.far_ref = bf16[2,512,128]{2,1,0:T(8,128)(2,1)} collective-permute-done((bf16[2,512,128]{2,1,0:T(8,128)(2,1)}, bf16[2,512,128]{2,1,0:T(8,128)(2,1)}, u32[]{:S(2)}, u32[]{:S(2)}) %collective-permute-start.6) | collective-permute-done | bytes 262176 | tf_op jit(solution)/shard_map/ppermute | solution.py:287
  32.0 0.0 collective-permute-start.7
  32.0 0.0 collective-permute-done.5.near_traded_ref
  32.0 0.7 copy-done.4
  32.7 3.1 %collective-permute-start.11 = (bf16[256,1024]{1,0:T(8,128)(2,1)}, bf16[256,1024]{1,0:T(8,128)(2,1)S(1)}, u32[]{:S(2)}, u32[]{:S(2)}) collective-permute-start(bf16[256,1024]{1,0:T(8,128)(2,1)} %get-tuple-element.33), channel_id=1, source_target_pairs={{0,4},{1,5},{2,6},{3,7},{4,0},{5,1},{6,2},{7,3},{8,12},{9,13},{10,... | collective-permute-start | bytes 1572872 | tf_op jit(solution)/shard_map/ppermute | solution.py:292
  35.8 0.1 add_add_fusion.info_ref
  35.9 0.1 copy.7.doc_ref
  36.0 0.1 copy.6.doc_ref
  36.2 0.1 add_add_fusion.1.info_ref
  36.3 0.0 collective-permute-done.4.near_traded_ref.fold_traded_ref
  36.3 0.0 collective-permute-start.16
  36.3 0.0 collective-permute-done.8.far_ref
  36.3 0.3 collective-permute-start.9
  36.6 0.0 collective-permute-done.7.far_traded_ref
  36.6 1.2 %copy-done.2 = bf16[2,512,512]{2,1,0:T(8,128)(2,1)S(1)} copy-done((bf16[2,512,512]{2,1,0:T(8,128)(2,1)S(1)}, bf16[2,512,512]{2,1,0:T(8,128)(2,1)}, u32[]{:S(2)}) %copy-start.2) | copy-done | bytes 1048600
  37.9 9.2 %attend0.1.own_ref = bf16[512,512]{1,0:T(8,128)(2,1)S(1)} custom-call(s32[3]{0:T(128)S(1)} %add_add_fusion.info_ref, bf16[2,512,512]{2,1,0:T(8,128)(2,1)S(1)} %copy-done.2, s32[512,1]{1,0:T(8,128)S(1)} %copy.6.doc_ref, bf16[2,512,128]{2,1,0:T(8,128)(2,1)S(1)} %pad_maximum_fusion.own_ref, bf16[2,512,128]{2,1,0:T(8,128)(2,1)S(1)} %collective-permute-done.traded_ref, ...), custom_call_target="tpu_custom_call" | custom-call | flops 4000000000 | bytes 1 | tf_op jit(solution)/shard_map/attend0/pallas_call | solution.py:135
  47.1 0.0 copy-start.1
  47.1 0.0 collective-permute-done.9.far_traded_ref
  47.1 1.7 %collective-permute-done.11.wf_ref = bf16[256,1024]{1,0:T(8,128)(2,1)S(1)} collective-permute-done((bf16[256,1024]{1,0:T(8,128)(2,1)}, bf16[256,1024]{1,0:T(8,128)(2,1)S(1)}, u32[]{:S(2)}, u32[]{:S(2)}) %collective-permute-start.11) | collective-permute-done | bytes 524320 | tf_op jit(solution)/shard_map/ppermute | solution.py:292
  48.7 0.0 collective-permute-done.10.ws_ref
  48.7 3.1 %collective-permute-start.14 = (bf16[512,512]{1,0:T(8,128)(2,1)S(1)}, bf16[512,512]{1,0:T(8,128)(2,1)S(1)}, u32[]{:S(2)}, u32[]{:S(2)}) collective-permute-start(bf16[512,512]{1,0:T(8,128)(2,1)S(1)} %attend0.1.own_ref), channel_id=1, source_target_pairs={{0,4},{1,5},{2,6},{3,7},{4,0},{5,1},{6,2},{7,3},{8,12},{9,13},{10,... | collective-permute-start | bytes 1572872 | tf_op jit(solution)/shard_map/ppermute | solution.py:292
  51.8 1.1 %collective-permute-start.13 = (bf16[512,512]{1,0:T(8,128)(2,1)S(1)}, bf16[512,512]{1,0:T(8,128)(2,1)S(1)}, u32[]{:S(2)}, u32[]{:S(2)}) collective-permute-start(bf16[512,512]{1,0:T(8,128)(2,1)S(1)} %attend0.1.own_ref), channel_id=1, source_target_pairs={{0,6},{1,7},{2,0},{3,1},{4,2},{5,3},{6,4},{7,5},{8,14},{9,15},{10,... | collective-permute-start | bytes 1572872 | tf_op jit(solution)/shard_map/ppermute | solution.py:292
  53.0 0.9 collective-permute-start.12
  53.9 9.0 %attend1.1.own_ref = bf16[512,512]{1,0:T(8,128)(2,1)S(1)} custom-call(s32[3]{0:T(128)S(1)} %add_add_fusion.1.info_ref, bf16[2,512,512]{2,1,0:T(8,128)(2,1)S(1)} %copy-done.2, s32[512,1]{1,0:T(8,128)S(1)} %copy.7.doc_ref, bf16[2,512,128]{2,1,0:T(8,128)(2,1)S(1)} %pad_maximum_fusion.1.own_ref, bf16[2,512,128]{2,1,0:T(8,128)(2,1)S(1)} %collective-permute-done.3.traded_ref, ...), custom_call_target="tpu_custom_call" | custom-call | flops 10737418240 | bytes 4194304 | tf_op jit(solution)/shard_map/attend1/pallas_call | solution.py:135
  62.9 0.1 collective-permute-start.15
  63.0 2.2 %collective-permute-done.14.far_ref = bf16[512,512]{1,0:T(8,128)(2,1)S(1)} collective-permute-done((bf16[512,512]{1,0:T(8,128)(2,1)S(1)}, bf16[512,512]{1,0:T(8,128)(2,1)S(1)}, u32[]{:S(2)}, u32[]{:S(2)}) %collective-permute-start.14) | collective-permute-done | bytes 524320 | tf_op jit(solution)/shard_map/ppermute | solution.py:292
  65.1 10.1 %collective-permute-done.13.right_ref = bf16[512,512]{1,0:T(8,128)(2,1)S(1)} collective-permute-done((bf16[512,512]{1,0:T(8,128)(2,1)S(1)}, bf16[512,512]{1,0:T(8,128)(2,1)S(1)}, u32[]{:S(2)}, u32[]{:S(2)}) %collective-permute-start.13) | collective-permute-done | bytes 524320 | tf_op jit(solution)/shard_map/ppermute | solution.py:292
  75.2 0.0 collective-permute-done.12.left_ref
  75.2 1.8 %own_part.1.part_ref = f32[4,512,512]{2,1,0:T(8,128)S(1)} custom-call(s32[3]{0:T(128)S(1)} %pad_add_fusion.info_ref, bf16[512,512]{1,0:T(8,128)(2,1)S(1)} %attend1.1.own_ref, bf16[512,4096]{1,0:T(8,128)(2,1)S(1)} %copy-done.1), custom_call_target="tpu_custom_call" | custom-call | flops 1000000000 | bytes 1 | tf_op jit(solution)/shard_map/own_part/pallas_call | solution.py:261
  77.0 0.0 collective-permute-done.15.peer_ref
  77.1 0.0 collective-permute-done.16.wm_ref
  77.1 0.1 collective-permute-start.17
  77.2 2.6 %collective-permute-done.17.wp_ref = bf16[1024,512]{1,0:T(8,128)(2,1)S(1)} collective-permute-done((bf16[1024,512]{1,0:T(8,128)(2,1)S(1)}, bf16[1024,512]{1,0:T(8,128)(2,1)S(1)}, u32[]{:S(2)}, u32[]{:S(2)}) %collective-permute-start.17) | collective-permute-done | bytes 1048608 | tf_op jit(solution)/shard_map/ppermute | solution.py:287
  79.8 1.9 %reduce_first.1 = (bf16[512,512]{1,0:T(8,128)(2,1)S(1)}, bf16[512,512]{1,0:T(8,128)(2,1)S(1)}, bf16[512,512]{1,0:T(8,128)(2,1)S(1)}, bf16[512,512]{1,0:T(8,128)(2,1)S(1)}) custom-call(s32[3]{0:T(128)S(1)} %pad_add_fusion.info_ref, bf16[512,512]{1,0:T(8,128)(2,1)S(1)} %collective-permute-done.15.peer_ref, f32[4,512,512]{2,1,0:T(8,128)S(1)} %own_part.1.part_ref, ...), custom_call_target="tpu_custom_call" | custom-call | bytes 1 | tf_op jit(solution)/shard_map/reduce_first/pallas_call | solution.py:261
  81.7 0.2 collective-permute-start.18
  81.9 0.4 collective-permute-start.19
  82.3 1.4 %collective-permute-start.22 = (bf16[512,512]{1,0:T(8,128)(2,1)S(1)}, bf16[512,512]{1,0:T(8,128)(2,1)S(1)}, u32[]{:S(2)}, u32[]{:S(2)}) collective-permute-start(bf16[512,512]{1,0:T(8,128)(2,1)S(1)} %get-tuple-element.45), channel_id=1, source_target_pairs={{0,2},{1,3},{2,4},{3,5},{4,6},{5,7},{6,0},{7,1},{8,10},{9,11},{10,... | collective-permute-start | bytes 1572872 | tf_op jit(solution)/shard_map/ppermute | solution.py:292
  83.7 1.8 %collective-permute-start.23 = (bf16[512,512]{1,0:T(8,128)(2,1)S(1)}, bf16[512,512]{1,0:T(8,128)(2,1)S(1)}, u32[]{:S(2)}, u32[]{:S(2)}) collective-permute-start(bf16[512,512]{1,0:T(8,128)(2,1)S(1)} %get-tuple-element.46), channel_id=1, source_target_pairs={{0,6},{1,7},{2,0},{3,1},{4,2},{5,3},{6,4},{7,5},{8,14},{9,15},{10,... | collective-permute-start | bytes 1572872 | tf_op jit(solution)/shard_map/ppermute | solution.py:292
  85.5 1.7 %collective-permute-start.21 = (bf16[512,512]{1,0:T(8,128)(2,1)S(1)}, bf16[512,512]{1,0:T(8,128)(2,1)S(1)}, u32[]{:S(2)}, u32[]{:S(2)}) collective-permute-start(bf16[512,512]{1,0:T(8,128)(2,1)S(1)} %get-tuple-element.39), channel_id=1, source_target_pairs={{0,4},{1,5},{2,6},{3,7},{4,0},{5,1},{6,2},{7,3},{8,12},{9,13},{10,... | collective-permute-start | bytes 1572872 | tf_op jit(solution)/shard_map/ppermute | solution.py:292
  87.2 2.9 %gather_first.1 = (bf16[512,512]{1,0:T(8,128)(2,1)S(1)}, bf16[512,512]{1,0:T(8,128)(2,1)S(1)}) custom-call(s32[3]{0:T(128)S(1)} %pad_add_fusion.info_ref, bf16[512,512]{1,0:T(8,128)(2,1)S(1)} %attend0.1.own_ref, bf16[512,512]{1,0:T(8,128)(2,1)S(1)} %collective-permute-done.12.left_ref, bf16[512,512]{1,0:T(8,128)(2,1)S(1)} %collective-permute-done.13.right_ref, ...), custom_call_target="tpu_custom_call" | custom-call | bytes 1 | tf_op jit(solution)/shard_map/gather_first/pallas_call | solution.py:261
  90.1 0.1 collective-permute-start.20
  90.2 7.2 %collective-permute-done.22.refs_1_ = bf16[512,512]{1,0:T(8,128)(2,1)S(1)} collective-permute-done((bf16[512,512]{1,0:T(8,128)(2,1)S(1)}, bf16[512,512]{1,0:T(8,128)(2,1)S(1)}, u32[]{:S(2)}, u32[]{:S(2)}) %collective-permute-start.22) | collective-permute-done | bytes 524320 | tf_op jit(solution)/shard_map/ppermute | solution.py:292
  97.5 10.5 %collective-permute-done.23.refs_2_ = bf16[512,512]{1,0:T(8,128)(2,1)S(1)} collective-permute-done((bf16[512,512]{1,0:T(8,128)(2,1)S(1)}, bf16[512,512]{1,0:T(8,128)(2,1)S(1)}, u32[]{:S(2)}, u32[]{:S(2)}) %collective-permute-start.23) | collective-permute-done | bytes 524320 | tf_op jit(solution)/shard_map/ppermute | solution.py:292
  108.0 1.6 %collective-permute-done.21.refs_0_ = bf16[512,512]{1,0:T(8,128)(2,1)S(1)} collective-permute-done((bf16[512,512]{1,0:T(8,128)(2,1)S(1)}, bf16[512,512]{1,0:T(8,128)(2,1)S(1)}, u32[]{:S(2)}, u32[]{:S(2)}) %collective-permute-start.21) | collective-permute-done | bytes 524320 | tf_op jit(solution)/shard_map/ppermute | solution.py:292
  109.6 0.8 total.1.done_ref
  110.4 1.7 %finish.1 = bf16[2,512,512]{2,1,0:T(8,128)(2,1)} custom-call(s32[3]{0:T(128)S(1)} %pad_add_fusion.info_ref, bf16[512,512]{1,0:T(8,128)(2,1)S(1)} %get-tuple-element.42.keep_ref, bf16[512,512]{1,0:T(8,128)(2,1)S(1)} %collective-permute-done.20.got_ref, bf16[512,512]{1,0:T(8,128)(2,1)S(1)} %total.1.done_ref), custom_call_target="tpu_custom_call" | custom-call | bytes 1 | tf_op jit(solution)/shard_map/finish/pallas_call | solution.py:261
  (16 shorter events, 0.1 us)
Async XLA Ops:
  0.0 32.0 %copy-start.6 = (s32[2,512]{1,0:T(2,128)S(1)}, s32[2,512]{1,0:T(2,128)}, u32[]{:S(2)}) copy-start(s32[2,512]{1,0:T(2,128)} %param.8) | copy-start | bytes 12292
  1.2 16.2 %collective-permute-start = (bf16[2,512,128]{2,1,0:T(8,128)(2,1)S(1)}, bf16[2,512,128]{2,1,0:T(8,128)(2,1)S(1)}, u32[]{:S(2)}, u32[]{:S(2)}) collective-permute-start(bf16[2,512,128]{2,1,0:T(8,128)(2,1)S(1)} %pad_maximum_fusion.own_ref), channel_id=1, source_target_pairs={{0,8},{8,0},{16,24},{24,16},{32,40},{40,32},{48,56},{56,48},{64,72... | collective-permute-start | bytes 786440 | tf_op jit(solution)/shard_map/ppermute | solution.py:287
  1.3 16.1 %collective-permute-start.3 = (bf16[2,512,128]{2,1,0:T(8,128)(2,1)S(1)}, bf16[2,512,128]{2,1,0:T(8,128)(2,1)S(1)}, u32[]{:S(2)}, u32[]{:S(2)}) collective-permute-start(bf16[2,512,128]{2,1,0:T(8,128)(2,1)S(1)} %pad_maximum_fusion.1.own_ref), channel_id=1, source_target_pairs={{0,8},{8,0},{16,24},{24,16},{32,40},{40,32},{48,56},{56,48},{64,72... | collective-permute-start | bytes 786440 | tf_op jit(solution)/shard_map/ppermute | solution.py:287
  1.9 15.5 %collective-permute-start.1 = (bf16[2,512,128]{2,1,0:T(8,128)(2,1)S(1)}, bf16[2,512,128]{2,1,0:T(8,128)(2,1)}, u32[]{:S(2)}, u32[]{:S(2)}) collective-permute-start(bf16[2,512,128]{2,1,0:T(8,128)(2,1)S(1)} %pad_maximum_fusion.own_ref), channel_id=1, source_target_pairs={{0,16},{8,24},{16,32},{24,40},{32,48},{40,56},{48,64},{56,72},{64,... | collective-permute-start | bytes 786440 | tf_op jit(solution)/shard_map/ppermute | solution.py:287
  5.7 12.3 %collective-permute-start.2 = (bf16[2,512,128]{2,1,0:T(8,128)(2,1)S(1)}, bf16[2,512,128]{2,1,0:T(8,128)(2,1)S(1)}, u32[]{:S(2)}, u32[]{:S(2)}) collective-permute-start(bf16[2,512,128]{2,1,0:T(8,128)(2,1)S(1)} %pad_maximum_fusion.1.own_ref), channel_id=1, source_target_pairs={{16,0},{24,8},{32,16},{40,24},{48,32},{56,40},{64,48},{72,56},{80,... | collective-permute-start | bytes 786440 | tf_op jit(solution)/shard_map/ppermute | solution.py:287
  12.4 2.2 %copy-start = (bf16[512,4096]{1,0:T(8,128)(2,1)S(1)}, bf16[512,4096]{1,0:T(8,128)(2,1)}, u32[]{:S(2)}) copy-start(bf16[512,4096]{1,0:T(8,128)(2,1)} %w_ref.5) | copy-start | bytes 12582916
  16.4 1.0 copy-start.3
  18.0 14.0 %collective-permute-start.6 = (bf16[2,512,128]{2,1,0:T(8,128)(2,1)}, bf16[2,512,128]{2,1,0:T(8,128)(2,1)}, u32[]{:S(2)}, u32[]{:S(2)}) collective-permute-start(bf16[2,512,128]{2,1,0:T(8,128)(2,1)} %collective-permute-done.1.near_ref.fold_near_ref), channel_id=1, source_target_pairs={{0,16},{8,24},{16,32},{24,40},{32,48},{40,56},{48,64},{56,72},{64,... | collective-permute-start | bytes 786440 | tf_op jit(solution)/shard_map/ppermute | solution.py:287
  19.9 28.8 %collective-permute-start.10 = (bf16[512,1024]{1,0:T(8,128)(2,1)}, bf16[512,1024]{1,0:T(8,128)(2,1)S(1)}, u32[]{:S(2)}, u32[]{:S(2)}) collective-permute-start(bf16[512,1024]{1,0:T(8,128)(2,1)} %get-tuple-element.31), channel_id=1, source_target_pairs={{0,2},{1,3},{2,4},{3,5},{4,6},{5,7},{6,0},{7,1},{8,14},{9,15},{10,... | collective-permute-start | bytes 3145736 | tf_op jit(solution)/shard_map/ppermute | solution.py:320
  21.5 10.5 %collective-permute-start.5 = (bf16[2,512,128]{2,1,0:T(8,128)(2,1)S(1)}, bf16[2,512,128]{2,1,0:T(8,128)(2,1)S(1)}, u32[]{:S(2)}, u32[]{:S(2)}) collective-permute-start(bf16[2,512,128]{2,1,0:T(8,128)(2,1)S(1)} %broadcast_select_fusion.near_ref), channel_id=1, source_target_pairs={{0,8},{8,0},{16,24},{24,16},{32,40},{40,32},{48,56},{56,48},{64,72... | collective-permute-start | bytes 786440 | tf_op jit(solution)/shard_map/ppermute | solution.py:287
  21.8 14.5 %collective-permute-start.8 = (bf16[2,512,128]{2,1,0:T(8,128)(2,1)S(1)}, bf16[2,512,128]{2,1,0:T(8,128)(2,1)}, u32[]{:S(2)}, u32[]{:S(2)}) collective-permute-start(bf16[2,512,128]{2,1,0:T(8,128)(2,1)S(1)} %broadcast_select_fusion.near_ref), channel_id=1, source_target_pairs={{16,0},{24,8},{32,16},{40,24},{48,32},{56,40},{64,48},{72,56},{80,... | collective-permute-start | bytes 786440 | tf_op jit(solution)/shard_map/ppermute | solution.py:287
  29.8 6.5 %collective-permute-start.4 = (bf16[2,512,128]{2,1,0:T(8,128)(2,1)}, bf16[2,512,128]{2,1,0:T(8,128)(2,1)}, u32[]{:S(2)}, u32[]{:S(2)}) collective-permute-start(bf16[2,512,128]{2,1,0:T(8,128)(2,1)} %collective-permute-done.1.near_ref.fold_near_ref), channel_id=1, source_target_pairs={{0,8},{8,0},{16,24},{24,16},{32,40},{40,32},{48,56},{56,48},{64,72... | collective-permute-start | bytes 786440 | tf_op jit(solution)/shard_map/ppermute | solution.py:287
  32.0 4.7 %collective-permute-start.7 = (bf16[2,512,128]{2,1,0:T(8,128)(2,1)}, bf16[2,512,128]{2,1,0:T(8,128)(2,1)}, u32[]{:S(2)}, u32[]{:S(2)}) collective-permute-start(bf16[2,512,128]{2,1,0:T(8,128)(2,1)} %collective-permute-done.6.far_ref), channel_id=1, source_target_pairs={{0,8},{8,0},{16,24},{24,16},{32,40},{40,32},{48,56},{56,48},{64,72... | collective-permute-start | bytes 786440 | tf_op jit(solution)/shard_map/ppermute | solution.py:287
  32.0 0.7 copy-start.4
  32.7 16.0 %collective-permute-start.11 = (bf16[256,1024]{1,0:T(8,128)(2,1)}, bf16[256,1024]{1,0:T(8,128)(2,1)S(1)}, u32[]{:S(2)}, u32[]{:S(2)}) collective-permute-start(bf16[256,1024]{1,0:T(8,128)(2,1)} %get-tuple-element.33), channel_id=1, source_target_pairs={{0,4},{1,5},{2,6},{3,7},{4,0},{5,1},{6,2},{7,3},{8,12},{9,13},{10,... | collective-permute-start | bytes 1572872 | tf_op jit(solution)/shard_map/ppermute | solution.py:292
  36.3 40.8 %collective-permute-start.16 = (bf16[1024,512]{1,0:T(8,128)(2,1)}, bf16[1024,512]{1,0:T(8,128)(2,1)S(1)}, u32[]{:S(2)}, u32[]{:S(2)}) collective-permute-start(bf16[1024,512]{1,0:T(8,128)(2,1)} %copy-done.3), channel_id=1, source_target_pairs={{0,1},{1,0},{2,3},{3,2},{4,5},{5,4},{6,7},{7,6},{8,9},{9,8},{10,11... | collective-permute-start | bytes 3145736 | tf_op jit(solution)/shard_map/ppermute | solution.py:292
  36.3 10.7 %collective-permute-start.9 = (bf16[2,512,128]{2,1,0:T(8,128)(2,1)}, bf16[2,512,128]{2,1,0:T(8,128)(2,1)S(1)}, u32[]{:S(2)}, u32[]{:S(2)}) collective-permute-start(bf16[2,512,128]{2,1,0:T(8,128)(2,1)} %collective-permute-done.8.far_ref), channel_id=1, source_target_pairs={{0,8},{8,0},{16,24},{24,16},{32,40},{40,32},{48,56},{56,48},{64,72... | collective-permute-start | bytes 786440 | tf_op jit(solution)/shard_map/ppermute | solution.py:287
  36.6 1.2 %copy-start.2 = (bf16[2,512,512]{2,1,0:T(8,128)(2,1)S(1)}, bf16[2,512,512]{2,1,0:T(8,128)(2,1)}, u32[]{:S(2)}) copy-start(bf16[2,512,512]{2,1,0:T(8,128)(2,1)} %q_ref.3) | copy-start | bytes 3145732
  37.9 16.0 %copy-start.5 = (bf16[2,512,128]{2,1,0:T(8,128)(2,1)S(1)}, bf16[2,512,128]{2,1,0:T(8,128)(2,1)}, u32[]{:S(2)}) copy-start(bf16[2,512,128]{2,1,0:T(8,128)(2,1)} %copy-done.4) | copy-start | bytes 786436
  47.1 28.2 %copy-start.1 = (bf16[512,4096]{1,0:T(8,128)(2,1)S(1)}, bf16[512,4096]{1,0:T(8,128)(2,1)}, u32[]{:S(2)}) copy-start(bf16[512,4096]{1,0:T(8,128)(2,1)} %w_ref.5) | copy-start | bytes 12582916
  48.7 16.4 %collective-permute-start.14 = (bf16[512,512]{1,0:T(8,128)(2,1)S(1)}, bf16[512,512]{1,0:T(8,128)(2,1)S(1)}, u32[]{:S(2)}, u32[]{:S(2)}) collective-permute-start(bf16[512,512]{1,0:T(8,128)(2,1)S(1)} %attend0.1.own_ref), channel_id=1, source_target_pairs={{0,4},{1,5},{2,6},{3,7},{4,0},{5,1},{6,2},{7,3},{8,12},{9,13},{10,... | collective-permute-start | bytes 1572872 | tf_op jit(solution)/shard_map/ppermute | solution.py:292
  51.8 23.4 %collective-permute-start.13 = (bf16[512,512]{1,0:T(8,128)(2,1)S(1)}, bf16[512,512]{1,0:T(8,128)(2,1)S(1)}, u32[]{:S(2)}, u32[]{:S(2)}) collective-permute-start(bf16[512,512]{1,0:T(8,128)(2,1)S(1)} %attend0.1.own_ref), channel_id=1, source_target_pairs={{0,6},{1,7},{2,0},{3,1},{4,2},{5,3},{6,4},{7,5},{8,14},{9,15},{10,... | collective-permute-start | bytes 1572872 | tf_op jit(solution)/shard_map/ppermute | solution.py:292
  53.0 22.2 %collective-permute-start.12 = (bf16[512,512]{1,0:T(8,128)(2,1)S(1)}, bf16[512,512]{1,0:T(8,128)(2,1)S(1)}, u32[]{:S(2)}, u32[]{:S(2)}) collective-permute-start(bf16[512,512]{1,0:T(8,128)(2,1)S(1)} %attend0.1.own_ref), channel_id=1, source_target_pairs={{0,2},{1,3},{2,4},{3,5},{4,6},{5,7},{6,0},{7,1},{8,10},{9,11},{10,... | collective-permute-start | bytes 1572872 | tf_op jit(solution)/shard_map/ppermute | solution.py:292
  62.9 14.2 %collective-permute-start.15 = (bf16[512,512]{1,0:T(8,128)(2,1)S(1)}, bf16[512,512]{1,0:T(8,128)(2,1)S(1)}, u32[]{:S(2)}, u32[]{:S(2)}) collective-permute-start(bf16[512,512]{1,0:T(8,128)(2,1)S(1)} %attend1.1.own_ref), channel_id=1, source_target_pairs={{0,1},{1,0},{2,3},{3,2},{4,5},{5,4},{6,7},{7,6},{8,9},{9,8},{10,11... | collective-permute-start | bytes 1572872 | tf_op jit(solution)/shard_map/ppermute | solution.py:292
  77.1 2.7 %collective-permute-start.17 = (bf16[1024,512]{1,0:T(8,128)(2,1)S(1)}, bf16[1024,512]{1,0:T(8,128)(2,1)S(1)}, u32[]{:S(2)}, u32[]{:S(2)}) collective-permute-start(bf16[1024,512]{1,0:T(8,128)(2,1)S(1)} %collective-permute-done.16.wm_ref), channel_id=1, source_target_pairs={{0,8},{8,0},{16,24},{24,16},{32,40},{40,32},{48,56},{56,48},{64,72... | collective-permute-start | bytes 3145736 | tf_op jit(solution)/shard_map/ppermute | solution.py:287
  81.7 5.5 %collective-permute-start.18 = (bf16[512,1024]{1,0:T(8,128)(2,1)S(1)}, bf16[512,1024]{1,0:T(8,128)(2,1)S(1)}, u32[]{:S(2)}, u32[]{:S(2)}) collective-permute-start(bf16[512,1024]{1,0:T(8,128)(2,1)S(1)} %collective-permute-done.10.ws_ref), channel_id=1, source_target_pairs={{0,8},{8,0},{16,24},{24,16},{32,40},{40,32},{48,56},{56,48},{64,72... | collective-permute-start | bytes 3145736 | tf_op jit(solution)/shard_map/ppermute | solution.py:287
  81.9 5.3 %collective-permute-start.19 = (bf16[256,1024]{1,0:T(8,128)(2,1)S(1)}, bf16[256,1024]{1,0:T(8,128)(2,1)S(1)}, u32[]{:S(2)}, u32[]{:S(2)}) collective-permute-start(bf16[256,1024]{1,0:T(8,128)(2,1)S(1)} %collective-permute-done.11.wf_ref), channel_id=1, source_target_pairs={{0,8},{8,0},{16,24},{24,16},{32,40},{40,32},{48,56},{56,48},{64,72... | collective-permute-start | bytes 1572872 | tf_op jit(solution)/shard_map/ppermute | solution.py:287
  82.3 15.2 %collective-permute-start.22 = (bf16[512,512]{1,0:T(8,128)(2,1)S(1)}, bf16[512,512]{1,0:T(8,128)(2,1)S(1)}, u32[]{:S(2)}, u32[]{:S(2)}) collective-permute-start(bf16[512,512]{1,0:T(8,128)(2,1)S(1)} %get-tuple-element.45), channel_id=1, source_target_pairs={{0,2},{1,3},{2,4},{3,5},{4,6},{5,7},{6,0},{7,1},{8,10},{9,11},{10,... | collective-permute-start | bytes 1572872 | tf_op jit(solution)/shard_map/ppermute | solution.py:292
  83.7 24.3 %collective-permute-start.23 = (bf16[512,512]{1,0:T(8,128)(2,1)S(1)}, bf16[512,512]{1,0:T(8,128)(2,1)S(1)}, u32[]{:S(2)}, u32[]{:S(2)}) collective-permute-start(bf16[512,512]{1,0:T(8,128)(2,1)S(1)} %get-tuple-element.46), channel_id=1, source_target_pairs={{0,6},{1,7},{2,0},{3,1},{4,2},{5,3},{6,4},{7,5},{8,14},{9,15},{10,... | collective-permute-start | bytes 1572872 | tf_op jit(solution)/shard_map/ppermute | solution.py:292
  85.5 24.0 %collective-permute-start.21 = (bf16[512,512]{1,0:T(8,128)(2,1)S(1)}, bf16[512,512]{1,0:T(8,128)(2,1)S(1)}, u32[]{:S(2)}, u32[]{:S(2)}) collective-permute-start(bf16[512,512]{1,0:T(8,128)(2,1)S(1)} %get-tuple-element.39), channel_id=1, source_target_pairs={{0,4},{1,5},{2,6},{3,7},{4,0},{5,1},{6,2},{7,3},{8,12},{9,13},{10,... | collective-permute-start | bytes 1572872 | tf_op jit(solution)/shard_map/ppermute | solution.py:292
  90.1 20.2 %collective-permute-start.20 = (bf16[512,512]{1,0:T(8,128)(2,1)S(1)}, bf16[512,512]{1,0:T(8,128)(2,1)S(1)}, u32[]{:S(2)}, u32[]{:S(2)}) collective-permute-start(bf16[512,512]{1,0:T(8,128)(2,1)S(1)} %get-tuple-element.43), channel_id=1, source_target_pairs={{0,1},{1,0},{2,3},{3,2},{4,5},{5,4},{6,7},{7,6},{8,9},{9,8},{10,11... | collective-permute-start | bytes 1572872 | tf_op jit(solution)/shard_map/ppermute | solution.py:292

commit v3 on v2

--- a/solution.py
+++ b/solution.py
@@ -353,9 +353,9 @@
     piece = jax.ShapeDtypeStruct((blk, width), BF16)
     [part] = project(
         own_part_kernel, "own_part", [jax.ShapeDtypeStruct((ring, blk, width), F32)],
-        [place, after(mixed1, left, right, opposite), out_weight], STEP,
-    )
-    w_peer2 = swap(after(w_peer, peer, part))
+        [place, after(mixed1, left, right, opposite), out_weight], 8 * STEP,
+    )
+    w_peer2 = swap(after(w_peer, mixed1))
     far, up, down, keep1 = project(
         reduce_first_kernel, "reduce_first", [piece] * 4, [place, peer, part, w_peer, w_peer2]
     )

time: 112 us -> 110 us (0.982)
  waiting for transfers between devices: 38.6 us -> 36 us
    ppermute x13, waiting for transfers between devices: 5.29 us -> 2.65 us  [ctx_move(): lax.ppermute(array, 'ctx', [(i, to(i)) for i in range(ctx_size) if 0 <= t...]
where the time goes in v3:
time: 110 us; the launch traced here: 109 us
  starting transfers between devices  37 us (34%)
  waiting for transfers between devices  36 us (33%)
  Pallas kernels  29 us (26%)
  local copies, waits for them, and re-layouts  6.55 us (6%)
    ppermute x10, waiting for transfers between devices, head_move(): return lax.ppermute(array, 'head', [(i, to(i)) for i in range(2 * ring)])  33.4 us
    ppermute x13, starting transfers between devices, ctx_move(): lax.ppermute(array, 'ctx', [(i, to(i)) for i in range(ctx_size) if 0 <= t...  22.3 us
    pallas_call x2, Pallas kernels, attention(): pl.pallas_call(functools.partial(attn_kernel, half), out_shape=[jax.Shape...  18.2 us
    ppermute x10, starting transfers between devices, head_move(): return lax.ppermute(array, 'head', [(i, to(i)) for i in range(2 * ring)])  13.1 us
    pallas_call x5, Pallas kernels, project(): pl.pallas_call(kernel, out_shape=outs, in_specs=[SMEM] + [VMEM] * (len(ar...  8.99 us
    unnamed x14, local copies, waits for them, and re-layouts  5.11 us
    ppermute x13, waiting for transfers between devices, ctx_move(): lax.ppermute(array, 'ctx', [(i, to(i)) for i in range(ctx_size) if 0 <= t...  2.65 us
  transfers between devices with their start and end apart: 24, of which 9 were waited for; matrix products, arithmetic and copies ran while one was open for 1% of the time, Pallas kernels for 23%

profile of v3, /device:TPU:24, one launch (start us, length us, event | category | flops | bytes accessed | tf_op | source)
XLA Modules:
  0.0 109.2 jit_solution(16462733409856483179)
XLA Ops:
  0.0 1.1 %fusion = (bf16[1,512,128]{2,1,0:T(8,128)(2,1)S(1)}, bf16[1,512,128]{2,1,0:T(8,128)(2,1)S(1)}, bf16[1,512,128]{2,1,0:T(8,128)(2,1)S(1)}, bf16[1,512,128]{2,1,0:T(8,128)(2,1)S(1)}) fusion(bf16[2,512,128]{2,1,0:T(8,128)(2,1)} %param.6, bf16[2,512,128]{2,1,0:T(8,128)(2,1)} %param.7), kind=kLoop, calls=%fused_computation.8 | loop fusion | bytes 1048576 | tf_op jit(solution)/shard_map/slice | solution.py:310
  1.2 0.1 collective-permute-start
  1.3 0.6 collective-permute-start.3
  1.9 3.8 %collective-permute-start.1 = (bf16[2,512,128]{2,1,0:T(8,128)(2,1)S(1)}, bf16[2,512,128]{2,1,0:T(8,128)(2,1)}, u32[]{:S(2)}, u32[]{:S(2)}) collective-permute-start(bf16[2,512,128]{2,1,0:T(8,128)(2,1)S(1)} %pad_maximum_fusion.own_ref), channel_id=1, source_target_pairs={{0,16},{8,24},{16,32},{24,40},{32,48},{40,56},{48,64},{56,72},{64,... | collective-permute-start | bytes 786440 | tf_op jit(solution)/shard_map/ppermute | solution.py:287
  5.7 6.5 %collective-permute-start.2 = (bf16[2,512,128]{2,1,0:T(8,128)(2,1)S(1)}, bf16[2,512,128]{2,1,0:T(8,128)(2,1)S(1)}, u32[]{:S(2)}, u32[]{:S(2)}) collective-permute-start(bf16[2,512,128]{2,1,0:T(8,128)(2,1)S(1)} %pad_maximum_fusion.1.own_ref), channel_id=1, source_target_pairs={{16,0},{24,8},{32,16},{40,24},{48,32},{56,40},{64,48},{72,56},{80,... | collective-permute-start | bytes 786440 | tf_op jit(solution)/shard_map/ppermute | solution.py:287
  12.3 0.1 pad_add_fusion.info_ref
  12.4 2.2 %copy-done = bf16[512,4096]{1,0:T(8,128)(2,1)S(1)} copy-done((bf16[512,4096]{1,0:T(8,128)(2,1)S(1)}, bf16[512,4096]{1,0:T(8,128)(2,1)}, u32[]{:S(2)}) %copy-start) | copy-done | bytes 4194328
  14.6 1.9 %split_weights.1 = (bf16[512,1024]{1,0:T(8,128)(2,1)}, bf16[256,1024]{1,0:T(8,128)(2,1)}, bf16[1024,512]{1,0:T(8,128)(2,1)S(1)}) custom-call(s32[3]{0:T(128)S(1)} %pad_add_fusion.info_ref, bf16[512,4096]{1,0:T(8,128)(2,1)S(1)} %copy-done), custom_call_target="tpu_custom_call" | custom-call | flops 1 | bytes 1 | tf_op jit(solution)/shard_map/split_weights/pallas_call | solution.py:172
  16.4 1.0 copy-done.3
  17.4 0.0 collective-permute-done.traded_ref
  17.4 0.0 collective-permute-done.3.traded_ref
  17.4 0.0 collective-permute-done.1.near_ref.fold_near_ref
  17.4 0.6 collective-permute-done.2
  18.0 1.9 %collective-permute-start.6 = (bf16[2,512,128]{2,1,0:T(8,128)(2,1)}, bf16[2,512,128]{2,1,0:T(8,128)(2,1)}, u32[]{:S(2)}, u32[]{:S(2)}) collective-permute-start(bf16[2,512,128]{2,1,0:T(8,128)(2,1)} %collective-permute-done.1.near_ref.fold_near_ref), channel_id=1, source_target_pairs={{0,16},{8,24},{16,32},{24,40},{32,48},{40,56},{48,64},{56,72},{64,... | collective-permute-start | bytes 786440 | tf_op jit(solution)/shard_map/ppermute | solution.py:287
  19.9 1.6 %collective-permute-start.10 = (bf16[512,1024]{1,0:T(8,128)(2,1)}, bf16[512,1024]{1,0:T(8,128)(2,1)S(1)}, u32[]{:S(2)}, u32[]{:S(2)}) collective-permute-start(bf16[512,1024]{1,0:T(8,128)(2,1)} %get-tuple-element.31), channel_id=1, source_target_pairs={{0,2},{1,3},{2,4},{3,5},{4,6},{5,7},{6,0},{7,1},{8,14},{9,15},{10,... | collective-permute-start | bytes 3145736 | tf_op jit(solution)/shard_map/ppermute | solution.py:320
  21.5 0.3 collective-permute-start.5
  21.8 8.0 %collective-permute-start.8 = (bf16[2,512,128]{2,1,0:T(8,128)(2,1)S(1)}, bf16[2,512,128]{2,1,0:T(8,128)(2,1)}, u32[]{:S(2)}, u32[]{:S(2)}) collective-permute-start(bf16[2,512,128]{2,1,0:T(8,128)(2,1)S(1)} %broadcast_select_fusion.near_ref), channel_id=1, source_target_pairs={{16,0},{24,8},{32,16},{40,24},{48,32},{56,40},{64,48},{72,56},{80,... | collective-permute-start | bytes 786440 | tf_op jit(solution)/shard_map/ppermute | solution.py:287
  29.8 0.2 collective-permute-start.4
  29.9 2.0 %collective-permute-done.6.far_ref = bf16[2,512,128]{2,1,0:T(8,128)(2,1)} collective-permute-done((bf16[2,512,128]{2,1,0:T(8,128)(2,1)}, bf16[2,512,128]{2,1,0:T(8,128)(2,1)}, u32[]{:S(2)}, u32[]{:S(2)}) %collective-permute-start.6) | collective-permute-done | bytes 262176 | tf_op jit(solution)/shard_map/ppermute | solution.py:287
  32.0 0.0 collective-permute-start.7
  32.0 0.0 collective-permute-done.5.near_traded_ref
  32.0 0.7 copy-done.4
  32.7 3.1 %collective-permute-start.11 = (bf16[256,1024]{1,0:T(8,128)(2,1)}, bf16[256,1024]{1,0:T(8,128)(2,1)S(1)}, u32[]{:S(2)}, u32[]{:S(2)}) collective-permute-start(bf16[256,1024]{1,0:T(8,128)(2,1)} %get-tuple-element.33), channel_id=1, source_target_pairs={{0,4},{1,5},{2,6},{3,7},{4,0},{5,1},{6,2},{7,3},{8,12},{9,13},{10,... | collective-permute-start | bytes 1572872 | tf_op jit(solution)/shard_map/ppermute | solution.py:292
  35.8 0.1 add_add_fusion.info_ref
  35.9 0.1 copy.7.doc_ref
  36.0 0.1 copy.6.doc_ref
  36.2 0.1 add_add_fusion.1.info_ref
  36.3 0.0 collective-permute-done.4.near_traded_ref.fold_traded_ref
  36.3 0.0 collective-permute-start.16
  36.3 0.0 collective-permute-done.8.far_ref
  36.3 0.3 collective-permute-start.9
  36.6 0.0 collective-permute-done.7.far_traded_ref
  36.6 1.2 %copy-done.2 = bf16[2,512,512]{2,1,0:T(8,128)(2,1)S(1)} copy-done((bf16[2,512,512]{2,1,0:T(8,128)(2,1)S(1)}, bf16[2,512,512]{2,1,0:T(8,128)(2,1)}, u32[]{:S(2)}) %copy-start.2) | copy-done | bytes 1048600
  37.9 9.2 %attend0.1.own_ref = bf16[512,512]{1,0:T(8,128)(2,1)S(1)} custom-call(s32[3]{0:T(128)S(1)} %add_add_fusion.info_ref, bf16[2,512,512]{2,1,0:T(8,128)(2,1)S(1)} %copy-done.2, s32[512,1]{1,0:T(8,128)S(1)} %copy.6.doc_ref, bf16[2,512,128]{2,1,0:T(8,128)(2,1)S(1)} %pad_maximum_fusion.own_ref, bf16[2,512,128]{2,1,0:T(8,128)(2,1)S(1)} %collective-permute-done.traded_ref, ...), custom_call_target="tpu_custom_call" | custom-call | flops 4000000000 | bytes 1 | tf_op jit(solution)/shard_map/attend0/pallas_call | solution.py:135
  47.1 0.0 copy-start.1
  47.1 0.0 collective-permute-done.9.far_traded_ref
  47.1 1.7 %collective-permute-done.11.wf_ref = bf16[256,1024]{1,0:T(8,128)(2,1)S(1)} collective-permute-done((bf16[256,1024]{1,0:T(8,128)(2,1)}, bf16[256,1024]{1,0:T(8,128)(2,1)S(1)}, u32[]{:S(2)}, u32[]{:S(2)}) %collective-permute-start.11) | collective-permute-done | bytes 524320 | tf_op jit(solution)/shard_map/ppermute | solution.py:292
  48.7 0.0 collective-permute-done.10.ws_ref
  48.7 3.1 %collective-permute-start.14 = (bf16[512,512]{1,0:T(8,128)(2,1)S(1)}, bf16[512,512]{1,0:T(8,128)(2,1)S(1)}, u32[]{:S(2)}, u32[]{:S(2)}) collective-permute-start(bf16[512,512]{1,0:T(8,128)(2,1)S(1)} %attend0.1.own_ref), channel_id=1, source_target_pairs={{0,4},{1,5},{2,6},{3,7},{4,0},{5,1},{6,2},{7,3},{8,12},{9,13},{10,... | collective-permute-start | bytes 1572872 | tf_op jit(solution)/shard_map/ppermute | solution.py:292
  51.8 1.1 %collective-permute-start.13 = (bf16[512,512]{1,0:T(8,128)(2,1)S(1)}, bf16[512,512]{1,0:T(8,128)(2,1)S(1)}, u32[]{:S(2)}, u32[]{:S(2)}) collective-permute-start(bf16[512,512]{1,0:T(8,128)(2,1)S(1)} %attend0.1.own_ref), channel_id=1, source_target_pairs={{0,6},{1,7},{2,0},{3,1},{4,2},{5,3},{6,4},{7,5},{8,14},{9,15},{10,... | collective-permute-start | bytes 1572872 | tf_op jit(solution)/shard_map/ppermute | solution.py:292
  53.0 0.9 collective-permute-start.12
  53.9 9.0 %attend1.1.own_ref = bf16[512,512]{1,0:T(8,128)(2,1)S(1)} custom-call(s32[3]{0:T(128)S(1)} %add_add_fusion.1.info_ref, bf16[2,512,512]{2,1,0:T(8,128)(2,1)S(1)} %copy-done.2, s32[512,1]{1,0:T(8,128)S(1)} %copy.7.doc_ref, bf16[2,512,128]{2,1,0:T(8,128)(2,1)S(1)} %pad_maximum_fusion.1.own_ref, bf16[2,512,128]{2,1,0:T(8,128)(2,1)S(1)} %collective-permute-done.3.traded_ref, ...), custom_call_target="tpu_custom_call" | custom-call | flops 10737418240 | bytes 4194304 | tf_op jit(solution)/shard_map/attend1/pallas_call | solution.py:135
  62.9 0.0 collective-permute-done.16.wm_ref
  62.9 0.1 collective-permute-start.17
  63.0 0.1 collective-permute-start.15
  63.1 2.0 %collective-permute-done.14.far_ref = bf16[512,512]{1,0:T(8,128)(2,1)S(1)} collective-permute-done((bf16[512,512]{1,0:T(8,128)(2,1)S(1)}, bf16[512,512]{1,0:T(8,128)(2,1)S(1)}, u32[]{:S(2)}, u32[]{:S(2)}) %collective-permute-start.14) | collective-permute-done | bytes 524320 | tf_op jit(solution)/shard_map/ppermute | solution.py:292
  65.1 10.1 %collective-permute-done.13.right_ref = bf16[512,512]{1,0:T(8,128)(2,1)S(1)} collective-permute-done((bf16[512,512]{1,0:T(8,128)(2,1)S(1)}, bf16[512,512]{1,0:T(8,128)(2,1)S(1)}, u32[]{:S(2)}, u32[]{:S(2)}) %collective-permute-start.13) | collective-permute-done | bytes 524320 | tf_op jit(solution)/shard_map/ppermute | solution.py:292
  75.2 1.8 %own_part.1.part_ref = f32[4,512,512]{2,1,0:T(8,128)S(1)} custom-call(s32[3]{0:T(128)S(1)} %pad_add_fusion.info_ref, bf16[512,512]{1,0:T(8,128)(2,1)S(1)} %attend1.1.own_ref, bf16[512,4096]{1,0:T(8,128)(2,1)S(1)} %copy-done.1), custom_call_target="tpu_custom_call" | custom-call | flops 8000000000 | bytes 1 | tf_op jit(solution)/shard_map/own_part/pallas_call | solution.py:261
  77.0 0.3 collective-permute-done.15.peer_ref
  77.3 1.8 %reduce_first.1 = (bf16[512,512]{1,0:T(8,128)(2,1)S(1)}, bf16[512,512]{1,0:T(8,128)(2,1)S(1)}, bf16[512,512]{1,0:T(8,128)(2,1)S(1)}, bf16[512,512]{1,0:T(8,128)(2,1)S(1)}) custom-call(s32[3]{0:T(128)S(1)} %pad_add_fusion.info_ref, bf16[512,512]{1,0:T(8,128)(2,1)S(1)} %collective-permute-done.15.peer_ref, f32[4,512,512]{2,1,0:T(8,128)S(1)} %own_part.1.part_ref, ...), custom_call_target="tpu_custom_call" | custom-call | bytes 1 | tf_op jit(solution)/shard_map/reduce_first/pallas_call | solution.py:261
  79.1 0.1 collective-permute-start.18
  79.2 0.5 collective-permute-start.19
  79.7 1.2 %collective-permute-start.22 = (bf16[512,512]{1,0:T(8,128)(2,1)S(1)}, bf16[512,512]{1,0:T(8,128)(2,1)S(1)}, u32[]{:S(2)}, u32[]{:S(2)}) collective-permute-start(bf16[512,512]{1,0:T(8,128)(2,1)S(1)} %get-tuple-element.45), channel_id=1, source_target_pairs={{0,2},{1,3},{2,4},{3,5},{4,6},{5,7},{6,0},{7,1},{8,10},{9,11},{10,... | collective-permute-start | bytes 1572872 | tf_op jit(solution)/shard_map/ppermute | solution.py:292
  80.9 2.1 %collective-permute-start.23 = (bf16[512,512]{1,0:T(8,128)(2,1)S(1)}, bf16[512,512]{1,0:T(8,128)(2,1)S(1)}, u32[]{:S(2)}, u32[]{:S(2)}) collective-permute-start(bf16[512,512]{1,0:T(8,128)(2,1)S(1)} %get-tuple-element.46), channel_id=1, source_target_pairs={{0,6},{1,7},{2,0},{3,1},{4,2},{5,3},{6,4},{7,5},{8,14},{9,15},{10,... | collective-permute-start | bytes 1572872 | tf_op jit(solution)/shard_map/ppermute | solution.py:292
  83.0 1.4 %collective-permute-start.21 = (bf16[512,512]{1,0:T(8,128)(2,1)S(1)}, bf16[512,512]{1,0:T(8,128)(2,1)S(1)}, u32[]{:S(2)}, u32[]{:S(2)}) collective-permute-start(bf16[512,512]{1,0:T(8,128)(2,1)S(1)} %get-tuple-element.39), channel_id=1, source_target_pairs={{0,4},{1,5},{2,6},{3,7},{4,0},{5,1},{6,2},{7,3},{8,12},{9,13},{10,... | collective-permute-start | bytes 1572872 | tf_op jit(solution)/shard_map/ppermute | solution.py:292
  84.4 0.0 collective-permute-done.19.wfp_ref
  84.4 0.0 collective-permute-done.18.wsp_ref
  84.4 2.9 %gather_first.1 = (bf16[512,512]{1,0:T(8,128)(2,1)S(1)}, bf16[512,512]{1,0:T(8,128)(2,1)S(1)}) custom-call(s32[3]{0:T(128)S(1)} %pad_add_fusion.info_ref, bf16[512,512]{1,0:T(8,128)(2,1)S(1)} %attend0.1.own_ref, bf16[512,512]{1,0:T(8,128)(2,1)S(1)} %collective-permute-done.12.left_ref, bf16[512,512]{1,0:T(8,128)(2,1)S(1)} %collective-permute-done.13.right_ref, ...), custom_call_target="tpu_custom_call" | custom-call | bytes 1 | tf_op jit(solution)/shard_map/gather_first/pallas_call | solution.py:261
  87.3 0.1 collective-permute-start.20
  87.4 7.7 %collective-permute-done.22.refs_1_ = bf16[512,512]{1,0:T(8,128)(2,1)S(1)} collective-permute-done((bf16[512,512]{1,0:T(8,128)(2,1)S(1)}, bf16[512,512]{1,0:T(8,128)(2,1)S(1)}, u32[]{:S(2)}, u32[]{:S(2)}) %collective-permute-start.22) | collective-permute-done | bytes 524320 | tf_op jit(solution)/shard_map/ppermute | solution.py:292
  95.1 10.3 %collective-permute-done.23.refs_2_ = bf16[512,512]{1,0:T(8,128)(2,1)S(1)} collective-permute-done((bf16[512,512]{1,0:T(8,128)(2,1)S(1)}, bf16[512,512]{1,0:T(8,128)(2,1)S(1)}, u32[]{:S(2)}, u32[]{:S(2)}) %collective-permute-start.23) | collective-permute-done | bytes 524320 | tf_op jit(solution)/shard_map/ppermute | solution.py:292
  105.4 1.3 %collective-permute-done.21.refs_0_ = bf16[512,512]{1,0:T(8,128)(2,1)S(1)} collective-permute-done((bf16[512,512]{1,0:T(8,128)(2,1)S(1)}, bf16[512,512]{1,0:T(8,128)(2,1)S(1)}, u32[]{:S(2)}, u32[]{:S(2)}) %collective-permute-start.21) | collective-permute-done | bytes 524320 | tf_op jit(solution)/shard_map/ppermute | solution.py:292
  106.7 0.8 total.1.done_ref
  107.5 1.7 %finish.1 = bf16[2,512,512]{2,1,0:T(8,128)(2,1)} custom-call(s32[3]{0:T(128)S(1)} %pad_add_fusion.info_ref, bf16[512,512]{1,0:T(8,128)(2,1)S(1)} %get-tuple-element.42.keep_ref, bf16[512,512]{1,0:T(8,128)(2,1)S(1)} %collective-permute-done.20.got_ref, bf16[512,512]{1,0:T(8,128)(2,1)S(1)} %total.1.done_ref), custom_call_target="tpu_custom_call" | custom-call | bytes 1 | tf_op jit(solution)/shard_map/finish/pallas_call | solution.py:261
  (16 shorter events, 0.1 us)
Async XLA Ops:
  0.0 32.0 %copy-start.6 = (s32[2,512]{1,0:T(2,128)S(1)}, s32[2,512]{1,0:T(2,128)}, u32[]{:S(2)}) copy-start(s32[2,512]{1,0:T(2,128)} %param.8) | copy-start | bytes 12292
  1.2 16.2 %collective-permute-start = (bf16[2,512,128]{2,1,0:T(8,128)(2,1)S(1)}, bf16[2,512,128]{2,1,0:T(8,128)(2,1)S(1)}, u32[]{:S(2)}, u32[]{:S(2)}) collective-permute-start(bf16[2,512,128]{2,1,0:T(8,128)(2,1)S(1)} %pad_maximum_fusion.own_ref), channel_id=1, source_target_pairs={{0,8},{8,0},{16,24},{24,16},{32,40},{40,32},{48,56},{56,48},{64,72... | collective-permute-start | bytes 786440 | tf_op jit(solution)/shard_map/ppermute | solution.py:287
  1.3 16.1 %collective-permute-start.3 = (bf16[2,512,128]{2,1,0:T(8,128)(2,1)S(1)}, bf16[2,512,128]{2,1,0:T(8,128)(2,1)S(1)}, u32[]{:S(2)}, u32[]{:S(2)}) collective-permute-start(bf16[2,512,128]{2,1,0:T(8,128)(2,1)S(1)} %pad_maximum_fusion.1.own_ref), channel_id=1, source_target_pairs={{0,8},{8,0},{16,24},{24,16},{32,40},{40,32},{48,56},{56,48},{64,72... | collective-permute-start | bytes 786440 | tf_op jit(solution)/shard_map/ppermute | solution.py:287
  1.9 15.5 %collective-permute-start.1 = (bf16[2,512,128]{2,1,0:T(8,128)(2,1)S(1)}, bf16[2,512,128]{2,1,0:T(8,128)(2,1)}, u32[]{:S(2)}, u32[]{:S(2)}) collective-permute-start(bf16[2,512,128]{2,1,0:T(8,128)(2,1)S(1)} %pad_maximum_fusion.own_ref), channel_id=1, source_target_pairs={{0,16},{8,24},{16,32},{24,40},{32,48},{40,56},{48,64},{56,72},{64,... | collective-permute-start | bytes 786440 | tf_op jit(solution)/shard_map/ppermute | solution.py:287
  5.7 12.3 %collective-permute-start.2 = (bf16[2,512,128]{2,1,0:T(8,128)(2,1)S(1)}, bf16[2,512,128]{2,1,0:T(8,128)(2,1)S(1)}, u32[]{:S(2)}, u32[]{:S(2)}) collective-permute-start(bf16[2,512,128]{2,1,0:T(8,128)(2,1)S(1)} %pad_maximum_fusion.1.own_ref), channel_id=1, source_target_pairs={{16,0},{24,8},{32,16},{40,24},{48,32},{56,40},{64,48},{72,56},{80,... | collective-permute-start | bytes 786440 | tf_op jit(solution)/shard_map/ppermute | solution.py:287
  12.4 2.2 %copy-start = (bf16[512,4096]{1,0:T(8,128)(2,1)S(1)}, bf16[512,4096]{1,0:T(8,128)(2,1)}, u32[]{:S(2)}) copy-start(bf16[512,4096]{1,0:T(8,128)(2,1)} %w_ref.5) | copy-start | bytes 12582916
  16.4 1.0 copy-start.3
  18.0 14.0 %collective-permute-start.6 = (bf16[2,512,128]{2,1,0:T(8,128)(2,1)}, bf16[2,512,128]{2,1,0:T(8,128)(2,1)}, u32[]{:S(2)}, u32[]{:S(2)}) collective-permute-start(bf16[2,512,128]{2,1,0:T(8,128)(2,1)} %collective-permute-done.1.near_ref.fold_near_ref), channel_id=1, source_target_pairs={{0,16},{8,24},{16,32},{24,40},{32,48},{40,56},{48,64},{56,72},{64,... | collective-permute-start | bytes 786440 | tf_op jit(solution)/shard_map/ppermute | solution.py:287
  19.9 28.8 %collective-permute-start.10 = (bf16[512,1024]{1,0:T(8,128)(2,1)}, bf16[512,1024]{1,0:T(8,128)(2,1)S(1)}, u32[]{:S(2)}, u32[]{:S(2)}) collective-permute-start(bf16[512,1024]{1,0:T(8,128)(2,1)} %get-tuple-element.31), channel_id=1, source_target_pairs={{0,2},{1,3},{2,4},{3,5},{4,6},{5,7},{6,0},{7,1},{8,14},{9,15},{10,... | collective-permute-start | bytes 3145736 | tf_op jit(solution)/shard_map/ppermute | solution.py:320
  21.5 10.5 %collective-permute-start.5 = (bf16[2,512,128]{2,1,0:T(8,128)(2,1)S(1)}, bf16[2,512,128]{2,1,0:T(8,128)(2,1)S(1)}, u32[]{:S(2)}, u32[]{:S(2)}) collective-permute-start(bf16[2,512,128]{2,1,0:T(8,128)(2,1)S(1)} %broadcast_select_fusion.near_ref), channel_id=1, source_target_pairs={{0,8},{8,0},{16,24},{24,16},{32,40},{40,32},{48,56},{56,48},{64,72... | collective-permute-start | bytes 786440 | tf_op jit(solution)/shard_map/ppermute | solution.py:287
  21.8 14.5 %collective-permute-start.8 = (bf16[2,512,128]{2,1,0:T(8,128)(2,1)S(1)}, bf16[2,512,128]{2,1,0:T(8,128)(2,1)}, u32[]{:S(2)}, u32[]{:S(2)}) collective-permute-start(bf16[2,512,128]{2,1,0:T(8,128)(2,1)S(1)} %broadcast_select_fusion.near_ref), channel_id=1, source_target_pairs={{16,0},{24,8},{32,16},{40,24},{48,32},{56,40},{64,48},{72,56},{80,... | collective-permute-start | bytes 786440 | tf_op jit(solution)/shard_map/ppermute | solution.py:287
  29.8 6.5 %collective-permute-start.4 = (bf16[2,512,128]{2,1,0:T(8,128)(2,1)}, bf16[2,512,128]{2,1,0:T(8,128)(2,1)}, u32[]{:S(2)}, u32[]{:S(2)}) collective-permute-start(bf16[2,512,128]{2,1,0:T(8,128)(2,1)} %collective-permute-done.1.near_ref.fold_near_ref), channel_id=1, source_target_pairs={{0,8},{8,0},{16,24},{24,16},{32,40},{40,32},{48,56},{56,48},{64,72... | collective-permute-start | bytes 786440 | tf_op jit(solution)/shard_map/ppermute | solution.py:287
  32.0 4.7 %collective-permute-start.7 = (bf16[2,512,128]{2,1,0:T(8,128)(2,1)}, bf16[2,512,128]{2,1,0:T(8,128)(2,1)}, u32[]{:S(2)}, u32[]{:S(2)}) collective-permute-start(bf16[2,512,128]{2,1,0:T(8,128)(2,1)} %collective-permute-done.6.far_ref), channel_id=1, source_target_pairs={{0,8},{8,0},{16,24},{24,16},{32,40},{40,32},{48,56},{56,48},{64,72... | collective-permute-start | bytes 786440 | tf_op jit(solution)/shard_map/ppermute | solution.py:287
  32.0 0.7 copy-start.4
  32.7 16.0 %collective-permute-start.11 = (bf16[256,1024]{1,0:T(8,128)(2,1)}, bf16[256,1024]{1,0:T(8,128)(2,1)S(1)}, u32[]{:S(2)}, u32[]{:S(2)}) collective-permute-start(bf16[256,1024]{1,0:T(8,128)(2,1)} %get-tuple-element.33), channel_id=1, source_target_pairs={{0,4},{1,5},{2,6},{3,7},{4,0},{5,1},{6,2},{7,3},{8,12},{9,13},{10,... | collective-permute-start | bytes 1572872 | tf_op jit(solution)/shard_map/ppermute | solution.py:292
  36.3 26.6 %collective-permute-start.16 = (bf16[1024,512]{1,0:T(8,128)(2,1)}, bf16[1024,512]{1,0:T(8,128)(2,1)S(1)}, u32[]{:S(2)}, u32[]{:S(2)}) collective-permute-start(bf16[1024,512]{1,0:T(8,128)(2,1)} %copy-done.3), channel_id=1, source_target_pairs={{0,1},{1,0},{2,3},{3,2},{4,5},{5,4},{6,7},{7,6},{8,9},{9,8},{10,11... | collective-permute-start | bytes 3145736 | tf_op jit(solution)/shard_map/ppermute | solution.py:292
  36.3 10.7 %collective-permute-start.9 = (bf16[2,512,128]{2,1,0:T(8,128)(2,1)}, bf16[2,512,128]{2,1,0:T(8,128)(2,1)S(1)}, u32[]{:S(2)}, u32[]{:S(2)}) collective-permute-start(bf16[2,512,128]{2,1,0:T(8,128)(2,1)} %collective-permute-done.8.far_ref), channel_id=1, source_target_pairs={{0,8},{8,0},{16,24},{24,16},{32,40},{40,32},{48,56},{56,48},{64,72... | collective-permute-start | bytes 786440 | tf_op jit(solution)/shard_map/ppermute | solution.py:287
  36.6 1.2 %copy-start.2 = (bf16[2,512,512]{2,1,0:T(8,128)(2,1)S(1)}, bf16[2,512,512]{2,1,0:T(8,128)(2,1)}, u32[]{:S(2)}) copy-start(bf16[2,512,512]{2,1,0:T(8,128)(2,1)} %q_ref.3) | copy-start | bytes 3145732
  37.9 16.0 %copy-start.5 = (bf16[2,512,128]{2,1,0:T(8,128)(2,1)S(1)}, bf16[2,512,128]{2,1,0:T(8,128)(2,1)}, u32[]{:S(2)}) copy-start(bf16[2,512,128]{2,1,0:T(8,128)(2,1)} %copy-done.4) | copy-start | bytes 786436
  47.1 28.2 %copy-start.1 = (bf16[512,4096]{1,0:T(8,128)(2,1)S(1)}, bf16[512,4096]{1,0:T(8,128)(2,1)}, u32[]{:S(2)}) copy-start(bf16[512,4096]{1,0:T(8,128)(2,1)} %w_ref.5) | copy-start | bytes 12582916
  48.7 16.4 %collective-permute-start.14 = (bf16[512,512]{1,0:T(8,128)(2,1)S(1)}, bf16[512,512]{1,0:T(8,128)(2,1)S(1)}, u32[]{:S(2)}, u32[]{:S(2)}) collective-permute-start(bf16[512,512]{1,0:T(8,128)(2,1)S(1)} %attend0.1.own_ref), channel_id=1, source_target_pairs={{0,4},{1,5},{2,6},{3,7},{4,0},{5,1},{6,2},{7,3},{8,12},{9,13},{10,... | collective-permute-start | bytes 1572872 | tf_op jit(solution)/shard_map/ppermute | solution.py:292
  51.8 23.4 %collective-permute-start.13 = (bf16[512,512]{1,0:T(8,128)(2,1)S(1)}, bf16[512,512]{1,0:T(8,128)(2,1)S(1)}, u32[]{:S(2)}, u32[]{:S(2)}) collective-permute-start(bf16[512,512]{1,0:T(8,128)(2,1)S(1)} %attend0.1.own_ref), channel_id=1, source_target_pairs={{0,6},{1,7},{2,0},{3,1},{4,2},{5,3},{6,4},{7,5},{8,14},{9,15},{10,... | collective-permute-start | bytes 1572872 | tf_op jit(solution)/shard_map/ppermute | solution.py:292
  53.0 22.2 %collective-permute-start.12 = (bf16[512,512]{1,0:T(8,128)(2,1)S(1)}, bf16[512,512]{1,0:T(8,128)(2,1)S(1)}, u32[]{:S(2)}, u32[]{:S(2)}) collective-permute-start(bf16[512,512]{1,0:T(8,128)(2,1)S(1)} %attend0.1.own_ref), channel_id=1, source_target_pairs={{0,2},{1,3},{2,4},{3,5},{4,6},{5,7},{6,0},{7,1},{8,10},{9,11},{10,... | collective-permute-start | bytes 1572872 | tf_op jit(solution)/shard_map/ppermute | solution.py:292
  62.9 14.4 %collective-permute-start.17 = (bf16[1024,512]{1,0:T(8,128)(2,1)S(1)}, bf16[1024,512]{1,0:T(8,128)(2,1)S(1)}, u32[]{:S(2)}, u32[]{:S(2)}) collective-permute-start(bf16[1024,512]{1,0:T(8,128)(2,1)S(1)} %collective-permute-done.16.wm_ref), channel_id=1, source_target_pairs={{0,8},{8,0},{16,24},{24,16},{32,40},{40,32},{48,56},{56,48},{64,72... | collective-permute-start | bytes 3145736 | tf_op jit(solution)/shard_map/ppermute | solution.py:287
  63.0 14.3 %collective-permute-start.15 = (bf16[512,512]{1,0:T(8,128)(2,1)S(1)}, bf16[512,512]{1,0:T(8,128)(2,1)S(1)}, u32[]{:S(2)}, u32[]{:S(2)}) collective-permute-start(bf16[512,512]{1,0:T(8,128)(2,1)S(1)} %attend1.1.own_ref), channel_id=1, source_target_pairs={{0,1},{1,0},{2,3},{3,2},{4,5},{5,4},{6,7},{7,6},{8,9},{9,8},{10,11... | collective-permute-start | bytes 1572872 | tf_op jit(solution)/shard_map/ppermute | solution.py:292
  79.1 5.3 %collective-permute-start.18 = (bf16[512,1024]{1,0:T(8,128)(2,1)S(1)}, bf16[512,1024]{1,0:T(8,128)(2,1)S(1)}, u32[]{:S(2)}, u32[]{:S(2)}) collective-permute-start(bf16[512,1024]{1,0:T(8,128)(2,1)S(1)} %collective-permute-done.10.ws_ref), channel_id=1, source_target_pairs={{0,8},{8,0},{16,24},{24,16},{32,40},{40,32},{48,56},{56,48},{64,72... | collective-permute-start | bytes 3145736 | tf_op jit(solution)/shard_map/ppermute | solution.py:287
  79.2 5.2 %collective-permute-start.19 = (bf16[256,1024]{1,0:T(8,128)(2,1)S(1)}, bf16[256,1024]{1,0:T(8,128)(2,1)S(1)}, u32[]{:S(2)}, u32[]{:S(2)}) collective-permute-start(bf16[256,1024]{1,0:T(8,128)(2,1)S(1)} %collective-permute-done.11.wf_ref), channel_id=1, source_target_pairs={{0,8},{8,0},{16,24},{24,16},{32,40},{40,32},{48,56},{56,48},{64,72... | collective-permute-start | bytes 1572872 | tf_op jit(solution)/shard_map/ppermute | solution.py:287
  79.7 15.4 %collective-permute-start.22 = (bf16[512,512]{1,0:T(8,128)(2,1)S(1)}, bf16[512,512]{1,0:T(8,128)(2,1)S(1)}, u32[]{:S(2)}, u32[]{:S(2)}) collective-permute-start(bf16[512,512]{1,0:T(8,128)(2,1)S(1)} %get-tuple-element.45), channel_id=1, source_target_pairs={{0,2},{1,3},{2,4},{3,5},{4,6},{5,7},{6,0},{7,1},{8,10},{9,11},{10,... | collective-permute-start | bytes 1572872 | tf_op jit(solution)/shard_map/ppermute | solution.py:292
  80.9 24.5 %collective-permute-start.23 = (bf16[512,512]{1,0:T(8,128)(2,1)S(1)}, bf16[512,512]{1,0:T(8,128)(2,1)S(1)}, u32[]{:S(2)}, u32[]{:S(2)}) collective-permute-start(bf16[512,512]{1,0:T(8,128)(2,1)S(1)} %get-tuple-element.46), channel_id=1, source_target_pairs={{0,6},{1,7},{2,0},{3,1},{4,2},{5,3},{6,4},{7,5},{8,14},{9,15},{10,... | collective-permute-start | bytes 1572872 | tf_op jit(solution)/shard_map/ppermute | solution.py:292
  83.0 23.7 %collective-permute-start.21 = (bf16[512,512]{1,0:T(8,128)(2,1)S(1)}, bf16[512,512]{1,0:T(8,128)(2,1)S(1)}, u32[]{:S(2)}, u32[]{:S(2)}) collective-permute-start(bf16[512,512]{1,0:T(8,128)(2,1)S(1)} %get-tuple-element.39), channel_id=1, source_target_pairs={{0,4},{1,5},{2,6},{3,7},{4,0},{5,1},{6,2},{7,3},{8,12},{9,13},{10,... | collective-permute-start | bytes 1572872 | tf_op jit(solution)/shard_map/ppermute | solution.py:292
  87.3 20.2 %collective-permute-start.20 = (bf16[512,512]{1,0:T(8,128)(2,1)S(1)}, bf16[512,512]{1,0:T(8,128)(2,1)S(1)}, u32[]{:S(2)}, u32[]{:S(2)}) collective-permute-start(bf16[512,512]{1,0:T(8,128)(2,1)S(1)} %get-tuple-element.43), channel_id=1, source_target_pairs={{0,1},{1,0},{2,3},{3,2},{4,5},{5,4},{6,7},{7,6},{8,9},{9,8},{10,11... | collective-permute-start | bytes 1572872 | tf_op jit(solution)/shard_map/ppermute | solution.py:292

commit v4 on v3

--- a/solution.py
+++ b/solution.py
@@ -40,8 +40,7 @@
     def fill(lag, ref):
         rows = pl.ds(lag * blk, blk)
         k = ref[0]
-        kk[rows, :HD] = k
-        kk[rows, HD:] = k
+        kk[rows, :] = k
         vv[rows, :HD] = ref[1]
         vv[rows, HD:] = jnp.ones((blk, HD), BF16)
 
@@ -68,65 +67,90 @@
     factor = HD ** -0.5 * math.log2(math.e)
     tiles = blk // TILE
     far = LAGS * blk
-    for t in range(tiles):
+    col = lax.broadcasted_iota(jnp.int32, (TILE, blk), 1)
+    row_t = lax.broadcasted_iota(jnp.int32, (TILE, TILE), 0)
+    col_t = lax.broadcasted_iota(jnp.int32, (TILE, TILE), 1)
+    tri = col_t <= row_t
+
+    def unit(t, a, sb):
         r0 = t * TILE
+        cols = slice(a * HD, (a + 1) * HD)
         rel = doc_ref[r0:r0 + TILE, :] - base
-        col = lax.broadcasted_iota(jnp.int32, (TILE, blk), 1)
-        row_t = lax.broadcasted_iota(jnp.int32, (TILE, TILE), 0)
-        col_t = lax.broadcasted_iota(jnp.int32, (TILE, TILE), 1)
-        tri = col_t <= row_t
-        for a in range(heads):
-            sb = sbuf.at[(t * heads + a) % 2]
-            qf = q_ref[half, r0:r0 + TILE, a * HD:(a + 1) * HD].astype(F32) * factor
-            hi = qf.astype(BF16)
-            lo = (qf - hi.astype(F32)).astype(BF16)
-            qq = jnp.concatenate([hi, lo], axis=1)
-
-            def scores(first, count):
-                return mm(qq, kk[first:first + count, :], NT)
-
-            def running(m, s):
-                for x in range(s.shape[1] // HD):
-                    p = s[:, x * HD:(x + 1) * HD]
-                    m = p if m is None else jnp.maximum(m, p)
-                return m
-
-            m = None
-            pieces = []
-            off = 0
-            for lag in (3, 2, 1):
-                s = jnp.where(col - lag * blk >= rel, scores(lag * blk, blk), NEG)
-                m = running(m, s)
-                sb[:, off:off + blk] = s
-                pieces.append((off, blk, lag * blk))
-                off += blk
-            for u in range(tiles):
-                if u == t:
-                    continue
-                lag = 0 if u < t else LAGS
-                first = lag * blk + u * TILE
-                s = jnp.where(col_t + (u * TILE - lag * blk) >= rel, scores(first, TILE), NEG)
-                m = running(m, s)
-                sb[:, off:off + TILE] = s
-                pieces.append((off, TILE, first))
-                off += TILE
+        q = q_ref[half, r0:r0 + TILE, cols]
+        state = {"m": None, "acc": jnp.zeros((TILE, 2 * HD), F32)}
+
+        def scores(first, count):
+            return mm(q, kk[first:first + count, :], NT) * factor
+
+        def keep(s, off):
+            for x in range(s.shape[1] // HD):
+                p = s[:, x * HD:(x + 1) * HD]
+                state["m"] = p if state["m"] is None else jnp.maximum(state["m"], p)
+            sb[:, off:off + s.shape[1]] = s
+
+        def whole(lag, off):
+            keep(jnp.where(col - lag * blk >= rel, scores(lag * blk, blk), NEG), off)
+
+        def part(lag, u, off):
+            s = scores(lag * blk + u * TILE, TILE)
+            keep(jnp.where(col_t + (u * TILE - lag * blk) >= rel, s, NEG), off)
+
+        def corner(off):
             s = jnp.where(tri, scores(r0, TILE), scores(far + r0, TILE))
             position = jnp.where(tri, col_t + r0, col_t + (r0 - far))
-            s = jnp.where(position >= rel, s, NEG)
-            m = running(m, s)
-            sb[:, off:off + TILE] = s
-            top = jnp.max(m, axis=1, keepdims=True)
-            acc = jnp.zeros((TILE, 2 * HD), F32)
-            for begin, count, first in pieces:
-                p = jnp.exp2(sb[:, begin:begin + count] - top).astype(BF16)
-                acc = acc + mm(p, vv[first:first + count, :])
-            p = jnp.exp2(sb[:, off:off + TILE] - top).astype(BF16)
+            keep(jnp.where(position >= rel, s, NEG), off)
+
+        def mix(begin, count, first):
+            p = jnp.exp2(sb[:, begin:begin + count] - state["top"]).astype(BF16)
+            state["acc"] = state["acc"] + mm(p, vv[first:first + count, :])
+
+        def mix_corner(off):
+            p = jnp.exp2(sb[:, off:off + TILE] - state["top"]).astype(BF16)
             zero = jnp.zeros_like(p)
-            acc = acc + mm(jnp.where(tri, p, zero), vv[r0:r0 + TILE, :])
-            acc = acc + mm(jnp.where(tri, zero, p), vv[far + r0:far + r0 + TILE, :])
+            acc = state["acc"] + mm(jnp.where(tri, p, zero), vv[r0:r0 + TILE, :])
+            state["acc"] = acc + mm(jnp.where(tri, zero, p), vv[far + r0:far + r0 + TILE, :])
+
+        def highest():
+            state["top"] = jnp.max(state["m"], axis=1, keepdims=True)
+
+        def store():
+            acc = state["acc"]
             result = (acc[:, :HD] / acc[:, HD:]).astype(BF16)
             count = out_refs[0].shape[0]
-            out_refs[r0 // count][r0 % count:r0 % count + TILE, a * HD:(a + 1) * HD] = result
+            out_refs[r0 // count][r0 % count:r0 % count + TILE, cols] = result
+
+        first_pass, second_pass = [], []
+        off = 0
+        for lag in (3, 2, 1):
+            first_pass.append(functools.partial(whole, lag, off))
+            second_pass.append(functools.partial(mix, off, blk, lag * blk))
+            off += blk
+        for u in range(tiles):
+            if u != t:
+                lag = 0 if u < t else LAGS
+                first_pass.append(functools.partial(part, lag, u, off))
+                second_pass.append(functools.partial(mix, off, TILE, lag * blk + u * TILE))
+                off += TILE
+        first_pass.append(functools.partial(corner, off))
+        second_pass.append(functools.partial(mix_corner, off))
+        return first_pass, highest, second_pass, store
+
+    units = [
+        unit(t, a, sbuf.at[(t * heads + a) % 2]) for t in range(tiles) for a in range(heads)
+    ]
+    for step in units[0][0]:
+        step()
+    units[0][1]()
+    for i, (_, _, second_pass, store) in enumerate(units):
+        following = units[i + 1][0] if i + 1 < len(units) else []
+        for j in range(max(len(following), len(second_pass))):
+            if j < len(following):
+                following[j]()
+            if j < len(second_pass):
+                second_pass[j]()
+        store()
+        if following:
+            units[i + 1][1]()
 
 
 def attention(half, outs, info, q, doc, *blocks):
@@ -138,7 +162,7 @@
         in_specs=[SMEM] + [VMEM] * (2 + len(blocks)),
         out_specs=[VMEM] * outs,
         scratch_shapes=[
-            pltpu.VMEM((keys, 2 * HD), BF16),
+            pltpu.VMEM((keys, HD), BF16),
             pltpu.VMEM((keys, 2 * HD), BF16),
             pltpu.VMEM((2, TILE, LAGS * rows), F32),
         ],

time: 110 us -> 110 us (level)
  Pallas kernels: 29 us -> 27.8 us
    pallas_call x2, Pallas kernels: 18.2 us -> 16.9 us  [attention(): pl.pallas_call(functools.partial(attn_kernel, half), out_shape=[jax.Shape...]
  transfers between devices with their start and end apart: 24 -> 24, of which waited for: 9 -> 8; matrix products, arithmetic and copies ran while one was open for 1% -> 1% of each run, Pallas kernels for 23% -> 22%
where the time goes in v4:
time: 110 us; the launch traced here: 109 us
  starting transfers between devices  37.3 us (34%)
  waiting for transfers between devices  37 us (34%)
  Pallas kernels  27.8 us (25%)
  local copies, waits for them, and re-layouts  6.55 us (6%)
    ppermute x10, waiting for transfers between devices, head_move(): return lax.ppermute(array, 'head', [(i, to(i)) for i in range(2 * ring)])  34.4 us
    ppermute x13, starting transfers between devices, ctx_move(): lax.ppermute(array, 'ctx', [(i, to(i)) for i in range(ctx_size) if 0 <= t...  22.3 us
    pallas_call x2, Pallas kernels, attention(): pl.pallas_call(functools.partial(attn_kernel, half), out_shape=[jax.Shape...  16.9 us
    ppermute x10, starting transfers between devices, head_move(): return lax.ppermute(array, 'head', [(i, to(i)) for i in range(2 * ring)])  13.4 us
    pallas_call x5, Pallas kernels, project(): pl.pallas_call(kernel, out_shape=outs, in_specs=[SMEM] + [VMEM] * (len(ar...  8.99 us
    unnamed x14, local copies, waits for them, and re-layouts  5.11 us
    ppermute x13, waiting for transfers between devices, ctx_move(): lax.ppermute(array, 'ctx', [(i, to(i)) for i in range(ctx_size) if 0 <= t...  2.65 us
  transfers between devices with their start and end apart: 24, of which 8 were waited for; matrix products, arithmetic and copies ran while one was open for 1% of the time, Pallas kernels for 22%

profile of v4, /device:TPU:24, one launch (start us, length us, event | category | flops | bytes accessed | tf_op | source)
XLA Modules:
  0.0 109.2 jit_solution(5366095931934768658)
XLA Ops:
  0.0 1.1 %fusion = (bf16[1,512,128]{2,1,0:T(8,128)(2,1)S(1)}, bf16[1,512,128]{2,1,0:T(8,128)(2,1)S(1)}, bf16[1,512,128]{2,1,0:T(8,128)(2,1)S(1)}, bf16[1,512,128]{2,1,0:T(8,128)(2,1)S(1)}) fusion(bf16[2,512,128]{2,1,0:T(8,128)(2,1)} %param.6, bf16[2,512,128]{2,1,0:T(8,128)(2,1)} %param.7), kind=kLoop, calls=%fused_computation.8 | loop fusion | bytes 1048576 | tf_op jit(solution)/shard_map/slice | solution.py:334
  1.2 0.1 collective-permute-start
  1.3 0.6 collective-permute-start.3
  1.9 3.8 %collective-permute-start.1 = (bf16[2,512,128]{2,1,0:T(8,128)(2,1)S(1)}, bf16[2,512,128]{2,1,0:T(8,128)(2,1)}, u32[]{:S(2)}, u32[]{:S(2)}) collective-permute-start(bf16[2,512,128]{2,1,0:T(8,128)(2,1)S(1)} %pad_maximum_fusion.own_ref), channel_id=1, source_target_pairs={{0,16},{8,24},{16,32},{24,40},{32,48},{40,56},{48,64},{56,72},{64,... | collective-permute-start | bytes 786440 | tf_op jit(solution)/shard_map/ppermute | solution.py:311
  5.7 6.5 %collective-permute-start.2 = (bf16[2,512,128]{2,1,0:T(8,128)(2,1)S(1)}, bf16[2,512,128]{2,1,0:T(8,128)(2,1)S(1)}, u32[]{:S(2)}, u32[]{:S(2)}) collective-permute-start(bf16[2,512,128]{2,1,0:T(8,128)(2,1)S(1)} %pad_maximum_fusion.1.own_ref), channel_id=1, source_target_pairs={{16,0},{24,8},{32,16},{40,24},{48,32},{56,40},{64,48},{72,56},{80,... | collective-permute-start | bytes 786440 | tf_op jit(solution)/shard_map/ppermute | solution.py:311
  12.3 0.1 pad_add_fusion.info_ref
  12.4 2.2 %copy-done = bf16[512,4096]{1,0:T(8,128)(2,1)S(1)} copy-done((bf16[512,4096]{1,0:T(8,128)(2,1)S(1)}, bf16[512,4096]{1,0:T(8,128)(2,1)}, u32[]{:S(2)}) %copy-start) | copy-done | bytes 4194328
  14.6 1.9 %split_weights.1 = (bf16[512,1024]{1,0:T(8,128)(2,1)}, bf16[256,1024]{1,0:T(8,128)(2,1)}, bf16[1024,512]{1,0:T(8,128)(2,1)S(1)}) custom-call(s32[3]{0:T(128)S(1)} %pad_add_fusion.info_ref, bf16[512,4096]{1,0:T(8,128)(2,1)S(1)} %copy-done), custom_call_target="tpu_custom_call" | custom-call | flops 1 | bytes 1 | tf_op jit(solution)/shard_map/split_weights/pallas_call | solution.py:196
  16.4 1.0 copy-done.3
  17.4 0.0 collective-permute-done.traded_ref
  17.4 0.0 collective-permute-done.3.traded_ref
  17.4 0.0 collective-permute-done.1.near_ref.fold_near_ref
  17.4 0.6 collective-permute-done.2
  18.0 1.9 %collective-permute-start.6 = (bf16[2,512,128]{2,1,0:T(8,128)(2,1)}, bf16[2,512,128]{2,1,0:T(8,128)(2,1)}, u32[]{:S(2)}, u32[]{:S(2)}) collective-permute-start(bf16[2,512,128]{2,1,0:T(8,128)(2,1)} %collective-permute-done.1.near_ref.fold_near_ref), channel_id=1, source_target_pairs={{0,16},{8,24},{16,32},{24,40},{32,48},{40,56},{48,64},{56,72},{64,... | collective-permute-start | bytes 786440 | tf_op jit(solution)/shard_map/ppermute | solution.py:311
  19.9 1.6 %collective-permute-start.10 = (bf16[512,1024]{1,0:T(8,128)(2,1)}, bf16[512,1024]{1,0:T(8,128)(2,1)S(1)}, u32[]{:S(2)}, u32[]{:S(2)}) collective-permute-start(bf16[512,1024]{1,0:T(8,128)(2,1)} %get-tuple-element.31), channel_id=1, source_target_pairs={{0,2},{1,3},{2,4},{3,5},{4,6},{5,7},{6,0},{7,1},{8,14},{9,15},{10,... | collective-permute-start | bytes 3145736 | tf_op jit(solution)/shard_map/ppermute | solution.py:344
  21.5 0.3 collective-permute-start.5
  21.8 8.0 %collective-permute-start.8 = (bf16[2,512,128]{2,1,0:T(8,128)(2,1)S(1)}, bf16[2,512,128]{2,1,0:T(8,128)(2,1)}, u32[]{:S(2)}, u32[]{:S(2)}) collective-permute-start(bf16[2,512,128]{2,1,0:T(8,128)(2,1)S(1)} %broadcast_select_fusion.near_ref), channel_id=1, source_target_pairs={{16,0},{24,8},{32,16},{40,24},{48,32},{56,40},{64,48},{72,56},{80,... | collective-permute-start | bytes 786440 | tf_op jit(solution)/shard_map/ppermute | solution.py:311
  29.8 0.2 collective-permute-start.4
  29.9 2.0 %collective-permute-done.6.far_ref = bf16[2,512,128]{2,1,0:T(8,128)(2,1)} collective-permute-done((bf16[2,512,128]{2,1,0:T(8,128)(2,1)}, bf16[2,512,128]{2,1,0:T(8,128)(2,1)}, u32[]{:S(2)}, u32[]{:S(2)}) %collective-permute-start.6) | collective-permute-done | bytes 262176 | tf_op jit(solution)/shard_map/ppermute | solution.py:311
  32.0 0.0 collective-permute-start.7
  32.0 0.0 collective-permute-done.5.near_traded_ref
  32.0 0.7 copy-done.4
  32.7 3.1 %collective-permute-start.11 = (bf16[256,1024]{1,0:T(8,128)(2,1)}, bf16[256,1024]{1,0:T(8,128)(2,1)S(1)}, u32[]{:S(2)}, u32[]{:S(2)}) collective-permute-start(bf16[256,1024]{1,0:T(8,128)(2,1)} %get-tuple-element.33), channel_id=1, source_target_pairs={{0,4},{1,5},{2,6},{3,7},{4,0},{5,1},{6,2},{7,3},{8,12},{9,13},{10,... | collective-permute-start | bytes 1572872 | tf_op jit(solution)/shard_map/ppermute | solution.py:316
  35.8 0.1 add_add_fusion.info_ref
  35.9 0.1 copy.7.doc_ref
  36.0 0.1 copy.6.doc_ref
  36.2 0.1 add_add_fusion.1.info_ref
  36.3 0.0 collective-permute-done.4.near_traded_ref.fold_traded_ref
  36.3 0.0 collective-permute-start.16
  36.3 0.0 collective-permute-done.8.far_ref
  36.3 0.3 collective-permute-start.9
  36.6 0.0 collective-permute-done.7.far_traded_ref
  36.6 1.2 %copy-done.2 = bf16[2,512,512]{2,1,0:T(8,128)(2,1)S(1)} copy-done((bf16[2,512,512]{2,1,0:T(8,128)(2,1)S(1)}, bf16[2,512,512]{2,1,0:T(8,128)(2,1)}, u32[]{:S(2)}) %copy-start.2) | copy-done | bytes 1048600
  37.9 8.6 %attend0.1.own_ref = bf16[512,512]{1,0:T(8,128)(2,1)S(1)} custom-call(s32[3]{0:T(128)S(1)} %add_add_fusion.info_ref, bf16[2,512,512]{2,1,0:T(8,128)(2,1)S(1)} %copy-done.2, s32[512,1]{1,0:T(8,128)S(1)} %copy.6.doc_ref, bf16[2,512,128]{2,1,0:T(8,128)(2,1)S(1)} %pad_maximum_fusion.own_ref, bf16[2,512,128]{2,1,0:T(8,128)(2,1)S(1)} %collective-permute-done.traded_ref, ...), custom_call_target="tpu_custom_call" | custom-call | flops 4000000000 | bytes 1 | tf_op jit(solution)/shard_map/attend0/pallas_call | solution.py:159
  46.4 0.0 copy-start.1
  46.4 0.0 collective-permute-done.9.far_traded_ref
  46.5 2.3 %collective-permute-done.11.wf_ref = bf16[256,1024]{1,0:T(8,128)(2,1)S(1)} collective-permute-done((bf16[256,1024]{1,0:T(8,128)(2,1)}, bf16[256,1024]{1,0:T(8,128)(2,1)S(1)}, u32[]{:S(2)}, u32[]{:S(2)}) %collective-permute-start.11) | collective-permute-done | bytes 524320 | tf_op jit(solution)/shard_map/ppermute | solution.py:316
  48.7 0.0 collective-permute-done.10.ws_ref
  48.7 3.1 %collective-permute-start.14 = (bf16[512,512]{1,0:T(8,128)(2,1)S(1)}, bf16[512,512]{1,0:T(8,128)(2,1)S(1)}, u32[]{:S(2)}, u32[]{:S(2)}) collective-permute-start(bf16[512,512]{1,0:T(8,128)(2,1)S(1)} %attend0.1.own_ref), channel_id=1, source_target_pairs={{0,4},{1,5},{2,6},{3,7},{4,0},{5,1},{6,2},{7,3},{8,12},{9,13},{10,... | collective-permute-start | bytes 1572872 | tf_op jit(solution)/shard_map/ppermute | solution.py:316
  51.8 1.1 %collective-permute-start.13 = (bf16[512,512]{1,0:T(8,128)(2,1)S(1)}, bf16[512,512]{1,0:T(8,128)(2,1)S(1)}, u32[]{:S(2)}, u32[]{:S(2)}) collective-permute-start(bf16[512,512]{1,0:T(8,128)(2,1)S(1)} %attend0.1.own_ref), channel_id=1, source_target_pairs={{0,6},{1,7},{2,0},{3,1},{4,2},{5,3},{6,4},{7,5},{8,14},{9,15},{10,... | collective-permute-start | bytes 1572872 | tf_op jit(solution)/shard_map/ppermute | solution.py:316
  53.0 0.9 collective-permute-start.12
  53.9 8.3 %attend1.1.own_ref = bf16[512,512]{1,0:T(8,128)(2,1)S(1)} custom-call(s32[3]{0:T(128)S(1)} %add_add_fusion.1.info_ref, bf16[2,512,512]{2,1,0:T(8,128)(2,1)S(1)} %copy-done.2, s32[512,1]{1,0:T(8,128)S(1)} %copy.7.doc_ref, bf16[2,512,128]{2,1,0:T(8,128)(2,1)S(1)} %pad_maximum_fusion.1.own_ref, bf16[2,512,128]{2,1,0:T(8,128)(2,1)S(1)} %collective-permute-done.3.traded_ref, ...), custom_call_target="tpu_custom_call" | custom-call | flops 10737418240 | bytes 4194304 | tf_op jit(solution)/shard_map/attend1/pallas_call | solution.py:159
  62.2 0.1 collective-permute-start.17
  62.3 0.1 collective-permute-start.15
  62.4 2.7 %collective-permute-done.14.far_ref = bf16[512,512]{1,0:T(8,128)(2,1)S(1)} collective-permute-done((bf16[512,512]{1,0:T(8,128)(2,1)S(1)}, bf16[512,512]{1,0:T(8,128)(2,1)S(1)}, u32[]{:S(2)}, u32[]{:S(2)}) %collective-permute-start.14) | collective-permute-done | bytes 524320 | tf_op jit(solution)/shard_map/ppermute | solution.py:316
  65.1 10.1 %collective-permute-done.13.right_ref = bf16[512,512]{1,0:T(8,128)(2,1)S(1)} collective-permute-done((bf16[512,512]{1,0:T(8,128)(2,1)S(1)}, bf16[512,512]{1,0:T(8,128)(2,1)S(1)}, u32[]{:S(2)}, u32[]{:S(2)}) %collective-permute-start.13) | collective-permute-done | bytes 524320 | tf_op jit(solution)/shard_map/ppermute | solution.py:316
  75.2 0.0 collective-permute-done.12.left_ref
  75.2 1.8 %own_part.1.part_ref = f32[4,512,512]{2,1,0:T(8,128)S(1)} custom-call(s32[3]{0:T(128)S(1)} %pad_add_fusion.info_ref, bf16[512,512]{1,0:T(8,128)(2,1)S(1)} %attend1.1.own_ref, bf16[512,4096]{1,0:T(8,128)(2,1)S(1)} %copy-done.1), custom_call_target="tpu_custom_call" | custom-call | flops 8000000000 | bytes 1 | tf_op jit(solution)/shard_map/own_part/pallas_call | solution.py:285
  77.1 0.0 collective-permute-done.17.wp_ref
  77.1 1.8 %reduce_first.1 = (bf16[512,512]{1,0:T(8,128)(2,1)S(1)}, bf16[512,512]{1,0:T(8,128)(2,1)S(1)}, bf16[512,512]{1,0:T(8,128)(2,1)S(1)}, bf16[512,512]{1,0:T(8,128)(2,1)S(1)}) custom-call(s32[3]{0:T(128)S(1)} %pad_add_fusion.info_ref, bf16[512,512]{1,0:T(8,128)(2,1)S(1)} %collective-permute-done.15.peer_ref, f32[4,512,512]{2,1,0:T(8,128)S(1)} %own_part.1.part_ref, ...), custom_call_target="tpu_custom_call" | custom-call | bytes 1 | tf_op jit(solution)/shard_map/reduce_first/pallas_call | solution.py:285
  78.9 0.1 collective-permute-start.18
  79.0 0.5 collective-permute-start.19
  79.5 1.4 %collective-permute-start.22 = (bf16[512,512]{1,0:T(8,128)(2,1)S(1)}, bf16[512,512]{1,0:T(8,128)(2,1)S(1)}, u32[]{:S(2)}, u32[]{:S(2)}) collective-permute-start(bf16[512,512]{1,0:T(8,128)(2,1)S(1)} %get-tuple-element.45), channel_id=1, source_target_pairs={{0,2},{1,3},{2,4},{3,5},{4,6},{5,7},{6,0},{7,1},{8,10},{9,11},{10,... | collective-permute-start | bytes 1572872 | tf_op jit(solution)/shard_map/ppermute | solution.py:316
  80.9 1.8 %collective-permute-start.23 = (bf16[512,512]{1,0:T(8,128)(2,1)S(1)}, bf16[512,512]{1,0:T(8,128)(2,1)S(1)}, u32[]{:S(2)}, u32[]{:S(2)}) collective-permute-start(bf16[512,512]{1,0:T(8,128)(2,1)S(1)} %get-tuple-element.46), channel_id=1, source_target_pairs={{0,6},{1,7},{2,0},{3,1},{4,2},{5,3},{6,4},{7,5},{8,14},{9,15},{10,... | collective-permute-start | bytes 1572872 | tf_op jit(solution)/shard_map/ppermute | solution.py:316
  82.7 1.7 %collective-permute-start.21 = (bf16[512,512]{1,0:T(8,128)(2,1)S(1)}, bf16[512,512]{1,0:T(8,128)(2,1)S(1)}, u32[]{:S(2)}, u32[]{:S(2)}) collective-permute-start(bf16[512,512]{1,0:T(8,128)(2,1)S(1)} %get-tuple-element.39), channel_id=1, source_target_pairs={{0,4},{1,5},{2,6},{3,7},{4,0},{5,1},{6,2},{7,3},{8,12},{9,13},{10,... | collective-permute-start | bytes 1572872 | tf_op jit(solution)/shard_map/ppermute | solution.py:316
  84.4 0.0 collective-permute-done.18.wsp_ref
  84.4 2.9 %gather_first.1 = (bf16[512,512]{1,0:T(8,128)(2,1)S(1)}, bf16[512,512]{1,0:T(8,128)(2,1)S(1)}) custom-call(s32[3]{0:T(128)S(1)} %pad_add_fusion.info_ref, bf16[512,512]{1,0:T(8,128)(2,1)S(1)} %attend0.1.own_ref, bf16[512,512]{1,0:T(8,128)(2,1)S(1)} %collective-permute-done.12.left_ref, bf16[512,512]{1,0:T(8,128)(2,1)S(1)} %collective-permute-done.13.right_ref, ...), custom_call_target="tpu_custom_call" | custom-call | bytes 1 | tf_op jit(solution)/shard_map/gather_first/pallas_call | solution.py:285
  87.3 0.1 collective-permute-start.20
  87.4 7.2 %collective-permute-done.22.refs_1_ = bf16[512,512]{1,0:T(8,128)(2,1)S(1)} collective-permute-done((bf16[512,512]{1,0:T(8,128)(2,1)S(1)}, bf16[512,512]{1,0:T(8,128)(2,1)S(1)}, u32[]{:S(2)}, u32[]{:S(2)}) %collective-permute-start.22) | collective-permute-done | bytes 524320 | tf_op jit(solution)/shard_map/ppermute | solution.py:316
  94.6 10.5 %collective-permute-done.23.refs_2_ = bf16[512,512]{1,0:T(8,128)(2,1)S(1)} collective-permute-done((bf16[512,512]{1,0:T(8,128)(2,1)S(1)}, bf16[512,512]{1,0:T(8,128)(2,1)S(1)}, u32[]{:S(2)}, u32[]{:S(2)}) %collective-permute-start.23) | collective-permute-done | bytes 524320 | tf_op jit(solution)/shard_map/ppermute | solution.py:316
  105.2 1.6 %collective-permute-done.21.refs_0_ = bf16[512,512]{1,0:T(8,128)(2,1)S(1)} collective-permute-done((bf16[512,512]{1,0:T(8,128)(2,1)S(1)}, bf16[512,512]{1,0:T(8,128)(2,1)S(1)}, u32[]{:S(2)}, u32[]{:S(2)}) %collective-permute-start.21) | collective-permute-done | bytes 524320 | tf_op jit(solution)/shard_map/ppermute | solution.py:316
  106.7 0.8 total.1.done_ref
  107.5 0.0 collective-permute-done.20.got_ref
  107.5 1.7 %finish.1 = bf16[2,512,512]{2,1,0:T(8,128)(2,1)} custom-call(s32[3]{0:T(128)S(1)} %pad_add_fusion.info_ref, bf16[512,512]{1,0:T(8,128)(2,1)S(1)} %get-tuple-element.42.keep_ref, bf16[512,512]{1,0:T(8,128)(2,1)S(1)} %collective-permute-done.20.got_ref, bf16[512,512]{1,0:T(8,128)(2,1)S(1)} %total.1.done_ref), custom_call_target="tpu_custom_call" | custom-call | bytes 1 | tf_op jit(solution)/shard_map/finish/pallas_call | solution.py:285
  (16 shorter events, 0.1 us)
Async XLA Ops:
  0.0 32.0 %copy-start.6 = (s32[2,512]{1,0:T(2,128)S(1)}, s32[2,512]{1,0:T(2,128)}, u32[]{:S(2)}) copy-start(s32[2,512]{1,0:T(2,128)} %param.8) | copy-start | bytes 12292
  1.2 16.2 %collective-permute-start = (bf16[2,512,128]{2,1,0:T(8,128)(2,1)S(1)}, bf16[2,512,128]{2,1,0:T(8,128)(2,1)S(1)}, u32[]{:S(2)}, u32[]{:S(2)}) collective-permute-start(bf16[2,512,128]{2,1,0:T(8,128)(2,1)S(1)} %pad_maximum_fusion.own_ref), channel_id=1, source_target_pairs={{0,8},{8,0},{16,24},{24,16},{32,40},{40,32},{48,56},{56,48},{64,72... | collective-permute-start | bytes 786440 | tf_op jit(solution)/shard_map/ppermute | solution.py:311
  1.3 16.1 %collective-permute-start.3 = (bf16[2,512,128]{2,1,0:T(8,128)(2,1)S(1)}, bf16[2,512,128]{2,1,0:T(8,128)(2,1)S(1)}, u32[]{:S(2)}, u32[]{:S(2)}) collective-permute-start(bf16[2,512,128]{2,1,0:T(8,128)(2,1)S(1)} %pad_maximum_fusion.1.own_ref), channel_id=1, source_target_pairs={{0,8},{8,0},{16,24},{24,16},{32,40},{40,32},{48,56},{56,48},{64,72... | collective-permute-start | bytes 786440 | tf_op jit(solution)/shard_map/ppermute | solution.py:311
  1.9 15.5 %collective-permute-start.1 = (bf16[2,512,128]{2,1,0:T(8,128)(2,1)S(1)}, bf16[2,512,128]{2,1,0:T(8,128)(2,1)}, u32[]{:S(2)}, u32[]{:S(2)}) collective-permute-start(bf16[2,512,128]{2,1,0:T(8,128)(2,1)S(1)} %pad_maximum_fusion.own_ref), channel_id=1, source_target_pairs={{0,16},{8,24},{16,32},{24,40},{32,48},{40,56},{48,64},{56,72},{64,... | collective-permute-start | bytes 786440 | tf_op jit(solution)/shard_map/ppermute | solution.py:311
  5.7 12.3 %collective-permute-start.2 = (bf16[2,512,128]{2,1,0:T(8,128)(2,1)S(1)}, bf16[2,512,128]{2,1,0:T(8,128)(2,1)S(1)}, u32[]{:S(2)}, u32[]{:S(2)}) collective-permute-start(bf16[2,512,128]{2,1,0:T(8,128)(2,1)S(1)} %pad_maximum_fusion.1.own_ref), channel_id=1, source_target_pairs={{16,0},{24,8},{32,16},{40,24},{48,32},{56,40},{64,48},{72,56},{80,... | collective-permute-start | bytes 786440 | tf_op jit(solution)/shard_map/ppermute | solution.py:311
  12.4 2.2 %copy-start = (bf16[512,4096]{1,0:T(8,128)(2,1)S(1)}, bf16[512,4096]{1,0:T(8,128)(2,1)}, u32[]{:S(2)}) copy-start(bf16[512,4096]{1,0:T(8,128)(2,1)} %w_ref.5) | copy-start | bytes 12582916
  16.4 1.0 copy-start.3
  18.0 14.0 %collective-permute-start.6 = (bf16[2,512,128]{2,1,0:T(8,128)(2,1)}, bf16[2,512,128]{2,1,0:T(8,128)(2,1)}, u32[]{:S(2)}, u32[]{:S(2)}) collective-permute-start(bf16[2,512,128]{2,1,0:T(8,128)(2,1)} %collective-permute-done.1.near_ref.fold_near_ref), channel_id=1, source_target_pairs={{0,16},{8,24},{16,32},{24,40},{32,48},{40,56},{48,64},{56,72},{64,... | collective-permute-start | bytes 786440 | tf_op jit(solution)/shard_map/ppermute | solution.py:311
  19.9 28.8 %collective-permute-start.10 = (bf16[512,1024]{1,0:T(8,128)(2,1)}, bf16[512,1024]{1,0:T(8,128)(2,1)S(1)}, u32[]{:S(2)}, u32[]{:S(2)}) collective-permute-start(bf16[512,1024]{1,0:T(8,128)(2,1)} %get-tuple-element.31), channel_id=1, source_target_pairs={{0,2},{1,3},{2,4},{3,5},{4,6},{5,7},{6,0},{7,1},{8,14},{9,15},{10,... | collective-permute-start | bytes 3145736 | tf_op jit(solution)/shard_map/ppermute | solution.py:344
  21.5 10.5 %collective-permute-start.5 = (bf16[2,512,128]{2,1,0:T(8,128)(2,1)S(1)}, bf16[2,512,128]{2,1,0:T(8,128)(2,1)S(1)}, u32[]{:S(2)}, u32[]{:S(2)}) collective-permute-start(bf16[2,512,128]{2,1,0:T(8,128)(2,1)S(1)} %broadcast_select_fusion.near_ref), channel_id=1, source_target_pairs={{0,8},{8,0},{16,24},{24,16},{32,40},{40,32},{48,56},{56,48},{64,72... | collective-permute-start | bytes 786440 | tf_op jit(solution)/shard_map/ppermute | solution.py:311
  21.8 14.5 %collective-permute-start.8 = (bf16[2,512,128]{2,1,0:T(8,128)(2,1)S(1)}, bf16[2,512,128]{2,1,0:T(8,128)(2,1)}, u32[]{:S(2)}, u32[]{:S(2)}) collective-permute-start(bf16[2,512,128]{2,1,0:T(8,128)(2,1)S(1)} %broadcast_select_fusion.near_ref), channel_id=1, source_target_pairs={{16,0},{24,8},{32,16},{40,24},{48,32},{56,40},{64,48},{72,56},{80,... | collective-permute-start | bytes 786440 | tf_op jit(solution)/shard_map/ppermute | solution.py:311
  29.8 6.5 %collective-permute-start.4 = (bf16[2,512,128]{2,1,0:T(8,128)(2,1)}, bf16[2,512,128]{2,1,0:T(8,128)(2,1)}, u32[]{:S(2)}, u32[]{:S(2)}) collective-permute-start(bf16[2,512,128]{2,1,0:T(8,128)(2,1)} %collective-permute-done.1.near_ref.fold_near_ref), channel_id=1, source_target_pairs={{0,8},{8,0},{16,24},{24,16},{32,40},{40,32},{48,56},{56,48},{64,72... | collective-permute-start | bytes 786440 | tf_op jit(solution)/shard_map/ppermute | solution.py:311
  32.0 4.7 %collective-permute-start.7 = (bf16[2,512,128]{2,1,0:T(8,128)(2,1)}, bf16[2,512,128]{2,1,0:T(8,128)(2,1)}, u32[]{:S(2)}, u32[]{:S(2)}) collective-permute-start(bf16[2,512,128]{2,1,0:T(8,128)(2,1)} %collective-permute-done.6.far_ref), channel_id=1, source_target_pairs={{0,8},{8,0},{16,24},{24,16},{32,40},{40,32},{48,56},{56,48},{64,72... | collective-permute-start | bytes 786440 | tf_op jit(solution)/shard_map/ppermute | solution.py:311
  32.0 0.7 copy-start.4
  32.7 16.0 %collective-permute-start.11 = (bf16[256,1024]{1,0:T(8,128)(2,1)}, bf16[256,1024]{1,0:T(8,128)(2,1)S(1)}, u32[]{:S(2)}, u32[]{:S(2)}) collective-permute-start(bf16[256,1024]{1,0:T(8,128)(2,1)} %get-tuple-element.33), channel_id=1, source_target_pairs={{0,4},{1,5},{2,6},{3,7},{4,0},{5,1},{6,2},{7,3},{8,12},{9,13},{10,... | collective-permute-start | bytes 1572872 | tf_op jit(solution)/shard_map/ppermute | solution.py:316
  36.3 25.9 %collective-permute-start.16 = (bf16[1024,512]{1,0:T(8,128)(2,1)}, bf16[1024,512]{1,0:T(8,128)(2,1)S(1)}, u32[]{:S(2)}, u32[]{:S(2)}) collective-permute-start(bf16[1024,512]{1,0:T(8,128)(2,1)} %copy-done.3), channel_id=1, source_target_pairs={{0,1},{1,0},{2,3},{3,2},{4,5},{5,4},{6,7},{7,6},{8,9},{9,8},{10,11... | collective-permute-start | bytes 3145736 | tf_op jit(solution)/shard_map/ppermute | solution.py:316
  36.3 10.1 %collective-permute-start.9 = (bf16[2,512,128]{2,1,0:T(8,128)(2,1)}, bf16[2,512,128]{2,1,0:T(8,128)(2,1)S(1)}, u32[]{:S(2)}, u32[]{:S(2)}) collective-permute-start(bf16[2,512,128]{2,1,0:T(8,128)(2,1)} %collective-permute-done.8.far_ref), channel_id=1, source_target_pairs={{0,8},{8,0},{16,24},{24,16},{32,40},{40,32},{48,56},{56,48},{64,72... | collective-permute-start | bytes 786440 | tf_op jit(solution)/shard_map/ppermute | solution.py:311
  36.6 1.2 %copy-start.2 = (bf16[2,512,512]{2,1,0:T(8,128)(2,1)S(1)}, bf16[2,512,512]{2,1,0:T(8,128)(2,1)}, u32[]{:S(2)}) copy-start(bf16[2,512,512]{2,1,0:T(8,128)(2,1)} %q_ref.3) | copy-start | bytes 3145732
  37.9 16.0 %copy-start.5 = (bf16[2,512,128]{2,1,0:T(8,128)(2,1)S(1)}, bf16[2,512,128]{2,1,0:T(8,128)(2,1)}, u32[]{:S(2)}) copy-start(bf16[2,512,128]{2,1,0:T(8,128)(2,1)} %copy-done.4) | copy-start | bytes 786436
  46.4 28.8 %copy-start.1 = (bf16[512,4096]{1,0:T(8,128)(2,1)S(1)}, bf16[512,4096]{1,0:T(8,128)(2,1)}, u32[]{:S(2)}) copy-start(bf16[512,4096]{1,0:T(8,128)(2,1)} %w_ref.5) | copy-start | bytes 12582916
  48.7 16.4 %collective-permute-start.14 = (bf16[512,512]{1,0:T(8,128)(2,1)S(1)}, bf16[512,512]{1,0:T(8,128)(2,1)S(1)}, u32[]{:S(2)}, u32[]{:S(2)}) collective-permute-start(bf16[512,512]{1,0:T(8,128)(2,1)S(1)} %attend0.1.own_ref), channel_id=1, source_target_pairs={{0,4},{1,5},{2,6},{3,7},{4,0},{5,1},{6,2},{7,3},{8,12},{9,13},{10,... | collective-permute-start | bytes 1572872 | tf_op jit(solution)/shard_map/ppermute | solution.py:316
  51.8 23.4 %collective-permute-start.13 = (bf16[512,512]{1,0:T(8,128)(2,1)S(1)}, bf16[512,512]{1,0:T(8,128)(2,1)S(1)}, u32[]{:S(2)}, u32[]{:S(2)}) collective-permute-start(bf16[512,512]{1,0:T(8,128)(2,1)S(1)} %attend0.1.own_ref), channel_id=1, source_target_pairs={{0,6},{1,7},{2,0},{3,1},{4,2},{5,3},{6,4},{7,5},{8,14},{9,15},{10,... | collective-permute-start | bytes 1572872 | tf_op jit(solution)/shard_map/ppermute | solution.py:316
  53.0 22.2 %collective-permute-start.12 = (bf16[512,512]{1,0:T(8,128)(2,1)S(1)}, bf16[512,512]{1,0:T(8,128)(2,1)S(1)}, u32[]{:S(2)}, u32[]{:S(2)}) collective-permute-start(bf16[512,512]{1,0:T(8,128)(2,1)S(1)} %attend0.1.own_ref), channel_id=1, source_target_pairs={{0,2},{1,3},{2,4},{3,5},{4,6},{5,7},{6,0},{7,1},{8,10},{9,11},{10,... | collective-permute-start | bytes 1572872 | tf_op jit(solution)/shard_map/ppermute | solution.py:316
  62.2 14.8 %collective-permute-start.17 = (bf16[1024,512]{1,0:T(8,128)(2,1)S(1)}, bf16[1024,512]{1,0:T(8,128)(2,1)S(1)}, u32[]{:S(2)}, u32[]{:S(2)}) collective-permute-start(bf16[1024,512]{1,0:T(8,128)(2,1)S(1)} %collective-permute-done.16.wm_ref), channel_id=1, source_target_pairs={{0,8},{8,0},{16,24},{24,16},{32,40},{40,32},{48,56},{56,48},{64,72... | collective-permute-start | bytes 3145736 | tf_op jit(solution)/shard_map/ppermute | solution.py:311
  62.3 14.7 %collective-permute-start.15 = (bf16[512,512]{1,0:T(8,128)(2,1)S(1)}, bf16[512,512]{1,0:T(8,128)(2,1)S(1)}, u32[]{:S(2)}, u32[]{:S(2)}) collective-permute-start(bf16[512,512]{1,0:T(8,128)(2,1)S(1)} %attend1.1.own_ref), channel_id=1, source_target_pairs={{0,1},{1,0},{2,3},{3,2},{4,5},{5,4},{6,7},{7,6},{8,9},{9,8},{10,11... | collective-permute-start | bytes 1572872 | tf_op jit(solution)/shard_map/ppermute | solution.py:316
  78.9 5.5 %collective-permute-start.18 = (bf16[512,1024]{1,0:T(8,128)(2,1)S(1)}, bf16[512,1024]{1,0:T(8,128)(2,1)S(1)}, u32[]{:S(2)}, u32[]{:S(2)}) collective-permute-start(bf16[512,1024]{1,0:T(8,128)(2,1)S(1)} %collective-permute-done.10.ws_ref), channel_id=1, source_target_pairs={{0,8},{8,0},{16,24},{24,16},{32,40},{40,32},{48,56},{56,48},{64,72... | collective-permute-start | bytes 3145736 | tf_op jit(solution)/shard_map/ppermute | solution.py:311
  79.0 5.4 %collective-permute-start.19 = (bf16[256,1024]{1,0:T(8,128)(2,1)S(1)}, bf16[256,1024]{1,0:T(8,128)(2,1)S(1)}, u32[]{:S(2)}, u32[]{:S(2)}) collective-permute-start(bf16[256,1024]{1,0:T(8,128)(2,1)S(1)} %collective-permute-done.11.wf_ref), channel_id=1, source_target_pairs={{0,8},{8,0},{16,24},{24,16},{32,40},{40,32},{48,56},{56,48},{64,72... | collective-permute-start | bytes 1572872 | tf_op jit(solution)/shard_map/ppermute | solution.py:311
  79.5 15.1 %collective-permute-start.22 = (bf16[512,512]{1,0:T(8,128)(2,1)S(1)}, bf16[512,512]{1,0:T(8,128)(2,1)S(1)}, u32[]{:S(2)}, u32[]{:S(2)}) collective-permute-start(bf16[512,512]{1,0:T(8,128)(2,1)S(1)} %get-tuple-element.45), channel_id=1, source_target_pairs={{0,2},{1,3},{2,4},{3,5},{4,6},{5,7},{6,0},{7,1},{8,10},{9,11},{10,... | collective-permute-start | bytes 1572872 | tf_op jit(solution)/shard_map/ppermute | solution.py:316
  80.9 24.2 %collective-permute-start.23 = (bf16[512,512]{1,0:T(8,128)(2,1)S(1)}, bf16[512,512]{1,0:T(8,128)(2,1)S(1)}, u32[]{:S(2)}, u32[]{:S(2)}) collective-permute-start(bf16[512,512]{1,0:T(8,128)(2,1)S(1)} %get-tuple-element.46), channel_id=1, source_target_pairs={{0,6},{1,7},{2,0},{3,1},{4,2},{5,3},{6,4},{7,5},{8,14},{9,15},{10,... | collective-permute-start | bytes 1572872 | tf_op jit(solution)/shard_map/ppermute | solution.py:316
  82.7 24.0 %collective-permute-start.21 = (bf16[512,512]{1,0:T(8,128)(2,1)S(1)}, bf16[512,512]{1,0:T(8,128)(2,1)S(1)}, u32[]{:S(2)}, u32[]{:S(2)}) collective-permute-start(bf16[512,512]{1,0:T(8,128)(2,1)S(1)} %get-tuple-element.39), channel_id=1, source_target_pairs={{0,4},{1,5},{2,6},{3,7},{4,0},{5,1},{6,2},{7,3},{8,12},{9,13},{10,... | collective-permute-start | bytes 1572872 | tf_op jit(solution)/shard_map/ppermute | solution.py:316
  87.3 20.2 %collective-permute-start.20 = (bf16[512,512]{1,0:T(8,128)(2,1)S(1)}, bf16[512,512]{1,0:T(8,128)(2,1)S(1)}, u32[]{:S(2)}, u32[]{:S(2)}) collective-permute-start(bf16[512,512]{1,0:T(8,128)(2,1)S(1)} %get-tuple-element.43), channel_id=1, source_target_pairs={{0,1},{1,0},{2,3},{3,2},{4,5},{5,4},{6,7},{7,6},{8,9},{9,8},{10,11... | collective-permute-start | bytes 1572872 | tf_op jit(solution)/shard_map/ppermute | solution.py:316

commit v5 on v4

--- a/solution.py
+++ b/solution.py
@@ -268,6 +268,11 @@
             ref[r, :] = (acc + mm(peer_ref[r, other], wp_ref[w_rows, :])).astype(BF16)
 
 
+def order_kernel(info_ref, o_ref):
+    for i in range(3):
+        o_ref[i] = info_ref[i]
+
+
 def total_kernel(info_ref, first_ref, *refs):
     *more, o_ref = refs
     total = first_ref[...].astype(F32)
@@ -377,11 +382,20 @@
     piece = jax.ShapeDtypeStruct((blk, width), BF16)
     [part] = project(
         own_part_kernel, "own_part", [jax.ShapeDtypeStruct((ring, blk, width), F32)],
-        [place, after(mixed1, left, right, opposite), out_weight], 8 * STEP,
+        [place, mixed1, out_weight],
     )
     w_peer2 = swap(after(w_peer, mixed1))
+    gathered_place = pl.pallas_call(
+        order_kernel,
+        out_shape=jax.ShapeDtypeStruct((3,), jnp.int32),
+        in_specs=[SMEM],
+        out_specs=SMEM,
+        compiler_params=pltpu.CompilerParams(vmem_limit_bytes=16 * 2**20),
+        cost_estimate=pl.CostEstimate(flops=8 * STEP, bytes_accessed=1, transcendentals=0),
+        name="order",
+    )(after(place, left, right, opposite, part))
     far, up, down, keep1 = project(
-        reduce_first_kernel, "reduce_first", [piece] * 4, [place, peer, part, w_peer, w_peer2]
+        reduce_first_kernel, "reduce_first", [piece] * 4, [gathered_place, peer, part, w_peer, w_peer2]
     )
     got_far, got_up, got_down = across(far), plus(up), minus(down)
     w_side2, w_far2 = swap(after(w_side, far)), swap(after(w_far, far))

time: 110 us -> 109 us (level)
  Pallas kernels: 27.8 us -> 29.3 us
  waiting for transfers between devices: 37 us -> 35.5 us
    ppermute x10, waiting for transfers between devices: 34.4 us -> 32.8 us  [head_move(): return lax.ppermute(array, 'head', [(i, to(i)) for i in range(2 * ring)])]
    pallas_call x0 -> x1, Pallas kernels: none -> 1.14 us  [on_device(): pl.pallas_call(order_kernel, out_shape=jax.ShapeDtypeStruct((3,), jnp.int...]
  transfers between devices with their start and end apart: 24 -> 24, of which waited for: 8 -> 9; matrix products, arithmetic and copies ran while one was open for 1% -> 1% of each run, Pallas kernels for 22% -> 24%
where the time goes in v5:
time: 109 us
  starting transfers between devices  36.8 us (34%)
  waiting for transfers between devices  35.5 us (33%)
  Pallas kernels  29.3 us (27%)
  local copies, waits for them, and re-layouts  6.55 us (6%)
    ppermute x10, waiting for transfers between devices, head_move(): return lax.ppermute(array, 'head', [(i, to(i)) for i in range(2 * ring)])  32.8 us
    ppermute x13, starting transfers between devices, ctx_move(): lax.ppermute(array, 'ctx', [(i, to(i)) for i in range(ctx_size) if 0 <= t...  22.3 us
    pallas_call x2, Pallas kernels, attention(): pl.pallas_call(functools.partial(attn_kernel, half), out_shape=[jax.Shape...  17.3 us
    ppermute x10, starting transfers between devices, head_move(): return lax.ppermute(array, 'head', [(i, to(i)) for i in range(2 * ring)])  12.9 us
    pallas_call x5, Pallas kernels, project(): pl.pallas_call(kernel, out_shape=outs, in_specs=[SMEM] + [VMEM] * (len(ar...  8.99 us
    unnamed x14, local copies, waits for them, and re-layouts  5.11 us
    ppermute x13, waiting for transfers between devices, ctx_move(): lax.ppermute(array, 'ctx', [(i, to(i)) for i in range(ctx_size) if 0 <= t...  2.65 us
  transfers between devices with their start and end apart: 24, of which 9 were waited for; matrix products, arithmetic and copies ran while one was open for 1% of the time, Pallas kernels for 24%

profile of v5, /device:TPU:24, one launch (start us, length us, event | category | flops | bytes accessed | tf_op | source)
XLA Modules:
  0.0 108.7 jit_solution(7740513847492709728)
XLA Ops:
  0.0 1.1 %fusion = (bf16[1,512,128]{2,1,0:T(8,128)(2,1)S(1)}, bf16[1,512,128]{2,1,0:T(8,128)(2,1)S(1)}, bf16[1,512,128]{2,1,0:T(8,128)(2,1)S(1)}, bf16[1,512,128]{2,1,0:T(8,128)(2,1)S(1)}) fusion(bf16[2,512,128]{2,1,0:T(8,128)(2,1)} %param.6, bf16[2,512,128]{2,1,0:T(8,128)(2,1)} %param.7), kind=kLoop, calls=%fused_computation.8 | loop fusion | bytes 1048576 | tf_op jit(solution)/shard_map/slice | solution.py:339
  1.2 0.1 collective-permute-start
  1.3 0.6 collective-permute-start.3
  1.9 3.8 %collective-permute-start.1 = (bf16[2,512,128]{2,1,0:T(8,128)(2,1)S(1)}, bf16[2,512,128]{2,1,0:T(8,128)(2,1)}, u32[]{:S(2)}, u32[]{:S(2)}) collective-permute-start(bf16[2,512,128]{2,1,0:T(8,128)(2,1)S(1)} %pad_maximum_fusion.own_ref), channel_id=1, source_target_pairs={{0,16},{8,24},{16,32},{24,40},{32,48},{40,56},{48,64},{56,72},{64,... | collective-permute-start | bytes 786440 | tf_op jit(solution)/shard_map/ppermute | solution.py:316
  5.7 6.5 %collective-permute-start.2 = (bf16[2,512,128]{2,1,0:T(8,128)(2,1)S(1)}, bf16[2,512,128]{2,1,0:T(8,128)(2,1)S(1)}, u32[]{:S(2)}, u32[]{:S(2)}) collective-permute-start(bf16[2,512,128]{2,1,0:T(8,128)(2,1)S(1)} %pad_maximum_fusion.1.own_ref), channel_id=1, source_target_pairs={{16,0},{24,8},{32,16},{40,24},{48,32},{56,40},{64,48},{72,56},{80,... | collective-permute-start | bytes 786440 | tf_op jit(solution)/shard_map/ppermute | solution.py:316
  12.3 0.1 pad_add_fusion.info_ref
  12.4 2.2 %copy-done = bf16[512,4096]{1,0:T(8,128)(2,1)S(1)} copy-done((bf16[512,4096]{1,0:T(8,128)(2,1)S(1)}, bf16[512,4096]{1,0:T(8,128)(2,1)}, u32[]{:S(2)}) %copy-start) | copy-done | bytes 4194328
  14.6 1.9 %split_weights.1 = (bf16[512,1024]{1,0:T(8,128)(2,1)}, bf16[256,1024]{1,0:T(8,128)(2,1)}, bf16[1024,512]{1,0:T(8,128)(2,1)S(1)}) custom-call(s32[3]{0:T(128)S(1)} %pad_add_fusion.info_ref, bf16[512,4096]{1,0:T(8,128)(2,1)S(1)} %copy-done), custom_call_target="tpu_custom_call" | custom-call | flops 1 | bytes 1 | tf_op jit(solution)/shard_map/split_weights/pallas_call | solution.py:196
  16.4 1.0 copy-done.3
  17.4 0.0 collective-permute-done.3.traded_ref
  17.4 0.0 collective-permute-done.1.near_ref.fold_near_ref
  17.4 0.6 collective-permute-done.2
  18.0 1.9 %collective-permute-start.6 = (bf16[2,512,128]{2,1,0:T(8,128)(2,1)}, bf16[2,512,128]{2,1,0:T(8,128)(2,1)}, u32[]{:S(2)}, u32[]{:S(2)}) collective-permute-start(bf16[2,512,128]{2,1,0:T(8,128)(2,1)} %collective-permute-done.1.near_ref.fold_near_ref), channel_id=1, source_target_pairs={{0,16},{8,24},{16,32},{24,40},{32,48},{40,56},{48,64},{56,72},{64,... | collective-permute-start | bytes 786440 | tf_op jit(solution)/shard_map/ppermute | solution.py:316
  19.9 1.6 %collective-permute-start.10 = (bf16[512,1024]{1,0:T(8,128)(2,1)}, bf16[512,1024]{1,0:T(8,128)(2,1)S(1)}, u32[]{:S(2)}, u32[]{:S(2)}) collective-permute-start(bf16[512,1024]{1,0:T(8,128)(2,1)} %get-tuple-element.31), channel_id=1, source_target_pairs={{0,2},{1,3},{2,4},{3,5},{4,6},{5,7},{6,0},{7,1},{8,14},{9,15},{10,... | collective-permute-start | bytes 3145736 | tf_op jit(solution)/shard_map/ppermute | solution.py:349
  21.5 0.3 collective-permute-start.5
  21.8 8.0 %collective-permute-start.8 = (bf16[2,512,128]{2,1,0:T(8,128)(2,1)S(1)}, bf16[2,512,128]{2,1,0:T(8,128)(2,1)}, u32[]{:S(2)}, u32[]{:S(2)}) collective-permute-start(bf16[2,512,128]{2,1,0:T(8,128)(2,1)S(1)} %broadcast_select_fusion.near_ref), channel_id=1, source_target_pairs={{16,0},{24,8},{32,16},{40,24},{48,32},{56,40},{64,48},{72,56},{80,... | collective-permute-start | bytes 786440 | tf_op jit(solution)/shard_map/ppermute | solution.py:316
  29.8 0.2 collective-permute-start.4
  29.9 2.0 %collective-permute-done.6.far_ref = bf16[2,512,128]{2,1,0:T(8,128)(2,1)} collective-permute-done((bf16[2,512,128]{2,1,0:T(8,128)(2,1)}, bf16[2,512,128]{2,1,0:T(8,128)(2,1)}, u32[]{:S(2)}, u32[]{:S(2)}) %collective-permute-start.6) | collective-permute-done | bytes 262176 | tf_op jit(solution)/shard_map/ppermute | solution.py:316
  32.0 0.0 collective-permute-start.7
  32.0 0.0 collective-permute-done.5.near_traded_ref
  32.0 0.7 copy-done.4
  32.7 3.1 %collective-permute-start.11 = (bf16[256,1024]{1,0:T(8,128)(2,1)}, bf16[256,1024]{1,0:T(8,128)(2,1)S(1)}, u32[]{:S(2)}, u32[]{:S(2)}) collective-permute-start(bf16[256,1024]{1,0:T(8,128)(2,1)} %get-tuple-element.33), channel_id=1, source_target_pairs={{0,4},{1,5},{2,6},{3,7},{4,0},{5,1},{6,2},{7,3},{8,12},{9,13},{10,... | collective-permute-start | bytes 1572872 | tf_op jit(solution)/shard_map/ppermute | solution.py:321
  35.8 0.1 add_add_fusion.info_ref
  35.9 0.1 copy.7.doc_ref
  36.0 0.1 copy.6.doc_ref
  36.2 0.1 add_add_fusion.1.info_ref
  36.3 0.0 collective-permute-done.4.near_traded_ref.fold_traded_ref
  36.3 0.0 collective-permute-start.16
  36.3 0.0 collective-permute-done.8.far_ref
  36.3 0.3 collective-permute-start.9
  36.6 0.0 collective-permute-done.7.far_traded_ref
  36.6 1.2 %copy-done.2 = bf16[2,512,512]{2,1,0:T(8,128)(2,1)S(1)} copy-done((bf16[2,512,512]{2,1,0:T(8,128)(2,1)S(1)}, bf16[2,512,512]{2,1,0:T(8,128)(2,1)}, u32[]{:S(2)}) %copy-start.2) | copy-done | bytes 1048600
  37.9 8.8 %attend0.1.own_ref = bf16[512,512]{1,0:T(8,128)(2,1)S(1)} custom-call(s32[3]{0:T(128)S(1)} %add_add_fusion.info_ref, bf16[2,512,512]{2,1,0:T(8,128)(2,1)S(1)} %copy-done.2, s32[512,1]{1,0:T(8,128)S(1)} %copy.6.doc_ref, bf16[2,512,128]{2,1,0:T(8,128)(2,1)S(1)} %pad_maximum_fusion.own_ref, bf16[2,512,128]{2,1,0:T(8,128)(2,1)S(1)} %collective-permute-done.traded_ref, ...), custom_call_target="tpu_custom_call" | custom-call | flops 4000000000 | bytes 1 | tf_op jit(solution)/shard_map/attend0/pallas_call | solution.py:159
  46.7 0.0 copy-start.1
  46.7 0.0 collective-permute-done.9.far_traded_ref
  46.7 2.1 %collective-permute-done.11.wf_ref = bf16[256,1024]{1,0:T(8,128)(2,1)S(1)} collective-permute-done((bf16[256,1024]{1,0:T(8,128)(2,1)}, bf16[256,1024]{1,0:T(8,128)(2,1)S(1)}, u32[]{:S(2)}, u32[]{:S(2)}) %collective-permute-start.11) | collective-permute-done | bytes 524320 | tf_op jit(solution)/shard_map/ppermute | solution.py:321
  48.7 3.1 %collective-permute-start.14 = (bf16[512,512]{1,0:T(8,128)(2,1)S(1)}, bf16[512,512]{1,0:T(8,128)(2,1)S(1)}, u32[]{:S(2)}, u32[]{:S(2)}) collective-permute-start(bf16[512,512]{1,0:T(8,128)(2,1)S(1)} %attend0.1.own_ref), channel_id=1, source_target_pairs={{0,4},{1,5},{2,6},{3,7},{4,0},{5,1},{6,2},{7,3},{8,12},{9,13},{10,... | collective-permute-start | bytes 1572872 | tf_op jit(solution)/shard_map/ppermute | solution.py:321
  51.8 1.1 %collective-permute-start.13 = (bf16[512,512]{1,0:T(8,128)(2,1)S(1)}, bf16[512,512]{1,0:T(8,128)(2,1)S(1)}, u32[]{:S(2)}, u32[]{:S(2)}) collective-permute-start(bf16[512,512]{1,0:T(8,128)(2,1)S(1)} %attend0.1.own_ref), channel_id=1, source_target_pairs={{0,6},{1,7},{2,0},{3,1},{4,2},{5,3},{6,4},{7,5},{8,14},{9,15},{10,... | collective-permute-start | bytes 1572872 | tf_op jit(solution)/shard_map/ppermute | solution.py:321
  53.0 0.9 collective-permute-start.12
  53.9 8.5 %attend1.1.own_ref = bf16[512,512]{1,0:T(8,128)(2,1)S(1)} custom-call(s32[3]{0:T(128)S(1)} %add_add_fusion.1.info_ref, bf16[2,512,512]{2,1,0:T(8,128)(2,1)S(1)} %copy-done.2, s32[512,1]{1,0:T(8,128)S(1)} %copy.7.doc_ref, bf16[2,512,128]{2,1,0:T(8,128)(2,1)S(1)} %pad_maximum_fusion.1.own_ref, bf16[2,512,128]{2,1,0:T(8,128)(2,1)S(1)} %collective-permute-done.3.traded_ref, ...), custom_call_target="tpu_custom_call" | custom-call | flops 10737418240 | bytes 4194304 | tf_op jit(solution)/shard_map/attend1/pallas_call | solution.py:159
  62.4 0.0 collective-permute-done.16.wm_ref
  62.4 0.1 collective-permute-start.17
  62.5 0.1 collective-permute-start.15
  62.7 1.8 %own_part.1.part_ref = f32[4,512,512]{2,1,0:T(8,128)S(1)} custom-call(s32[3]{0:T(128)S(1)} %pad_add_fusion.info_ref, bf16[512,512]{1,0:T(8,128)(2,1)S(1)} %attend1.1.own_ref, bf16[512,4096]{1,0:T(8,128)(2,1)S(1)} %copy-done.1), custom_call_target="tpu_custom_call" | custom-call | bytes 1 | tf_op jit(solution)/shard_map/own_part/pallas_call | solution.py:290
  64.5 0.7 collective-permute-done.14.far_ref
  65.1 10.1 %collective-permute-done.13.right_ref = bf16[512,512]{1,0:T(8,128)(2,1)S(1)} collective-permute-done((bf16[512,512]{1,0:T(8,128)(2,1)S(1)}, bf16[512,512]{1,0:T(8,128)(2,1)S(1)}, u32[]{:S(2)}, u32[]{:S(2)}) %collective-permute-start.13) | collective-permute-done | bytes 524320 | tf_op jit(solution)/shard_map/ppermute | solution.py:321
  75.2 0.0 collective-permute-done.12.left_ref
  75.2 1.1 %order.1.info_ref = s32[3]{0:T(128)S(1)} custom-call(s32[3]{0:T(128)S(1)} %pad_add_fusion.info_ref), custom_call_target="tpu_custom_call" | custom-call | flops 8000000000 | bytes 1 | tf_op jit(solution)/shard_map/order/pallas_call | solution.py:388
  76.4 0.5 collective-permute-done.15.peer_ref
  76.9 0.0 collective-permute-done.17.wp_ref
  76.9 1.8 %reduce_first.1 = (bf16[512,512]{1,0:T(8,128)(2,1)S(1)}, bf16[512,512]{1,0:T(8,128)(2,1)S(1)}, bf16[512,512]{1,0:T(8,128)(2,1)S(1)}, bf16[512,512]{1,0:T(8,128)(2,1)S(1)}) custom-call(s32[3]{0:T(128)S(1)} %order.1.info_ref, bf16[512,512]{1,0:T(8,128)(2,1)S(1)} %collective-permute-done.15.peer_ref, f32[4,512,512]{2,1,0:T(8,128)S(1)} %own_part.1.part_ref, ...), custom_call_target="tpu_custom_call" | custom-call | bytes 1 | tf_op jit(solution)/shard_map/reduce_first/pallas_call | solution.py:290
  78.7 0.1 collective-permute-start.18
  78.8 0.5 collective-permute-start.19
  79.3 0.9 collective-permute-start.22
  80.3 2.3 %collective-permute-start.23 = (bf16[512,512]{1,0:T(8,128)(2,1)S(1)}, bf16[512,512]{1,0:T(8,128)(2,1)S(1)}, u32[]{:S(2)}, u32[]{:S(2)}) collective-permute-start(bf16[512,512]{1,0:T(8,128)(2,1)S(1)} %get-tuple-element.46), channel_id=1, source_target_pairs={{0,6},{1,7},{2,0},{3,1},{4,2},{5,3},{6,4},{7,5},{8,14},{9,15},{10,... | collective-permute-start | bytes 1572872 | tf_op jit(solution)/shard_map/ppermute | solution.py:321
  82.6 1.2 %collective-permute-start.21 = (bf16[512,512]{1,0:T(8,128)(2,1)S(1)}, bf16[512,512]{1,0:T(8,128)(2,1)S(1)}, u32[]{:S(2)}, u32[]{:S(2)}) collective-permute-start(bf16[512,512]{1,0:T(8,128)(2,1)S(1)} %get-tuple-element.39), channel_id=1, source_target_pairs={{0,4},{1,5},{2,6},{3,7},{4,0},{5,1},{6,2},{7,3},{8,12},{9,13},{10,... | collective-permute-start | bytes 1572872 | tf_op jit(solution)/shard_map/ppermute | solution.py:321
  83.7 0.0 collective-permute-done.19.wfp_ref
  83.8 2.9 %gather_first.1 = (bf16[512,512]{1,0:T(8,128)(2,1)S(1)}, bf16[512,512]{1,0:T(8,128)(2,1)S(1)}) custom-call(s32[3]{0:T(128)S(1)} %pad_add_fusion.info_ref, bf16[512,512]{1,0:T(8,128)(2,1)S(1)} %attend0.1.own_ref, bf16[512,512]{1,0:T(8,128)(2,1)S(1)} %collective-permute-done.12.left_ref, bf16[512,512]{1,0:T(8,128)(2,1)S(1)} %collective-permute-done.13.right_ref, ...), custom_call_target="tpu_custom_call" | custom-call | bytes 1 | tf_op jit(solution)/shard_map/gather_first/pallas_call | solution.py:290
  86.7 0.1 collective-permute-start.20
  86.8 7.9 %collective-permute-done.22.refs_1_ = bf16[512,512]{1,0:T(8,128)(2,1)S(1)} collective-permute-done((bf16[512,512]{1,0:T(8,128)(2,1)S(1)}, bf16[512,512]{1,0:T(8,128)(2,1)S(1)}, u32[]{:S(2)}, u32[]{:S(2)}) %collective-permute-start.22) | collective-permute-done | bytes 524320 | tf_op jit(solution)/shard_map/ppermute | solution.py:321
  94.7 10.3 %collective-permute-done.23.refs_2_ = bf16[512,512]{1,0:T(8,128)(2,1)S(1)} collective-permute-done((bf16[512,512]{1,0:T(8,128)(2,1)S(1)}, bf16[512,512]{1,0:T(8,128)(2,1)S(1)}, u32[]{:S(2)}, u32[]{:S(2)}) %collective-permute-start.23) | collective-permute-done | bytes 524320 | tf_op jit(solution)/shard_map/ppermute | solution.py:321
  105.0 1.3 %collective-permute-done.21.refs_0_ = bf16[512,512]{1,0:T(8,128)(2,1)S(1)} collective-permute-done((bf16[512,512]{1,0:T(8,128)(2,1)S(1)}, bf16[512,512]{1,0:T(8,128)(2,1)S(1)}, u32[]{:S(2)}, u32[]{:S(2)}) %collective-permute-start.21) | collective-permute-done | bytes 524320 | tf_op jit(solution)/shard_map/ppermute | solution.py:321
  106.3 0.8 total.1.done_ref
  107.1 1.7 %finish.1 = bf16[2,512,512]{2,1,0:T(8,128)(2,1)} custom-call(s32[3]{0:T(128)S(1)} %pad_add_fusion.info_ref, bf16[512,512]{1,0:T(8,128)(2,1)S(1)} %get-tuple-element.42.keep_ref, bf16[512,512]{1,0:T(8,128)(2,1)S(1)} %collective-permute-done.20.got_ref, bf16[512,512]{1,0:T(8,128)(2,1)S(1)} %total.1.done_ref), custom_call_target="tpu_custom_call" | custom-call | bytes 1 | tf_op jit(solution)/shard_map/finish/pallas_call | solution.py:290
  (17 shorter events, 0.1 us)
Async XLA Ops:
  0.0 32.0 %copy-start.6 = (s32[2,512]{1,0:T(2,128)S(1)}, s32[2,512]{1,0:T(2,128)}, u32[]{:S(2)}) copy-start(s32[2,512]{1,0:T(2,128)} %param.8) | copy-start | bytes 12292
  1.2 16.2 %collective-permute-start = (bf16[2,512,128]{2,1,0:T(8,128)(2,1)S(1)}, bf16[2,512,128]{2,1,0:T(8,128)(2,1)S(1)}, u32[]{:S(2)}, u32[]{:S(2)}) collective-permute-start(bf16[2,512,128]{2,1,0:T(8,128)(2,1)S(1)} %pad_maximum_fusion.own_ref), channel_id=1, source_target_pairs={{0,8},{8,0},{16,24},{24,16},{32,40},{40,32},{48,56},{56,48},{64,72... | collective-permute-start | bytes 786440 | tf_op jit(solution)/shard_map/ppermute | solution.py:316
  1.3 16.1 %collective-permute-start.3 = (bf16[2,512,128]{2,1,0:T(8,128)(2,1)S(1)}, bf16[2,512,128]{2,1,0:T(8,128)(2,1)S(1)}, u32[]{:S(2)}, u32[]{:S(2)}) collective-permute-start(bf16[2,512,128]{2,1,0:T(8,128)(2,1)S(1)} %pad_maximum_fusion.1.own_ref), channel_id=1, source_target_pairs={{0,8},{8,0},{16,24},{24,16},{32,40},{40,32},{48,56},{56,48},{64,72... | collective-permute-start | bytes 786440 | tf_op jit(solution)/shard_map/ppermute | solution.py:316
  1.9 15.5 %collective-permute-start.1 = (bf16[2,512,128]{2,1,0:T(8,128)(2,1)S(1)}, bf16[2,512,128]{2,1,0:T(8,128)(2,1)}, u32[]{:S(2)}, u32[]{:S(2)}) collective-permute-start(bf16[2,512,128]{2,1,0:T(8,128)(2,1)S(1)} %pad_maximum_fusion.own_ref), channel_id=1, source_target_pairs={{0,16},{8,24},{16,32},{24,40},{32,48},{40,56},{48,64},{56,72},{64,... | collective-permute-start | bytes 786440 | tf_op jit(solution)/shard_map/ppermute | solution.py:316
  5.7 12.3 %collective-permute-start.2 = (bf16[2,512,128]{2,1,0:T(8,128)(2,1)S(1)}, bf16[2,512,128]{2,1,0:T(8,128)(2,1)S(1)}, u32[]{:S(2)}, u32[]{:S(2)}) collective-permute-start(bf16[2,512,128]{2,1,0:T(8,128)(2,1)S(1)} %pad_maximum_fusion.1.own_ref), channel_id=1, source_target_pairs={{16,0},{24,8},{32,16},{40,24},{48,32},{56,40},{64,48},{72,56},{80,... | collective-permute-start | bytes 786440 | tf_op jit(solution)/shard_map/ppermute | solution.py:316
  12.4 2.2 %copy-start = (bf16[512,4096]{1,0:T(8,128)(2,1)S(1)}, bf16[512,4096]{1,0:T(8,128)(2,1)}, u32[]{:S(2)}) copy-start(bf16[512,4096]{1,0:T(8,128)(2,1)} %w_ref.5) | copy-start | bytes 12582916
  16.4 1.0 copy-start.3
  18.0 14.0 %collective-permute-start.6 = (bf16[2,512,128]{2,1,0:T(8,128)(2,1)}, bf16[2,512,128]{2,1,0:T(8,128)(2,1)}, u32[]{:S(2)}, u32[]{:S(2)}) collective-permute-start(bf16[2,512,128]{2,1,0:T(8,128)(2,1)} %collective-permute-done.1.near_ref.fold_near_ref), channel_id=1, source_target_pairs={{0,16},{8,24},{16,32},{24,40},{32,48},{40,56},{48,64},{56,72},{64,... | collective-permute-start | bytes 786440 | tf_op jit(solution)/shard_map/ppermute | solution.py:316
  19.9 28.8 %collective-permute-start.10 = (bf16[512,1024]{1,0:T(8,128)(2,1)}, bf16[512,1024]{1,0:T(8,128)(2,1)S(1)}, u32[]{:S(2)}, u32[]{:S(2)}) collective-permute-start(bf16[512,1024]{1,0:T(8,128)(2,1)} %get-tuple-element.31), channel_id=1, source_target_pairs={{0,2},{1,3},{2,4},{3,5},{4,6},{5,7},{6,0},{7,1},{8,14},{9,15},{10,... | collective-permute-start | bytes 3145736 | tf_op jit(solution)/shard_map/ppermute | solution.py:349
  21.5 10.5 %collective-permute-start.5 = (bf16[2,512,128]{2,1,0:T(8,128)(2,1)S(1)}, bf16[2,512,128]{2,1,0:T(8,128)(2,1)S(1)}, u32[]{:S(2)}, u32[]{:S(2)}) collective-permute-start(bf16[2,512,128]{2,1,0:T(8,128)(2,1)S(1)} %broadcast_select_fusion.near_ref), channel_id=1, source_target_pairs={{0,8},{8,0},{16,24},{24,16},{32,40},{40,32},{48,56},{56,48},{64,72... | collective-permute-start | bytes 786440 | tf_op jit(solution)/shard_map/ppermute | solution.py:316
  21.8 14.5 %collective-permute-start.8 = (bf16[2,512,128]{2,1,0:T(8,128)(2,1)S(1)}, bf16[2,512,128]{2,1,0:T(8,128)(2,1)}, u32[]{:S(2)}, u32[]{:S(2)}) collective-permute-start(bf16[2,512,128]{2,1,0:T(8,128)(2,1)S(1)} %broadcast_select_fusion.near_ref), channel_id=1, source_target_pairs={{16,0},{24,8},{32,16},{40,24},{48,32},{56,40},{64,48},{72,56},{80,... | collective-permute-start | bytes 786440 | tf_op jit(solution)/shard_map/ppermute | solution.py:316
  29.8 6.5 %collective-permute-start.4 = (bf16[2,512,128]{2,1,0:T(8,128)(2,1)}, bf16[2,512,128]{2,1,0:T(8,128)(2,1)}, u32[]{:S(2)}, u32[]{:S(2)}) collective-permute-start(bf16[2,512,128]{2,1,0:T(8,128)(2,1)} %collective-permute-done.1.near_ref.fold_near_ref), channel_id=1, source_target_pairs={{0,8},{8,0},{16,24},{24,16},{32,40},{40,32},{48,56},{56,48},{64,72... | collective-permute-start | bytes 786440 | tf_op jit(solution)/shard_map/ppermute | solution.py:316
  32.0 4.7 %collective-permute-start.7 = (bf16[2,512,128]{2,1,0:T(8,128)(2,1)}, bf16[2,512,128]{2,1,0:T(8,128)(2,1)}, u32[]{:S(2)}, u32[]{:S(2)}) collective-permute-start(bf16[2,512,128]{2,1,0:T(8,128)(2,1)} %collective-permute-done.6.far_ref), channel_id=1, source_target_pairs={{0,8},{8,0},{16,24},{24,16},{32,40},{40,32},{48,56},{56,48},{64,72... | collective-permute-start | bytes 786440 | tf_op jit(solution)/shard_map/ppermute | solution.py:316
  32.0 0.7 copy-start.4
  32.7 16.0 %collective-permute-start.11 = (bf16[256,1024]{1,0:T(8,128)(2,1)}, bf16[256,1024]{1,0:T(8,128)(2,1)S(1)}, u32[]{:S(2)}, u32[]{:S(2)}) collective-permute-start(bf16[256,1024]{1,0:T(8,128)(2,1)} %get-tuple-element.33), channel_id=1, source_target_pairs={{0,4},{1,5},{2,6},{3,7},{4,0},{5,1},{6,2},{7,3},{8,12},{9,13},{10,... | collective-permute-start | bytes 1572872 | tf_op jit(solution)/shard_map/ppermute | solution.py:321
  36.3 26.2 %collective-permute-start.16 = (bf16[1024,512]{1,0:T(8,128)(2,1)}, bf16[1024,512]{1,0:T(8,128)(2,1)S(1)}, u32[]{:S(2)}, u32[]{:S(2)}) collective-permute-start(bf16[1024,512]{1,0:T(8,128)(2,1)} %copy-done.3), channel_id=1, source_target_pairs={{0,1},{1,0},{2,3},{3,2},{4,5},{5,4},{6,7},{7,6},{8,9},{9,8},{10,11... | collective-permute-start | bytes 3145736 | tf_op jit(solution)/shard_map/ppermute | solution.py:321
  36.3 10.3 %collective-permute-start.9 = (bf16[2,512,128]{2,1,0:T(8,128)(2,1)}, bf16[2,512,128]{2,1,0:T(8,128)(2,1)S(1)}, u32[]{:S(2)}, u32[]{:S(2)}) collective-permute-start(bf16[2,512,128]{2,1,0:T(8,128)(2,1)} %collective-permute-done.8.far_ref), channel_id=1, source_target_pairs={{0,8},{8,0},{16,24},{24,16},{32,40},{40,32},{48,56},{56,48},{64,72... | collective-permute-start | bytes 786440 | tf_op jit(solution)/shard_map/ppermute | solution.py:316
  36.6 1.2 %copy-start.2 = (bf16[2,512,512]{2,1,0:T(8,128)(2,1)S(1)}, bf16[2,512,512]{2,1,0:T(8,128)(2,1)}, u32[]{:S(2)}) copy-start(bf16[2,512,512]{2,1,0:T(8,128)(2,1)} %q_ref.3) | copy-start | bytes 3145732
  37.9 16.0 %copy-start.5 = (bf16[2,512,128]{2,1,0:T(8,128)(2,1)S(1)}, bf16[2,512,128]{2,1,0:T(8,128)(2,1)}, u32[]{:S(2)}) copy-start(bf16[2,512,128]{2,1,0:T(8,128)(2,1)} %copy-done.4) | copy-start | bytes 786436
  46.7 16.0 %copy-start.1 = (bf16[512,4096]{1,0:T(8,128)(2,1)S(1)}, bf16[512,4096]{1,0:T(8,128)(2,1)}, u32[]{:S(2)}) copy-start(bf16[512,4096]{1,0:T(8,128)(2,1)} %w_ref.5) | copy-start | bytes 12582916
  48.7 16.4 %collective-permute-start.14 = (bf16[512,512]{1,0:T(8,128)(2,1)S(1)}, bf16[512,512]{1,0:T(8,128)(2,1)S(1)}, u32[]{:S(2)}, u32[]{:S(2)}) collective-permute-start(bf16[512,512]{1,0:T(8,128)(2,1)S(1)} %attend0.1.own_ref), channel_id=1, source_target_pairs={{0,4},{1,5},{2,6},{3,7},{4,0},{5,1},{6,2},{7,3},{8,12},{9,13},{10,... | collective-permute-start | bytes 1572872 | tf_op jit(solution)/shard_map/ppermute | solution.py:321
  51.8 23.4 %collective-permute-start.13 = (bf16[512,512]{1,0:T(8,128)(2,1)S(1)}, bf16[512,512]{1,0:T(8,128)(2,1)S(1)}, u32[]{:S(2)}, u32[]{:S(2)}) collective-permute-start(bf16[512,512]{1,0:T(8,128)(2,1)S(1)} %attend0.1.own_ref), channel_id=1, source_target_pairs={{0,6},{1,7},{2,0},{3,1},{4,2},{5,3},{6,4},{7,5},{8,14},{9,15},{10,... | collective-permute-start | bytes 1572872 | tf_op jit(solution)/shard_map/ppermute | solution.py:321
  53.0 22.2 %collective-permute-start.12 = (bf16[512,512]{1,0:T(8,128)(2,1)S(1)}, bf16[512,512]{1,0:T(8,128)(2,1)S(1)}, u32[]{:S(2)}, u32[]{:S(2)}) collective-permute-start(bf16[512,512]{1,0:T(8,128)(2,1)S(1)} %attend0.1.own_ref), channel_id=1, source_target_pairs={{0,2},{1,3},{2,4},{3,5},{4,6},{5,7},{6,0},{7,1},{8,10},{9,11},{10,... | collective-permute-start | bytes 1572872 | tf_op jit(solution)/shard_map/ppermute | solution.py:321
  62.4 14.4 %collective-permute-start.17 = (bf16[1024,512]{1,0:T(8,128)(2,1)S(1)}, bf16[1024,512]{1,0:T(8,128)(2,1)S(1)}, u32[]{:S(2)}, u32[]{:S(2)}) collective-permute-start(bf16[1024,512]{1,0:T(8,128)(2,1)S(1)} %collective-permute-done.16.wm_ref), channel_id=1, source_target_pairs={{0,8},{8,0},{16,24},{24,16},{32,40},{40,32},{48,56},{56,48},{64,72... | collective-permute-start | bytes 3145736 | tf_op jit(solution)/shard_map/ppermute | solution.py:316
  62.5 14.3 %collective-permute-start.15 = (bf16[512,512]{1,0:T(8,128)(2,1)S(1)}, bf16[512,512]{1,0:T(8,128)(2,1)S(1)}, u32[]{:S(2)}, u32[]{:S(2)}) collective-permute-start(bf16[512,512]{1,0:T(8,128)(2,1)S(1)} %attend1.1.own_ref), channel_id=1, source_target_pairs={{0,1},{1,0},{2,3},{3,2},{4,5},{5,4},{6,7},{7,6},{8,9},{9,8},{10,11... | collective-permute-start | bytes 1572872 | tf_op jit(solution)/shard_map/ppermute | solution.py:321
  78.7 5.0 %collective-permute-start.18 = (bf16[512,1024]{1,0:T(8,128)(2,1)S(1)}, bf16[512,1024]{1,0:T(8,128)(2,1)S(1)}, u32[]{:S(2)}, u32[]{:S(2)}) collective-permute-start(bf16[512,1024]{1,0:T(8,128)(2,1)S(1)} %collective-permute-done.10.ws_ref), channel_id=1, source_target_pairs={{0,8},{8,0},{16,24},{24,16},{32,40},{40,32},{48,56},{56,48},{64,72... | collective-permute-start | bytes 3145736 | tf_op jit(solution)/shard_map/ppermute | solution.py:316
  78.8 4.9 %collective-permute-start.19 = (bf16[256,1024]{1,0:T(8,128)(2,1)S(1)}, bf16[256,1024]{1,0:T(8,128)(2,1)S(1)}, u32[]{:S(2)}, u32[]{:S(2)}) collective-permute-start(bf16[256,1024]{1,0:T(8,128)(2,1)S(1)} %collective-permute-done.11.wf_ref), channel_id=1, source_target_pairs={{0,8},{8,0},{16,24},{24,16},{32,40},{40,32},{48,56},{56,48},{64,72... | collective-permute-start | bytes 1572872 | tf_op jit(solution)/shard_map/ppermute | solution.py:316
  79.3 15.4 %collective-permute-start.22 = (bf16[512,512]{1,0:T(8,128)(2,1)S(1)}, bf16[512,512]{1,0:T(8,128)(2,1)S(1)}, u32[]{:S(2)}, u32[]{:S(2)}) collective-permute-start(bf16[512,512]{1,0:T(8,128)(2,1)S(1)} %get-tuple-element.45), channel_id=1, source_target_pairs={{0,2},{1,3},{2,4},{3,5},{4,6},{5,7},{6,0},{7,1},{8,10},{9,11},{10,... | collective-permute-start | bytes 1572872 | tf_op jit(solution)/shard_map/ppermute | solution.py:321
  80.3 24.7 %collective-permute-start.23 = (bf16[512,512]{1,0:T(8,128)(2,1)S(1)}, bf16[512,512]{1,0:T(8,128)(2,1)S(1)}, u32[]{:S(2)}, u32[]{:S(2)}) collective-permute-start(bf16[512,512]{1,0:T(8,128)(2,1)S(1)} %get-tuple-element.46), channel_id=1, source_target_pairs={{0,6},{1,7},{2,0},{3,1},{4,2},{5,3},{6,4},{7,5},{8,14},{9,15},{10,... | collective-permute-start | bytes 1572872 | tf_op jit(solution)/shard_map/ppermute | solution.py:321
  82.6 23.7 %collective-permute-start.21 = (bf16[512,512]{1,0:T(8,128)(2,1)S(1)}, bf16[512,512]{1,0:T(8,128)(2,1)S(1)}, u32[]{:S(2)}, u32[]{:S(2)}) collective-permute-start(bf16[512,512]{1,0:T(8,128)(2,1)S(1)} %get-tuple-element.39), channel_id=1, source_target_pairs={{0,4},{1,5},{2,6},{3,7},{4,0},{5,1},{6,2},{7,3},{8,12},{9,13},{10,... | collective-permute-start | bytes 1572872 | tf_op jit(solution)/shard_map/ppermute | solution.py:321
  86.7 20.4 %collective-permute-start.20 = (bf16[512,512]{1,0:T(8,128)(2,1)S(1)}, bf16[512,512]{1,0:T(8,128)(2,1)S(1)}, u32[]{:S(2)}, u32[]{:S(2)}) collective-permute-start(bf16[512,512]{1,0:T(8,128)(2,1)S(1)} %get-tuple-element.43), channel_id=1, source_target_pairs={{0,1},{1,0},{2,3},{3,2},{4,5},{5,4},{6,7},{7,6},{8,9},{9,8},{10,11... | collective-permute-start | bytes 1572872 | tf_op jit(solution)/shard_map/ppermute | solution.py:321

commit v6 on v4

--- a/solution.py
+++ b/solution.py
@@ -167,7 +167,7 @@
             pltpu.VMEM((2, TILE, LAGS * rows), F32),
         ],
         compiler_params=pltpu.CompilerParams(vmem_limit_bytes=16 * 2**20),
-        cost_estimate=pl.CostEstimate(flops=4 * 10**9, bytes_accessed=1, transcendentals=0) if half == 0 else pl.CostEstimate(
+        cost_estimate=pl.CostEstimate(flops=2 * 10**9, bytes_accessed=1, transcendentals=0) if half == 0 else pl.CostEstimate(
             flops=16 * rows * cols * keys, bytes_accessed=4 * 2**20,
             transcendentals=rows * cols // HD * keys,
         ),

time: 110 us -> 114 us (1.036)
  waiting for transfers between devices: 37 us -> 47 us
  starting transfers between devices: 37.3 us -> 32.2 us
    ppermute x13, waiting for transfers between devices: 2.65 us -> 12.1 us  [ctx_move(): lax.ppermute(array, 'ctx', [(i, to(i)) for i in range(ctx_size) if 0 <= t...]
    ppermute x10, starting transfers between devices: 13.4 us -> 8.02 us  [head_move(): return lax.ppermute(array, 'head', [(i, to(i)) for i in range(2 * ring)])]
    unnamed x14 -> x12, local copies, waits for them, and re-layouts: 5.11 us -> 4.41 us
  transfers between devices with their start and end apart: 24 -> 24, of which waited for: 8 -> 10; matrix products, arithmetic and copies ran while one was open for 1% -> 1% of each run, Pallas kernels for 22% -> 22%
where the time goes in v6:
time: 114 us
  waiting for transfers between devices  47 us (41%)
  starting transfers between devices  32.2 us (28%)
  Pallas kernels  27.9 us (24%)
  local copies, waits for them, and re-layouts  5.85 us (5%)
    ppermute x10, waiting for transfers between devices, head_move(): return lax.ppermute(array, 'head', [(i, to(i)) for i in range(2 * ring)])  35 us
    ppermute x13, starting transfers between devices, ctx_move(): lax.ppermute(array, 'ctx', [(i, to(i)) for i in range(ctx_size) if 0 <= t...  22.7 us
    pallas_call x2, Pallas kernels, attention(): pl.pallas_call(functools.partial(attn_kernel, half), out_shape=[jax.Shape...  17 us
    ppermute x13, waiting for transfers between devices, ctx_move(): lax.ppermute(array, 'ctx', [(i, to(i)) for i in range(ctx_size) if 0 <= t...  12.1 us
    pallas_call x5, Pallas kernels, project(): pl.pallas_call(kernel, out_shape=outs, in_specs=[SMEM] + [VMEM] * (len(ar...  8.99 us
    ppermute x10, starting transfers between devices, head_move(): return lax.ppermute(array, 'head', [(i, to(i)) for i in range(2 * ring)])  8.02 us
    unnamed x12, local copies, waits for them, and re-layouts  4.41 us
  transfers between devices with their start and end apart: 24, of which 10 were waited for; matrix products, arithmetic and copies ran while one was open for 1% of the time, Pallas kernels for 22%

profile of v6, /device:TPU:24, one launch (start us, length us, event | category | flops | bytes accessed | tf_op | source)
XLA Modules:
  0.0 113.5 jit_solution(5741854761157680190)
XLA Ops:
  0.0 1.1 %fusion = (bf16[1,512,128]{2,1,0:T(8,128)(2,1)S(1)}, bf16[1,512,128]{2,1,0:T(8,128)(2,1)S(1)}, bf16[1,512,128]{2,1,0:T(8,128)(2,1)S(1)}, bf16[1,512,128]{2,1,0:T(8,128)(2,1)S(1)}) fusion(bf16[2,512,128]{2,1,0:T(8,128)(2,1)} %param.6, bf16[2,512,128]{2,1,0:T(8,128)(2,1)} %param.7), kind=kLoop, calls=%fused_computation.8 | loop fusion | bytes 1048576 | tf_op jit(solution)/shard_map/slice | solution.py:334
  1.2 0.1 collective-permute-start
  1.3 0.6 collective-permute-start.3
  1.9 3.8 %collective-permute-start.1 = (bf16[2,512,128]{2,1,0:T(8,128)(2,1)S(1)}, bf16[2,512,128]{2,1,0:T(8,128)(2,1)}, u32[]{:S(2)}, u32[]{:S(2)}) collective-permute-start(bf16[2,512,128]{2,1,0:T(8,128)(2,1)S(1)} %pad_maximum_fusion.own_ref), channel_id=1, source_target_pairs={{0,16},{8,24},{16,32},{24,40},{32,48},{40,56},{48,64},{56,72},{64,... | collective-permute-start | bytes 786440 | tf_op jit(solution)/shard_map/ppermute | solution.py:311
  5.7 6.5 %collective-permute-start.2 = (bf16[2,512,128]{2,1,0:T(8,128)(2,1)S(1)}, bf16[2,512,128]{2,1,0:T(8,128)(2,1)S(1)}, u32[]{:S(2)}, u32[]{:S(2)}) collective-permute-start(bf16[2,512,128]{2,1,0:T(8,128)(2,1)S(1)} %pad_maximum_fusion.1.own_ref), channel_id=1, source_target_pairs={{16,0},{24,8},{32,16},{40,24},{48,32},{56,40},{64,48},{72,56},{80,... | collective-permute-start | bytes 786440 | tf_op jit(solution)/shard_map/ppermute | solution.py:311
  12.3 0.1 pad_add_fusion.info_ref
  12.4 2.2 %copy-done = bf16[512,4096]{1,0:T(8,128)(2,1)S(1)} copy-done((bf16[512,4096]{1,0:T(8,128)(2,1)S(1)}, bf16[512,4096]{1,0:T(8,128)(2,1)}, u32[]{:S(2)}) %copy-start) | copy-done | bytes 4194328
  14.6 1.9 %split_weights.1 = (bf16[512,1024]{1,0:T(8,128)(2,1)}, bf16[256,1024]{1,0:T(8,128)(2,1)}, bf16[1024,512]{1,0:T(8,128)(2,1)S(1)}) custom-call(s32[3]{0:T(128)S(1)} %pad_add_fusion.info_ref, bf16[512,4096]{1,0:T(8,128)(2,1)S(1)} %copy-done), custom_call_target="tpu_custom_call" | custom-call | flops 1 | bytes 1 | tf_op jit(solution)/shard_map/split_weights/pallas_call | solution.py:196
  16.4 1.0 copy-done.4
  17.4 0.0 collective-permute-done.traded_ref
  17.4 0.0 collective-permute-done.3.traded_ref
  17.4 0.0 collective-permute-done.1.near_ref.fold_near_ref
  17.4 0.6 collective-permute-done.2
  18.0 1.5 %collective-permute-start.10 = (bf16[512,1024]{1,0:T(8,128)(2,1)}, bf16[512,1024]{1,0:T(8,128)(2,1)S(1)}, u32[]{:S(2)}, u32[]{:S(2)}) collective-permute-start(bf16[512,1024]{1,0:T(8,128)(2,1)} %get-tuple-element.31), channel_id=1, source_target_pairs={{0,2},{1,3},{2,4},{3,5},{4,6},{5,7},{6,0},{7,1},{8,14},{9,15},{10,... | collective-permute-start | bytes 3145736 | tf_op jit(solution)/shard_map/ppermute | solution.py:344
  19.5 8.0 %collective-permute-start.8 = (bf16[2,512,128]{2,1,0:T(8,128)(2,1)S(1)}, bf16[2,512,128]{2,1,0:T(8,128)(2,1)}, u32[]{:S(2)}, u32[]{:S(2)}) collective-permute-start(bf16[2,512,128]{2,1,0:T(8,128)(2,1)S(1)} %broadcast_select_fusion.near_ref), channel_id=1, source_target_pairs={{16,0},{24,8},{32,16},{40,24},{48,32},{56,40},{64,48},{72,56},{80,... | collective-permute-start | bytes 786440 | tf_op jit(solution)/shard_map/ppermute | solution.py:311
  27.5 1.9 %collective-permute-start.6 = (bf16[2,512,128]{2,1,0:T(8,128)(2,1)}, bf16[2,512,128]{2,1,0:T(8,128)(2,1)}, u32[]{:S(2)}, u32[]{:S(2)}) collective-permute-start(bf16[2,512,128]{2,1,0:T(8,128)(2,1)} %collective-permute-done.1.near_ref.fold_near_ref), channel_id=1, source_target_pairs={{0,16},{8,24},{16,32},{24,40},{32,48},{40,56},{48,64},{56,72},{64,... | collective-permute-start | bytes 786440 | tf_op jit(solution)/shard_map/ppermute | solution.py:311
  29.5 0.1 collective-permute-start.5
  29.6 0.5 collective-permute-start.4
  30.1 3.3 %collective-permute-done.8.far_ref = bf16[2,512,128]{2,1,0:T(8,128)(2,1)} collective-permute-done((bf16[2,512,128]{2,1,0:T(8,128)(2,1)S(1)}, bf16[2,512,128]{2,1,0:T(8,128)(2,1)}, u32[]{:S(2)}, u32[]{:S(2)}) %collective-permute-start.8) | collective-permute-done | bytes 262176 | tf_op jit(solution)/shard_map/ppermute | solution.py:311
  33.4 0.8 collective-permute-start.11
  34.2 7.4 %collective-permute-done.6.far_ref = bf16[2,512,128]{2,1,0:T(8,128)(2,1)} collective-permute-done((bf16[2,512,128]{2,1,0:T(8,128)(2,1)}, bf16[2,512,128]{2,1,0:T(8,128)(2,1)}, u32[]{:S(2)}, u32[]{:S(2)}) %collective-permute-start.6) | collective-permute-done | bytes 262176 | tf_op jit(solution)/shard_map/ppermute | solution.py:311
  41.6 0.0 collective-permute-start.7
  41.6 0.1 copy.7.doc_ref
  41.7 0.1 copy.6.doc_ref
  41.9 0.1 add_add_fusion.info_ref
  42.0 0.0 collective-permute-done.5.near_traded_ref
  42.0 0.5 collective-permute-start.9
  42.5 0.1 add_add_fusion.1.info_ref
  42.6 0.0 collective-permute-done.4.near_traded_ref.fold_traded_ref
  42.6 0.0 collective-permute-start.16
  42.6 0.8 collective-permute-done.7.far_traded_ref
  43.4 1.2 %copy-done.2 = bf16[2,512,512]{2,1,0:T(8,128)(2,1)S(1)} copy-done((bf16[2,512,512]{2,1,0:T(8,128)(2,1)S(1)}, bf16[2,512,512]{2,1,0:T(8,128)(2,1)}, u32[]{:S(2)}) %copy-start.2) | copy-done | bytes 1048600
  44.7 8.6 %attend0.1.own_ref = bf16[512,512]{1,0:T(8,128)(2,1)S(1)} custom-call(s32[3]{0:T(128)S(1)} %add_add_fusion.info_ref, bf16[2,512,512]{2,1,0:T(8,128)(2,1)S(1)} %copy-done.2, s32[512,1]{1,0:T(8,128)S(1)} %copy.6.doc_ref, bf16[2,512,128]{2,1,0:T(8,128)(2,1)S(1)} %pad_maximum_fusion.own_ref, bf16[2,512,128]{2,1,0:T(8,128)(2,1)S(1)} %collective-permute-done.traded_ref, ...), custom_call_target="tpu_custom_call" | custom-call | flops 2000000000 | bytes 1 | tf_op jit(solution)/shard_map/attend0/pallas_call | solution.py:159
  53.3 0.0 copy-start.1
  53.3 0.0 collective-permute-done.9.far_traded_ref
  53.3 0.0 collective-permute-done.11.wf_ref
  53.3 0.0 collective-permute-done.10.ws_ref
  53.3 1.0 collective-permute-start.14
  54.4 1.4 %collective-permute-start.13 = (bf16[512,512]{1,0:T(8,128)(2,1)S(1)}, bf16[512,512]{1,0:T(8,128)(2,1)S(1)}, u32[]{:S(2)}, u32[]{:S(2)}) collective-permute-start(bf16[512,512]{1,0:T(8,128)(2,1)S(1)} %attend0.1.own_ref), channel_id=1, source_target_pairs={{0,6},{1,7},{2,0},{3,1},{4,2},{5,3},{6,4},{7,5},{8,14},{9,15},{10,... | collective-permute-start | bytes 1572872 | tf_op jit(solution)/shard_map/ppermute | solution.py:316
  55.8 0.6 collective-permute-start.12
  56.4 8.4 %attend1.1.own_ref = bf16[512,512]{1,0:T(8,128)(2,1)S(1)} custom-call(s32[3]{0:T(128)S(1)} %add_add_fusion.1.info_ref, bf16[2,512,512]{2,1,0:T(8,128)(2,1)S(1)} %copy-done.3, s32[512,1]{1,0:T(8,128)S(1)} %copy.7.doc_ref, bf16[2,512,128]{2,1,0:T(8,128)(2,1)S(1)} %pad_maximum_fusion.1.own_ref, bf16[2,512,128]{2,1,0:T(8,128)(2,1)S(1)} %collective-permute-done.3.traded_ref, ...), custom_call_target="tpu_custom_call" | custom-call | flops 10737418240 | bytes 4194304 | tf_op jit(solution)/shard_map/attend1/pallas_call | solution.py:159
  64.8 3.1 %collective-permute-done.16.wm_ref = bf16[1024,512]{1,0:T(8,128)(2,1)S(1)} collective-permute-done((bf16[1024,512]{1,0:T(8,128)(2,1)}, bf16[1024,512]{1,0:T(8,128)(2,1)S(1)}, u32[]{:S(2)}, u32[]{:S(2)}) %collective-permute-start.16) | collective-permute-done | bytes 1048608 | tf_op jit(solution)/shard_map/ppermute | solution.py:316
  67.9 0.0 collective-permute-start.17
  67.9 0.3 collective-permute-start.15
  68.2 1.5 %collective-permute-done.14.far_ref = bf16[512,512]{1,0:T(8,128)(2,1)S(1)} collective-permute-done((bf16[512,512]{1,0:T(8,128)(2,1)S(1)}, bf16[512,512]{1,0:T(8,128)(2,1)S(1)}, u32[]{:S(2)}, u32[]{:S(2)}) %collective-permute-start.14) | collective-permute-done | bytes 524320 | tf_op jit(solution)/shard_map/ppermute | solution.py:316
  69.7 8.6 %collective-permute-done.13.right_ref = bf16[512,512]{1,0:T(8,128)(2,1)S(1)} collective-permute-done((bf16[512,512]{1,0:T(8,128)(2,1)S(1)}, bf16[512,512]{1,0:T(8,128)(2,1)S(1)}, u32[]{:S(2)}, u32[]{:S(2)}) %collective-permute-start.13) | collective-permute-done | bytes 524320 | tf_op jit(solution)/shard_map/ppermute | solution.py:316
  78.3 1.8 %collective-permute-done.12.left_ref = bf16[512,512]{1,0:T(8,128)(2,1)S(1)} collective-permute-done((bf16[512,512]{1,0:T(8,128)(2,1)S(1)}, bf16[512,512]{1,0:T(8,128)(2,1)S(1)}, u32[]{:S(2)}, u32[]{:S(2)}) %collective-permute-start.12) | collective-permute-done | bytes 524320 | tf_op jit(solution)/shard_map/ppermute | solution.py:316
  80.1 1.8 %own_part.1.part_ref = f32[4,512,512]{2,1,0:T(8,128)S(1)} custom-call(s32[3]{0:T(128)S(1)} %pad_add_fusion.info_ref, bf16[512,512]{1,0:T(8,128)(2,1)S(1)} %attend1.1.own_ref, bf16[512,4096]{1,0:T(8,128)(2,1)S(1)} %copy-done.1), custom_call_target="tpu_custom_call" | custom-call | flops 8000000000 | bytes 1 | tf_op jit(solution)/shard_map/own_part/pallas_call | solution.py:285
  81.9 0.3 collective-permute-done.15.peer_ref
  82.3 0.0 collective-permute-done.17.wp_ref
  82.3 1.8 %reduce_first.1 = (bf16[512,512]{1,0:T(8,128)(2,1)S(1)}, bf16[512,512]{1,0:T(8,128)(2,1)S(1)}, bf16[512,512]{1,0:T(8,128)(2,1)S(1)}, bf16[512,512]{1,0:T(8,128)(2,1)S(1)}) custom-call(s32[3]{0:T(128)S(1)} %pad_add_fusion.info_ref, bf16[512,512]{1,0:T(8,128)(2,1)S(1)} %collective-permute-done.15.peer_ref, f32[4,512,512]{2,1,0:T(8,128)S(1)} %own_part.1.part_ref, ...), custom_call_target="tpu_custom_call" | custom-call | bytes 1 | tf_op jit(solution)/shard_map/reduce_first/pallas_call | solution.py:285
  84.1 0.1 collective-permute-start.18
  84.2 0.5 collective-permute-start.19
  84.7 0.0 collective-permute-start.22
  84.7 3.2 %collective-permute-start.23 = (bf16[512,512]{1,0:T(8,128)(2,1)S(1)}, bf16[512,512]{1,0:T(8,128)(2,1)S(1)}, u32[]{:S(2)}, u32[]{:S(2)}) collective-permute-start(bf16[512,512]{1,0:T(8,128)(2,1)S(1)} %get-tuple-element.46), channel_id=1, source_target_pairs={{0,6},{1,7},{2,0},{3,1},{4,2},{5,3},{6,4},{7,5},{8,14},{9,15},{10,... | collective-permute-start | bytes 1572872 | tf_op jit(solution)/shard_map/ppermute | solution.py:316
  87.9 0.0 collective-permute-start.21
  87.9 0.0 collective-permute-done.19.wfp_ref
  87.9 0.0 collective-permute-done.18.wsp_ref
  87.9 2.9 %gather_first.1 = (bf16[512,512]{1,0:T(8,128)(2,1)S(1)}, bf16[512,512]{1,0:T(8,128)(2,1)S(1)}) custom-call(s32[3]{0:T(128)S(1)} %pad_add_fusion.info_ref, bf16[512,512]{1,0:T(8,128)(2,1)S(1)} %attend0.1.own_ref, bf16[512,512]{1,0:T(8,128)(2,1)S(1)} %collective-permute-done.12.left_ref, bf16[512,512]{1,0:T(8,128)(2,1)S(1)} %collective-permute-done.13.right_ref, ...), custom_call_target="tpu_custom_call" | custom-call | bytes 1 | tf_op jit(solution)/shard_map/gather_first/pallas_call | solution.py:285
  90.9 0.6 collective-permute-start.20
  91.5 19.6 %collective-permute-done.22.refs_1_ = bf16[512,512]{1,0:T(8,128)(2,1)S(1)} collective-permute-done((bf16[512,512]{1,0:T(8,128)(2,1)S(1)}, bf16[512,512]{1,0:T(8,128)(2,1)S(1)}, u32[]{:S(2)}, u32[]{:S(2)}) %collective-permute-start.22) | collective-permute-done | bytes 524320 | tf_op jit(solution)/shard_map/ppermute | solution.py:316
  111.1 0.8 total.1.done_ref
  111.9 0.0 collective-permute-done.20.got_ref
  111.9 1.7 %finish.1 = bf16[2,512,512]{2,1,0:T(8,128)(2,1)} custom-call(s32[3]{0:T(128)S(1)} %pad_add_fusion.info_ref, bf16[512,512]{1,0:T(8,128)(2,1)S(1)} %get-tuple-element.42.keep_ref, bf16[512,512]{1,0:T(8,128)(2,1)S(1)} %collective-permute-done.20.got_ref, bf16[512,512]{1,0:T(8,128)(2,1)S(1)} %total.1.done_ref), custom_call_target="tpu_custom_call" | custom-call | bytes 1 | tf_op jit(solution)/shard_map/finish/pallas_call | solution.py:285
  (14 shorter events, 0.1 us)
Async XLA Ops:
  0.0 41.6 %copy-start.5 = (s32[2,512]{1,0:T(2,128)S(1)}, s32[2,512]{1,0:T(2,128)}, u32[]{:S(2)}) copy-start(s32[2,512]{1,0:T(2,128)} %param.8) | copy-start | bytes 12292
  1.2 16.2 %collective-permute-start = (bf16[2,512,128]{2,1,0:T(8,128)(2,1)S(1)}, bf16[2,512,128]{2,1,0:T(8,128)(2,1)S(1)}, u32[]{:S(2)}, u32[]{:S(2)}) collective-permute-start(bf16[2,512,128]{2,1,0:T(8,128)(2,1)S(1)} %pad_maximum_fusion.own_ref), channel_id=1, source_target_pairs={{0,8},{8,0},{16,24},{24,16},{32,40},{40,32},{48,56},{56,48},{64,72... | collective-permute-start | bytes 786440 | tf_op jit(solution)/shard_map/ppermute | solution.py:311
  1.3 16.1 %collective-permute-start.3 = (bf16[2,512,128]{2,1,0:T(8,128)(2,1)S(1)}, bf16[2,512,128]{2,1,0:T(8,128)(2,1)S(1)}, u32[]{:S(2)}, u32[]{:S(2)}) collective-permute-start(bf16[2,512,128]{2,1,0:T(8,128)(2,1)S(1)} %pad_maximum_fusion.1.own_ref), channel_id=1, source_target_pairs={{0,8},{8,0},{16,24},{24,16},{32,40},{40,32},{48,56},{56,48},{64,72... | collective-permute-start | bytes 786440 | tf_op jit(solution)/shard_map/ppermute | solution.py:311
  1.9 15.5 %collective-permute-start.1 = (bf16[2,512,128]{2,1,0:T(8,128)(2,1)S(1)}, bf16[2,512,128]{2,1,0:T(8,128)(2,1)}, u32[]{:S(2)}, u32[]{:S(2)}) collective-permute-start(bf16[2,512,128]{2,1,0:T(8,128)(2,1)S(1)} %pad_maximum_fusion.own_ref), channel_id=1, source_target_pairs={{0,16},{8,24},{16,32},{24,40},{32,48},{40,56},{48,64},{56,72},{64,... | collective-permute-start | bytes 786440 | tf_op jit(solution)/shard_map/ppermute | solution.py:311
  5.7 12.3 %collective-permute-start.2 = (bf16[2,512,128]{2,1,0:T(8,128)(2,1)S(1)}, bf16[2,512,128]{2,1,0:T(8,128)(2,1)S(1)}, u32[]{:S(2)}, u32[]{:S(2)}) collective-permute-start(bf16[2,512,128]{2,1,0:T(8,128)(2,1)S(1)} %pad_maximum_fusion.1.own_ref), channel_id=1, source_target_pairs={{16,0},{24,8},{32,16},{40,24},{48,32},{56,40},{64,48},{72,56},{80,... | collective-permute-start | bytes 786440 | tf_op jit(solution)/shard_map/ppermute | solution.py:311
  12.4 2.2 %copy-start = (bf16[512,4096]{1,0:T(8,128)(2,1)S(1)}, bf16[512,4096]{1,0:T(8,128)(2,1)}, u32[]{:S(2)}) copy-start(bf16[512,4096]{1,0:T(8,128)(2,1)} %w_ref.5) | copy-start | bytes 12582916
  16.4 1.0 copy-start.4
  18.0 35.3 %collective-permute-start.10 = (bf16[512,1024]{1,0:T(8,128)(2,1)}, bf16[512,1024]{1,0:T(8,128)(2,1)S(1)}, u32[]{:S(2)}, u32[]{:S(2)}) collective-permute-start(bf16[512,1024]{1,0:T(8,128)(2,1)} %get-tuple-element.31), channel_id=1, source_target_pairs={{0,2},{1,3},{2,4},{3,5},{4,6},{5,7},{6,0},{7,1},{8,14},{9,15},{10,... | collective-permute-start | bytes 3145736 | tf_op jit(solution)/shard_map/ppermute | solution.py:344
  19.5 13.9 %collective-permute-start.8 = (bf16[2,512,128]{2,1,0:T(8,128)(2,1)S(1)}, bf16[2,512,128]{2,1,0:T(8,128)(2,1)}, u32[]{:S(2)}, u32[]{:S(2)}) collective-permute-start(bf16[2,512,128]{2,1,0:T(8,128)(2,1)S(1)} %broadcast_select_fusion.near_ref), channel_id=1, source_target_pairs={{16,0},{24,8},{32,16},{40,24},{48,32},{56,40},{64,48},{72,56},{80,... | collective-permute-start | bytes 786440 | tf_op jit(solution)/shard_map/ppermute | solution.py:311
  27.5 14.0 %collective-permute-start.6 = (bf16[2,512,128]{2,1,0:T(8,128)(2,1)}, bf16[2,512,128]{2,1,0:T(8,128)(2,1)}, u32[]{:S(2)}, u32[]{:S(2)}) collective-permute-start(bf16[2,512,128]{2,1,0:T(8,128)(2,1)} %collective-permute-done.1.near_ref.fold_near_ref), channel_id=1, source_target_pairs={{0,16},{8,24},{16,32},{24,40},{32,48},{40,56},{48,64},{56,72},{64,... | collective-permute-start | bytes 786440 | tf_op jit(solution)/shard_map/ppermute | solution.py:311
  29.5 12.5 %collective-permute-start.5 = (bf16[2,512,128]{2,1,0:T(8,128)(2,1)S(1)}, bf16[2,512,128]{2,1,0:T(8,128)(2,1)}, u32[]{:S(2)}, u32[]{:S(2)}) collective-permute-start(bf16[2,512,128]{2,1,0:T(8,128)(2,1)S(1)} %broadcast_select_fusion.near_ref), channel_id=1, source_target_pairs={{0,8},{8,0},{16,24},{24,16},{32,40},{40,32},{48,56},{56,48},{64,72... | collective-permute-start | bytes 786440 | tf_op jit(solution)/shard_map/ppermute | solution.py:311
  29.6 13.0 %collective-permute-start.4 = (bf16[2,512,128]{2,1,0:T(8,128)(2,1)}, bf16[2,512,128]{2,1,0:T(8,128)(2,1)}, u32[]{:S(2)}, u32[]{:S(2)}) collective-permute-start(bf16[2,512,128]{2,1,0:T(8,128)(2,1)} %collective-permute-done.1.near_ref.fold_near_ref), channel_id=1, source_target_pairs={{0,8},{8,0},{16,24},{24,16},{32,40},{40,32},{48,56},{56,48},{64,72... | collective-permute-start | bytes 786440 | tf_op jit(solution)/shard_map/ppermute | solution.py:311
  33.4 19.9 %collective-permute-start.11 = (bf16[256,1024]{1,0:T(8,128)(2,1)}, bf16[256,1024]{1,0:T(8,128)(2,1)S(1)}, u32[]{:S(2)}, u32[]{:S(2)}) collective-permute-start(bf16[256,1024]{1,0:T(8,128)(2,1)} %get-tuple-element.33), channel_id=1, source_target_pairs={{0,4},{1,5},{2,6},{3,7},{4,0},{5,1},{6,2},{7,3},{8,12},{9,13},{10,... | collective-permute-start | bytes 1572872 | tf_op jit(solution)/shard_map/ppermute | solution.py:316
  41.6 1.9 %collective-permute-start.7 = (bf16[2,512,128]{2,1,0:T(8,128)(2,1)}, bf16[2,512,128]{2,1,0:T(8,128)(2,1)}, u32[]{:S(2)}, u32[]{:S(2)}) collective-permute-start(bf16[2,512,128]{2,1,0:T(8,128)(2,1)} %collective-permute-done.6.far_ref), channel_id=1, source_target_pairs={{0,8},{8,0},{16,24},{24,16},{32,40},{40,32},{48,56},{56,48},{64,72... | collective-permute-start | bytes 786440 | tf_op jit(solution)/shard_map/ppermute | solution.py:311
  42.0 11.3 %collective-permute-start.9 = (bf16[2,512,128]{2,1,0:T(8,128)(2,1)}, bf16[2,512,128]{2,1,0:T(8,128)(2,1)S(1)}, u32[]{:S(2)}, u32[]{:S(2)}) collective-permute-start(bf16[2,512,128]{2,1,0:T(8,128)(2,1)} %collective-permute-done.8.far_ref), channel_id=1, source_target_pairs={{0,8},{8,0},{16,24},{24,16},{32,40},{40,32},{48,56},{56,48},{64,72... | collective-permute-start | bytes 786440 | tf_op jit(solution)/shard_map/ppermute | solution.py:311
  42.6 25.3 %collective-permute-start.16 = (bf16[1024,512]{1,0:T(8,128)(2,1)}, bf16[1024,512]{1,0:T(8,128)(2,1)S(1)}, u32[]{:S(2)}, u32[]{:S(2)}) collective-permute-start(bf16[1024,512]{1,0:T(8,128)(2,1)} %copy-done.4), channel_id=1, source_target_pairs={{0,1},{1,0},{2,3},{3,2},{4,5},{5,4},{6,7},{7,6},{8,9},{9,8},{10,11... | collective-permute-start | bytes 3145736 | tf_op jit(solution)/shard_map/ppermute | solution.py:316
  43.4 1.2 %copy-start.2 = (bf16[2,512,512]{2,1,0:T(8,128)(2,1)S(1)}, bf16[2,512,512]{2,1,0:T(8,128)(2,1)}, u32[]{:S(2)}) copy-start(bf16[2,512,512]{2,1,0:T(8,128)(2,1)} %q_ref.3) | copy-start | bytes 3145732
  44.7 11.7 %copy-start.3 = (bf16[2,512,512]{2,1,0:T(8,128)(2,1)S(1)}, bf16[2,512,512]{2,1,0:T(8,128)(2,1)}, u32[]{:S(2)}) copy-start(bf16[2,512,512]{2,1,0:T(8,128)(2,1)} %q_ref.3) | copy-start | bytes 3145732
  53.3 26.8 %copy-start.1 = (bf16[512,4096]{1,0:T(8,128)(2,1)S(1)}, bf16[512,4096]{1,0:T(8,128)(2,1)}, u32[]{:S(2)}) copy-start(bf16[512,4096]{1,0:T(8,128)(2,1)} %w_ref.5) | copy-start | bytes 12582916
  53.3 16.4 %collective-permute-start.14 = (bf16[512,512]{1,0:T(8,128)(2,1)S(1)}, bf16[512,512]{1,0:T(8,128)(2,1)S(1)}, u32[]{:S(2)}, u32[]{:S(2)}) collective-permute-start(bf16[512,512]{1,0:T(8,128)(2,1)S(1)} %attend0.1.own_ref), channel_id=1, source_target_pairs={{0,4},{1,5},{2,6},{3,7},{4,0},{5,1},{6,2},{7,3},{8,12},{9,13},{10,... | collective-permute-start | bytes 1572872 | tf_op jit(solution)/shard_map/ppermute | solution.py:316
  54.4 23.9 %collective-permute-start.13 = (bf16[512,512]{1,0:T(8,128)(2,1)S(1)}, bf16[512,512]{1,0:T(8,128)(2,1)S(1)}, u32[]{:S(2)}, u32[]{:S(2)}) collective-permute-start(bf16[512,512]{1,0:T(8,128)(2,1)S(1)} %attend0.1.own_ref), channel_id=1, source_target_pairs={{0,6},{1,7},{2,0},{3,1},{4,2},{5,3},{6,4},{7,5},{8,14},{9,15},{10,... | collective-permute-start | bytes 1572872 | tf_op jit(solution)/shard_map/ppermute | solution.py:316
  55.8 24.3 %collective-permute-start.12 = (bf16[512,512]{1,0:T(8,128)(2,1)S(1)}, bf16[512,512]{1,0:T(8,128)(2,1)S(1)}, u32[]{:S(2)}, u32[]{:S(2)}) collective-permute-start(bf16[512,512]{1,0:T(8,128)(2,1)S(1)} %attend0.1.own_ref), channel_id=1, source_target_pairs={{0,2},{1,3},{2,4},{3,5},{4,6},{5,7},{6,0},{7,1},{8,10},{9,11},{10,... | collective-permute-start | bytes 1572872 | tf_op jit(solution)/shard_map/ppermute | solution.py:316
  67.9 14.3 %collective-permute-start.17 = (bf16[1024,512]{1,0:T(8,128)(2,1)S(1)}, bf16[1024,512]{1,0:T(8,128)(2,1)S(1)}, u32[]{:S(2)}, u32[]{:S(2)}) collective-permute-start(bf16[1024,512]{1,0:T(8,128)(2,1)S(1)} %collective-permute-done.16.wm_ref), channel_id=1, source_target_pairs={{0,8},{8,0},{16,24},{24,16},{32,40},{40,32},{48,56},{56,48},{64,72... | collective-permute-start | bytes 3145736 | tf_op jit(solution)/shard_map/ppermute | solution.py:311
  67.9 14.3 %collective-permute-start.15 = (bf16[512,512]{1,0:T(8,128)(2,1)S(1)}, bf16[512,512]{1,0:T(8,128)(2,1)S(1)}, u32[]{:S(2)}, u32[]{:S(2)}) collective-permute-start(bf16[512,512]{1,0:T(8,128)(2,1)S(1)} %attend1.1.own_ref), channel_id=1, source_target_pairs={{0,1},{1,0},{2,3},{3,2},{4,5},{5,4},{6,7},{7,6},{8,9},{9,8},{10,11... | collective-permute-start | bytes 1572872 | tf_op jit(solution)/shard_map/ppermute | solution.py:316
  84.1 3.8 %collective-permute-start.18 = (bf16[512,1024]{1,0:T(8,128)(2,1)S(1)}, bf16[512,1024]{1,0:T(8,128)(2,1)S(1)}, u32[]{:S(2)}, u32[]{:S(2)}) collective-permute-start(bf16[512,1024]{1,0:T(8,128)(2,1)S(1)} %collective-permute-done.10.ws_ref), channel_id=1, source_target_pairs={{0,8},{8,0},{16,24},{24,16},{32,40},{40,32},{48,56},{56,48},{64,72... | collective-permute-start | bytes 3145736 | tf_op jit(solution)/shard_map/ppermute | solution.py:311
  84.2 3.7 %collective-permute-start.19 = (bf16[256,1024]{1,0:T(8,128)(2,1)S(1)}, bf16[256,1024]{1,0:T(8,128)(2,1)S(1)}, u32[]{:S(2)}, u32[]{:S(2)}) collective-permute-start(bf16[256,1024]{1,0:T(8,128)(2,1)S(1)} %collective-permute-done.11.wf_ref), channel_id=1, source_target_pairs={{0,8},{8,0},{16,24},{24,16},{32,40},{40,32},{48,56},{56,48},{64,72... | collective-permute-start | bytes 1572872 | tf_op jit(solution)/shard_map/ppermute | solution.py:311
  84.7 26.4 %collective-permute-start.22 = (bf16[512,512]{1,0:T(8,128)(2,1)S(1)}, bf16[512,512]{1,0:T(8,128)(2,1)S(1)}, u32[]{:S(2)}, u32[]{:S(2)}) collective-permute-start(bf16[512,512]{1,0:T(8,128)(2,1)S(1)} %get-tuple-element.45), channel_id=1, source_target_pairs={{0,2},{1,3},{2,4},{3,5},{4,6},{5,7},{6,0},{7,1},{8,10},{9,11},{10,... | collective-permute-start | bytes 1572872 | tf_op jit(solution)/shard_map/ppermute | solution.py:316
  84.7 26.4 %collective-permute-start.23 = (bf16[512,512]{1,0:T(8,128)(2,1)S(1)}, bf16[512,512]{1,0:T(8,128)(2,1)S(1)}, u32[]{:S(2)}, u32[]{:S(2)}) collective-permute-start(bf16[512,512]{1,0:T(8,128)(2,1)S(1)} %get-tuple-element.46), channel_id=1, source_target_pairs={{0,6},{1,7},{2,0},{3,1},{4,2},{5,3},{6,4},{7,5},{8,14},{9,15},{10,... | collective-permute-start | bytes 1572872 | tf_op jit(solution)/shard_map/ppermute | solution.py:316
  87.9 23.1 %collective-permute-start.21 = (bf16[512,512]{1,0:T(8,128)(2,1)S(1)}, bf16[512,512]{1,0:T(8,128)(2,1)S(1)}, u32[]{:S(2)}, u32[]{:S(2)}) collective-permute-start(bf16[512,512]{1,0:T(8,128)(2,1)S(1)} %get-tuple-element.39), channel_id=1, source_target_pairs={{0,4},{1,5},{2,6},{3,7},{4,0},{5,1},{6,2},{7,3},{8,12},{9,13},{10,... | collective-permute-start | bytes 1572872 | tf_op jit(solution)/shard_map/ppermute | solution.py:316
  90.9 21.0 %collective-permute-start.20 = (bf16[512,512]{1,0:T(8,128)(2,1)S(1)}, bf16[512,512]{1,0:T(8,128)(2,1)S(1)}, u32[]{:S(2)}, u32[]{:S(2)}) collective-permute-start(bf16[512,512]{1,0:T(8,128)(2,1)S(1)} %get-tuple-element.43), channel_id=1, source_target_pairs={{0,1},{1,0},{2,3},{3,2},{4,5},{5,4},{6,7},{7,6},{8,9},{9,8},{10,11... | collective-permute-start | bytes 1572872 | tf_op jit(solution)/shard_map/ppermute | solution.py:316
